TPU v7x, 256 devices: a whole 4x4x8 slice. The times are simulated.
256 devices in a mesh: aux: 8 (over y_lo, x), occ: 32 (over z, y_hi, core).
Axes of the slice: x: 4, y: 4 (y_hi: 2, y_lo: 2; y = y_hi * 2 + y_lo), z: 8, core: 2. Of those that a mesh axis runs over, the one named last changes fastest.
Arguments:
- orbital_slabs: bfloat16 [256, 64, 24576], P('occ', None, 'aux'), may hold values from -0.5 to 0.5
- occ_energy: bfloat16 [256], P('occ'), may hold values from -1.1953125 to -0.29882812
- virt_energy: bfloat16 [64], replicated, may hold values from 0.29882812 to 2.5
- pair_kept: int32 [32], replicated, may hold values 0 or 1
Outputs:
- gamma: bfloat16 [256, 64, 24576], P('occ', None, 'aux')
- virt_density: float32 [64, 64], replicated
All inputs are finite; a program needn't handle non-finite values.
Results may differ from a plain program's by a relative error of at most 0.019.
Values may be sent and summed in bfloat16 or wider, within the bound.
No kernel may reach another device: no remote copies, remote signals or barrier semaphores. Data moves between devices by JAX's collectives and lax.ppermute only.
A program may use at most 64 MiB of HBM per device.

v0:
```python
import jax
import jax.numpy as jnp
from jax import lax
from jax.sharding import PartitionSpec as P


def passed_along(value, axis, by):
    count = lax.axis_size(axis)
    return lax.ppermute(value, axis, [(i, (i + by) % count) for i in range(count)])


def contract_rows(left, right):
    return lax.dot_general(
        left, right, (((1,), (1,)), ((), ())), preferred_element_type=jnp.float32
    )


def contract_first(left, right):
    return lax.dot_general(
        left, right, (((0,), (0,)), ((), ())), preferred_element_type=jnp.float32
    )


def level_gap(energy, virt_energy):
    return (energy.astype(jnp.float32)[:, None] - virt_energy.astype(jnp.float32)[None, :]).reshape(
        -1
    )


def pair_terms(left, right, left_energy, right_energy, virt_energy, keep):
    occ_count, virt_count, aux_count = left.shape
    rows = occ_count * virt_count
    partial_value = contract_rows(left.reshape(rows, aux_count), right.reshape(rows, aux_count))
    gap_left = level_gap(left_energy, virt_energy)
    gap_right = level_gap(right_energy, virt_energy)
    integrals = lax.psum(partial_value.astype(jnp.bfloat16), "aux").astype(jnp.float32)
    amplitude = (keep * integrals / (gap_left[:, None] + gap_right[None, :])).astype(jnp.bfloat16)
    wide = amplitude.reshape(occ_count, virt_count, occ_count, virt_count).astype(jnp.float32)
    tilde = (2.0 * wide - wide.transpose(0, 3, 2, 1)).astype(jnp.bfloat16)
    return (amplitude, tilde.reshape(rows, rows))


def pair_density(amplitude, tilde, occ_count, virt_count, both):
    amp_four = amplitude.reshape(occ_count, virt_count, occ_count, virt_count)
    til_four = tilde.reshape(occ_count, virt_count, occ_count, virt_count)
    total = jnp.einsum("iajc,ibjc->ab", til_four, amp_four, preferred_element_type=jnp.float32)
    if both:
        total = total + jnp.einsum(
            "icja,icjb->ab", til_four, amp_four, preferred_element_type=jnp.float32
        )
    return total


def body(orbital_slabs, occ_energy, virt_energy, pair_kept):
    occ_count, virt_count, aux_count = orbital_slabs.shape
    rows = occ_count * virt_count
    flat = orbital_slabs.reshape(rows, aux_count)
    place = lax.axis_index("occ")
    empty = jnp.zeros((rows, aux_count), jnp.float32)

    def forward_product(tilde, slabs):
        return jnp.dot(tilde, slabs, preferred_element_type=jnp.float32)

    def backward_product(tilde, slabs):
        return contract_first(tilde, slabs)

    def nothing(tilde, slabs):
        return empty

    next_slabs, next_energy = passed_along((orbital_slabs, occ_energy), "occ", -1)
    keep_next = pair_kept[place].astype(jnp.float32)
    amp_self, tilde_self = pair_terms(
        orbital_slabs, orbital_slabs, occ_energy, occ_energy, virt_energy, 1.0
    )
    own = jnp.dot(tilde_self, flat, preferred_element_type=jnp.float32)
    amp_next, tilde_next = pair_terms(
        orbital_slabs, next_slabs, occ_energy, next_energy, virt_energy, keep_next
    )
    flat_next = next_slabs.reshape(rows, aux_count)
    own = own + lax.cond(keep_next > 0.0, forward_product, nothing, tilde_next, flat_next)
    outgoing = lax.cond(keep_next > 0.0, backward_product, nothing, tilde_next, flat).astype(
        jnp.bfloat16
    )
    returned = passed_along(outgoing, "occ", 1)
    gamma = (
        (own + returned.astype(jnp.float32))
        .astype(jnp.bfloat16)
        .reshape(occ_count, virt_count, aux_count)
    )
    local_density = pair_density(amp_self, tilde_self, occ_count, virt_count, False)
    local_density = local_density + pair_density(amp_next, tilde_next, occ_count, virt_count, True)
    total_density = lax.psum(local_density, "occ")
    virt_density = total_density / (4.0 * occ_count * occ_count * virt_count)
    return (gamma, virt_density)


def solution(mesh):
    return jax.shard_map(
        body,
        mesh=mesh,
        in_specs=(P("occ", None, "aux"), P("occ"), P(), P()),
        out_specs=(P("occ", None, "aux"), P()),
        check_vma=False,
    )
```

profile of v0, /device:TPU:2, one launch (start us, length us, event | category | flops | bytes accessed | tf_op | source)
XLA Modules:
  0.0 332.6 jit_solution(15859124297612220523)
XLA Ops:
  7.2 8.0 %collective-permute-start = (bf16[8,64,3072]{2,1,0:T(8,128)(2,1)}, bf16[8,64,3072]{2,1,0:T(8,128)(2,1)S(1)}, u32[]{:S(2)}, u32[]{:S(2)}) collective-permute-start(bf16[8,64,3072]{2,1,0:T(8,128)(2,1)} %param.8), channel_id=1, source_target_pairs={{0,31},{1,0},{2,1},{3,2},{4,3},{5,4},{6,5},{7,6},{8,7},{9,8},{10,9... | collective-permute-start | bytes 9437192 | tf_op jit(solution)/shard_map/ppermute | solution.py:9
  15.2 5.6 %convolution_convert_fusion.1 = bf16[512,512]{1,0:T(8,128)(2,1)} fusion(bf16[512,3072]{1,0:T(8,128)(2,1)} %bitcast.46), kind=kOutput, calls=%fused_computation.8 | convolution fusion | flops 1610874880 | bytes 3670016 | tf_op jit(solution)/shard_map/dot_general | solution.py:13
  20.8 29.5 %collective-permute-done = bf16[8,64,3072]{2,1,0:T(8,128)(2,1)S(1)} collective-permute-done((bf16[8,64,3072]{2,1,0:T(8,128)(2,1)}, bf16[8,64,3072]{2,1,0:T(8,128)(2,1)S(1)}, u32[]{:S(2)}, u32[]{:S(2)}) %collective-permute-start) | collective-permute-done | bytes 3145760 | tf_op jit(solution)/shard_map/ppermute | solution.py:9
  50.3 1.7 copy-done.6
  52.0 2.6 convolution_convert_fusion
  54.7 5.5 %collective-permute-start.1 = (bf16[8]{0:T(256)(128)(2,1)S(1)}, bf16[8]{0:T(256)(128)(2,1)S(1)}, u32[]{:S(2)}, u32[]{:S(2)}) collective-permute-start(bf16[8]{0:T(256)(128)(2,1)S(1)} %copy-done.9), channel_id=1, source_target_pairs={{0,31},{1,0},{2,1},{3,2},{4,3},{5,4},{6,5},{7,6},{8,7},{9,8},{10,9... | collective-permute-start | bytes 56 | tf_op jit(solution)/shard_map/ppermute | solution.py:9
  61.7 72.3 %all-reduce.3.cloned.1.call-done = (bf16[512,512]{1,0:T(8,128)(2,1)}, bf16[512,512]{1,0:T(8,128)(2,1)}) async-done(((bf16[512,512]{1,0:T(8,128)(2,1)}, bf16[512,512]{1,0:T(8,128)(2,1)}), (bf16[512,512]{1,0:T(8,128)(2,1)}, bf16[512,512]{1,0:T(8,128)(2,1)})) %all-reduce.3.cloned.1.call-update) | async-done | bytes 1048592 | tf_op jit(solution)/shard_map/psum | solution.py:36
  134.0 2.6 divide_convert_fusion.1
  136.6 2.4 reshape.80
  139.0 2.8 copy.17
  141.8 3.1 fusion.2
  144.9 2.7 copy.18
  147.6 2.6 reshape.81
  150.1 4.5 %conditional.3 = (bf16[512,3072]{1,0:T(8,128)(2,1)}) conditional(s32[]{:T(128)} %convert_element_type.72, () %tuple.22, (bf16[512,512]{1,0:T(8,128)(2,1)}, bf16[512,3072]{1,0:T(8,128)(2,1)S(1)}) %tuple.34), branch_computations={%region_4.0_spmd, %region_5.0_spmd} | conditional | flops 1610612736 | bytes 6815752 | solution.py:81
  150.1 4.5 %fusion.12 = bf16[512,3072]{1,0:T(8,128)(2,1)} fusion(bf16[512,512]{1,0:T(8,128)(2,1)} %get-tuple-element.16, bf16[512,3072]{1,0:T(8,128)(2,1)S(1)} %get-tuple-element.17), kind=kOutput, calls=%fused_computation.26 | convolution fusion | flops 1610612736 | bytes 6815744 | tf_op jit(solution)/shard_map/cond/branch_1_fun/dot_general | solution.py:19
  154.7 1.6 reshape.77
  157.3 1.5 convert_multiply_fusion
  158.8 2.1 copy.16
  162.1 2.6 reshape.78
  164.6 6.7 %conditional.2 = (f32[512,3072]{1,0:T(8,128)}) conditional(s32[]{:T(128)} %convert_element_type.72, () %tuple.20, (bf16[512,512]{1,0:T(8,128)(2,1)}, bf16[512,3072]{1,0:T(8,128)(2,1)}) %tuple.35), branch_computations={%region_2.0_spmd, %region_3.0_spmd} | conditional | flops 1610612736 | bytes 9961480 | solution.py:80
  164.6 6.7 %fusion.11 = f32[512,3072]{1,0:T(8,128)} fusion(bf16[512,512]{1,0:T(8,128)(2,1)} %get-tuple-element.11, bf16[512,3072]{1,0:T(8,128)(2,1)} %get-tuple-element.12), kind=kOutput, calls=%fused_computation.25 | convolution fusion | flops 1610612736 | bytes 9961472 | tf_op jit(solution)/shard_map/cond/branch_1_fun/dot_general | solution.py:62
  173.3 142.5 %psum.23 = f32[64,64]{1,0:T(8,128)S(1)} all-reduce(f32[64,64]{1,0:T(8,128)S(1)} %fusion.3), channel_id=1, replica_groups=mesh['aux'=8,'occ'=32] {'occ'}, use_global_device_ids=true, to_apply=%region_6.0 | all-reduce | flops 4096 | bytes 32768 | tf_op jit(solution)/shard_map/psum | solution.py:92
  316.4 4.0 %fusion.13 = f32[512,3072]{1,0:T(8,128)S(1)} fusion(bf16[512,512]{1,0:T(8,128)(2,1)} %reshape.78, bf16[512,3072]{1,0:T(8,128)(2,1)} %bitcast.47), kind=kOutput, calls=%fused_computation.27 | convolution fusion | flops 1610612736 | bytes 9961472 | tf_op jit(solution)/shard_map/dot_general | solution.py:75
  320.4 5.3 %add_convert_fusion = bf16[512,3072]{1,0:T(8,128)(2,1)} fusion(bf16[512,3072]{1,0:T(8,128)(2,1)} %collective-permute-done.2, f32[512,3072]{1,0:T(8,128)S(1)} %fusion.13, f32[512,3072]{1,0:T(8,128)S(1)} %bitcast.45), kind=kLoop, calls=%fused_computation | loop fusion | flops 6291456 | bytes 18874368 | tf_op jit(solution)/shard_map/convert_element_type | solution.py:87
  (42 shorter events, 5.6 us)
Async XLA Ops:
  7.2 126.8 %all-reduce.3.cloned.1.call-start = ((), (), s32[]{:S(2)}) async-start(), calls=%async_computation | async-start | bytes 2097152 | tf_op jit(solution)/shard_map/psum | solution.py:36
  7.2 43.1 %collective-permute-start = (bf16[8,64,3072]{2,1,0:T(8,128)(2,1)}, bf16[8,64,3072]{2,1,0:T(8,128)(2,1)S(1)}, u32[]{:S(2)}, u32[]{:S(2)}) collective-permute-start(bf16[8,64,3072]{2,1,0:T(8,128)(2,1)} %param.8), channel_id=1, source_target_pairs={{0,31},{1,0},{2,1},{3,2},{4,3},{5,4},{6,5},{7,6},{8,7},{9,8},{10,9... | collective-permute-start | bytes 9437192 | tf_op jit(solution)/shard_map/ppermute | solution.py:9
  15.2 36.8 %copy-start = (bf16[8,64,3072]{2,1,0:T(8,128)(2,1)S(1)}, bf16[8,64,3072]{2,1,0:T(8,128)(2,1)}, u32[]{:S(2)}) copy-start(bf16[8,64,3072]{2,1,0:T(8,128)(2,1)} %param.8) | copy-start | bytes 9437188
  50.3 1.7 copy-start.6
  52.0 2.7 copy-start.9
  52.0 8.2 %copy-start.7 = (s32[32]{0:T(128)S(1)}, s32[32]{0:T(128)}, u32[]{:S(2)}) copy-start(s32[32]{0:T(128)} %param.11) | copy-start | bytes 388
  52.0 9.4 %copy-start.8 = (bf16[64]{0:T(256)(128)(2,1)S(1)}, bf16[64]{0:T(256)(128)(2,1)}, u32[]{:S(2)}) copy-start(bf16[64]{0:T(256)(128)(2,1)} %param.10) | copy-start | bytes 388
  54.7 6.8 %collective-permute-start.1 = (bf16[8]{0:T(256)(128)(2,1)S(1)}, bf16[8]{0:T(256)(128)(2,1)S(1)}, u32[]{:S(2)}, u32[]{:S(2)}) collective-permute-start(bf16[8]{0:T(256)(128)(2,1)S(1)} %copy-done.9), channel_id=1, source_target_pairs={{0,31},{1,0},{2,1},{3,2},{4,3},{5,4},{6,5},{7,6},{8,7},{9,8},{10,9... | collective-permute-start | bytes 56 | tf_op jit(solution)/shard_map/ppermute | solution.py:9
  154.7 165.7 %collective-permute-start.2 = (bf16[512,3072]{1,0:T(8,128)(2,1)}, bf16[512,3072]{1,0:T(8,128)(2,1)}, u32[]{:S(2)}, u32[]{:S(2)}) collective-permute-start(bf16[512,3072]{1,0:T(8,128)(2,1)} %get-tuple-element.29), channel_id=1, source_target_pairs={{0,1},{1,2},{2,3},{3,4},{4,5},{5,6},{6,7},{7,8},{8,9},{9,10},{10,1... | collective-permute-start | bytes 9437192 | tf_op jit(solution)/shard_map/ppermute | solution.py:9
  156.3 1.0 copy-start.2
  164.6 6.7 %copy-start.1 = (bf16[8,64,8,64]{3,2,1,0:T(8,128)(2,1)S(1)}, bf16[8,64,8,64]{3,2,1,0:T(8,128)(2,1)}, u32[]{:S(2)}) copy-start(bf16[8,64,8,64]{3,2,1,0:T(8,128)(2,1)} %reshape.80) | copy-start | bytes 1572868
  164.6 6.7 %copy-start.4 = (bf16[8,64,8,64]{1,2,3,0:T(8,128)(2,1)S(1)}, bf16[8,64,8,64]{1,2,3,0:T(8,128)(2,1)}, u32[]{:S(2)}) copy-start(bf16[8,64,8,64]{1,2,3,0:T(8,128)(2,1)} %fusion.2) | copy-start | bytes 1572868
  171.3 1.2 copy-start.3
  171.3 1.5 copy-start.5
  172.8 147.6 %slice-start = ((s8[6291456]{0:T(1024)(128)(4,1)}), s8[2097152]{0:T(1024)(128)(4,1)S(1)}, s32[]{:S(2)}) async-start(s8[6291456]{0:T(1024)(128)(4,1)} %bitcast.44), calls=%async_computation.1 | async-start | bytes 4194304
  316.4 4.0 %slice-start.1 = ((s8[6291456]{0:T(1024)(128)(4,1)}), s8[4194304]{0:T(1024)(128)(4,1)S(1)}, s32[]{:S(2)}) async-start(s8[6291456]{0:T(1024)(128)(4,1)} %bitcast.44), calls=%async_computation.2 | async-start | bytes 8388608
Sparse Core Ops, SparseCore 0:
  54.8 79.1 all-reduce.2
where the time goes:
time: 334 us; the launch traced here: 333 us
  blocking collectives  143 us (43%)
  waiting for transfers between devices  102 us (31%)
  matrix products  24.7 us (7%)
  local copies, waits for them, and re-layouts  20.8 us (6%)
  between operations  14.8 us (4%)
  other arithmetic  14.4 us (4%)
  starting transfers between devices  13.5 us (4%)
    psum x1, blocking collectives, body(): total_density = lax.psum(local_density, 'occ')  143 us
    psum x1, waiting for transfers between devices, pair_terms(): lax.psum(partial_value.astype(jnp.bfloat16), 'aux').astype(jnp.float32)  72.3 us
    ppermute x3, waiting for transfers between devices, passed_along(): lax.ppermute(value, axis, [(i, (i + by) % count) for i in range(count)])  29.5 us
    ppermute x3, starting transfers between devices, passed_along(): lax.ppermute(value, axis, [(i, (i + by) % count) for i in range(count)])  13.5 us
    dot_general x2, matrix products, contract_rows(): lax.dot_general(left, right, (((1,), (1,)), ((), ())), preferred_element_...  8.23 us
  transfers between devices with their start and end apart: 4, of which 2 were waited for; matrix products, arithmetic and copies ran while one was open for 9% of the time, Pallas kernels for 0%

commit v1 on v0

v1 whole, which is shorter than its diff:
```python
import functools

import jax
import jax.numpy as jnp
from jax import lax
from jax.experimental import pallas as pl
from jax.experimental.pallas import tpu as pltpu
from jax.sharding import PartitionSpec as P

F32 = jnp.float32
BF16 = jnp.bfloat16
MIB = 1 << 20
X = 4
Q = 128


def params(mib):
    return pltpu.CompilerParams(
        dimension_semantics=("arbitrary",), vmem_limit_bytes=mib * MIB
    )


def rows_product(left, right):
    return lax.dot_general(left, right, (((1,), (1,)), ((), ())), preferred_element_type=F32)


def product(left, right):
    return lax.dot_general(left, right, (((1,), (0,)), ((), ())), preferred_element_type=F32)


def early_integrals_kernel(info, own, other, o0, o1, o2, o3, total_own, total_inner):
    step = pl.program_id(0)

    @pl.when(step == 0)
    def _():
        total_own[...] = jnp.zeros_like(total_own)
        total_inner[...] = jnp.zeros_like(total_inner)

    mine = own[...]
    theirs = other[...]
    total_own[...] += rows_product(mine, mine)

    def half(block, parity):
        return jnp.concatenate(
            [block[(2 * q + parity) * 64 : (2 * q + parity + 1) * 64] for q in range(4)], axis=0
        )

    @pl.when(info[0] == 0)
    def _():
        total_inner[...] += rows_product(half(mine, 0), theirs)

    @pl.when(info[0] == 1)
    def _():
        total_inner[...] += rows_product(half(theirs, 1), mine)

    @pl.when(step == pl.num_programs(0) - 1)
    def _():
        for d, out in enumerate((o0, o1, o2, o3)):
            q = lax.rem(info[1] + d, X)
            out[0:128, :] = total_own[pl.ds(pl.multiple_of(q * 128, 128), 128), :].astype(BF16)
            out[128:192, :] = total_inner[pl.ds(pl.multiple_of(q * 64, 64), 64), :].astype(BF16)


def early_integrals(info, own, other):
    rows, aux = own.shape
    width = 768
    slab = pl.BlockSpec((rows, width), lambda s, info: (0, s))
    piece = pl.BlockSpec((192, rows), lambda s, info: (0, 0))
    return pl.pallas_call(
        early_integrals_kernel,
        grid_spec=pltpu.PrefetchScalarGridSpec(
            num_scalar_prefetch=1,
            grid=(aux // width,),
            in_specs=[slab, slab],
            out_specs=[piece] * 4,
            scratch_shapes=[pltpu.VMEM((rows, rows), F32), pltpu.VMEM((rows // 2, rows), F32)],
        ),
        out_shape=[jax.ShapeDtypeStruct((192, rows), BF16)] * 4,
        compiler_params=params(32),
        cost_estimate=pl.CostEstimate(
            flops=3 * rows * rows * aux, bytes_accessed=4 * rows * aux, transcendentals=0
        ),
        name="early_integrals",
    )(info, own, other)


def late_integrals_kernel(info, own, following, o0, o1, o2, o3, total):
    step = pl.program_id(0)

    @pl.when(info[0] == 1)
    def _():
        @pl.when(step == 0)
        def _():
            total[...] = jnp.zeros_like(total)

        total[...] += rows_product(own[...], following[...])

        @pl.when(step == pl.num_programs(0) - 1)
        def _():
            for d, out in enumerate((o0, o1, o2, o3)):
                q = lax.rem(info[1] + d, X)
                out[...] = total[pl.ds(pl.multiple_of(q * 128, 128), 128), :].astype(BF16)

    @pl.when(jnp.logical_and(info[0] == 0, step == 0))
    def _():
        for out in (o0, o1, o2, o3):
            out[...] = jnp.zeros_like(out)


def late_integrals(info, own, following):
    rows, aux = own.shape
    width = 768
    slab = pl.BlockSpec((rows, width), lambda s, info: (0, s * info[0]))
    piece = pl.BlockSpec((Q, rows), lambda s, info: (0, 0))
    return pl.pallas_call(
        late_integrals_kernel,
        grid_spec=pltpu.PrefetchScalarGridSpec(
            num_scalar_prefetch=1,
            grid=(aux // width,),
            in_specs=[slab, slab],
            out_specs=[piece] * 4,
            scratch_shapes=[pltpu.VMEM((rows, rows), F32)],
        ),
        out_shape=[jax.ShapeDtypeStruct((Q, rows), BF16)] * 4,
        compiler_params=params(32),
        cost_estimate=pl.CostEstimate(
            flops=2 * rows * rows * aux, bytes_accessed=4 * rows * aux, transcendentals=0
        ),
        name="late_integrals",
    )(info, own, following)


def block_transposed(wide):
    turned = wide.T
    top, bottom = turned[:64], turned[64:]
    low = lax.broadcasted_iota(jnp.int32, (64, 128), 1) < 64
    first = jnp.where(low, top, pltpu.roll(bottom, 64, 1))
    second = jnp.where(low, pltpu.roll(top, 64, 1), bottom)
    return jnp.concatenate([first, second], axis=0), turned


def diagonal_blocks(square):
    return square[:64, :64] + pltpu.roll(square[64:, :], 64, 1)[:, :64]


def tilde_rows(integrals, gap_left, gap_right, keep, store):
    first = jnp.zeros((128, 128), F32)
    second = jnp.zeros((128, 128), F32)
    for J in range(4):
        at = slice(J * 128, (J + 1) * 128)
        amp = (keep * integrals(at) / (gap_left + gap_right[:, at])).astype(BF16)
        wide = amp.astype(F32)
        swapped, turned = block_transposed(wide)
        tilde_wide = (2.0 * wide - swapped).astype(BF16).astype(F32)
        tilde = tilde_wide.astype(BF16)
        tilde_turned = tilde_wide.T.astype(BF16)
        first += rows_product(tilde, amp)
        second += rows_product(tilde_turned, turned.astype(BF16))
        store(J, tilde, tilde_turned)
    return diagonal_blocks(first), diagonal_blocks(second)


def early_tilde_kernel(info, keep, sums, inner_other, gl_own, gr_own, gl_in, gr_in, out, density):
    def store_own(J, tilde, turned):
        out[J] = tilde

    own_first, _ = tilde_rows(
        lambda at: sums[0:128, at], gl_own[...], gr_own[...], 1.0, store_own
    )
    left_home = info[0] == 0

    def inner(at):
        mine, theirs = sums[128:192, at], inner_other[:, at]
        return jnp.concatenate(
            [jnp.where(left_home, mine, theirs), jnp.where(left_home, theirs, mine)], axis=0
        )

    def store_inner(J, tilde, turned):
        out[4 + J] = jnp.where(left_home, tilde, turned)

    first, second = tilde_rows(inner, gl_in[...], gr_in[...], keep[0], store_inner)
    density[...] = own_first + jnp.where(left_home, first + second, 0.0)


SMEM = pl.BlockSpec(memory_space=pltpu.SMEM)
VMEM = pl.BlockSpec(memory_space=pltpu.VMEM)


def early_tilde(info, keep, sums, inner_other, *gaps):
    return pl.pallas_call(
        early_tilde_kernel,
        in_specs=[SMEM, SMEM] + [VMEM] * 6,
        out_specs=[VMEM, VMEM],
        out_shape=[jax.ShapeDtypeStruct((8, 128, 128), BF16), jax.ShapeDtypeStruct((64, 64), F32)],
        compiler_params=pltpu.CompilerParams(vmem_limit_bytes=32 * MIB),
        cost_estimate=pl.CostEstimate(flops=1 << 26, bytes_accessed=1 << 20, transcendentals=0),
        name="early_tilde",
    )(info, keep, sums, inner_other, *gaps)


def late_tilde_kernel(info, keep, mine, partner, near, far, early, gl, gr, out, density):
    left_home = info[0] == 1

    def outer(at):
        here = mine[:, at].astype(F32) + partner[:, at].astype(F32)
        there = near[:, at].astype(F32) + far[:, at].astype(F32)
        return jnp.where(left_home, here, there)

    def store(J, tilde, turned):
        out[J] = jnp.where(left_home, tilde, turned)

    first, second = tilde_rows(outer, gl[...], gr[...], keep[1], store)
    density[...] = early[...] + jnp.where(left_home, first + second, 0.0)


def late_tilde(info, keep, *rest):
    return pl.pallas_call(
        late_tilde_kernel,
        in_specs=[SMEM, SMEM] + [VMEM] * 7,
        out_specs=[VMEM, VMEM],
        out_shape=[jax.ShapeDtypeStruct((4, 128, 128), BF16), jax.ShapeDtypeStruct((64, 64), F32)],
        compiler_params=pltpu.CompilerParams(vmem_limit_bytes=32 * MIB),
        cost_estimate=pl.CostEstimate(flops=1 << 25, bytes_accessed=1 << 20, transcendentals=0),
        name="late_tilde",
    )(info, keep, *rest)


def early_gamma_kernel(info, p0, p1, p2, p3, own, other, out, factors):
    @pl.when(pl.program_id(0) == 0)
    def _():
        for d, piece in enumerate((p0, p1, p2, p3)):
            q = lax.rem(info[1] + X - d, X)
            here = pl.ds(pl.multiple_of(q * 128, 128), 128)
            for J in range(4):
                factors[here, J * 128 : (J + 1) * 128] = piece[J]

            @pl.when(info[0] == 0)
            def _():
                for J in range(4):
                    factors[here, 512 + J * 128 : 512 + (J + 1) * 128] = piece[4 + J]

            @pl.when(info[0] == 1)
            def _():
                column = pl.ds(pl.multiple_of(512 + q * 128, 128), 128)
                for J in range(4):
                    factors[J * 128 : (J + 1) * 128, column] = piece[4 + J]

    out[...] = product(factors[:, :512], own[...]) + product(factors[:, 512:], other[...])


def early_gamma(info, pieces, own, other):
    rows, aux = own.shape
    width = 768
    slab = pl.BlockSpec((rows, width), lambda s, info: (0, s))
    piece = pl.BlockSpec((8, 128, 128), lambda s, info: (0, 0, 0))
    return pl.pallas_call(
        early_gamma_kernel,
        grid_spec=pltpu.PrefetchScalarGridSpec(
            num_scalar_prefetch=1,
            grid=(aux // width,),
            in_specs=[piece] * 4 + [slab, slab],
            out_specs=slab,
            scratch_shapes=[pltpu.VMEM((rows, 2 * rows), BF16)],
        ),
        out_shape=jax.ShapeDtypeStruct((rows, aux), F32),
        compiler_params=params(32),
        cost_estimate=pl.CostEstimate(
            flops=4 * rows * rows * aux, bytes_accessed=8 * rows * aux, transcendentals=0
        ),
        name="early_gamma",
    )(info, *pieces, own, other)


def late_gamma_kernel(info, p0, p1, p2, p3, early, following, preceding, out, factors):
    @pl.when(pl.program_id(0) == 0)
    def _():
        for d, piece in enumerate((p0, p1, p2, p3)):
            q = lax.rem(info[1] + X - d, X)
            here = pl.ds(pl.multiple_of(q * 128, 128), 128)

            @pl.when(info[0] == 1)
            def _():
                for J in range(4):
                    factors[here, J * 128 : (J + 1) * 128] = piece[J]

            @pl.when(info[0] == 0)
            def _():
                for J in range(4):
                    factors[J * 128 : (J + 1) * 128, here] = piece[J]

    @pl.when(info[0] == 1)
    def _():
        out[...] = (early[...] + product(factors[...], following[...])).astype(BF16)

    @pl.when(info[0] == 0)
    def _():
        out[...] = (early[...] + product(factors[...], preceding[...])).astype(BF16)


def late_gamma(info, pieces, early, following, preceding):
    rows, aux = early.shape
    width = 768
    slab = pl.BlockSpec((rows, width), lambda s, info: (0, s))
    on_left = pl.BlockSpec((rows, width), lambda s, info: (0, s * info[0]))
    on_right = pl.BlockSpec((rows, width), lambda s, info: (0, s * (1 - info[0])))
    piece = pl.BlockSpec((4, 128, 128), lambda s, info: (0, 0, 0))
    return pl.pallas_call(
        late_gamma_kernel,
        grid_spec=pltpu.PrefetchScalarGridSpec(
            num_scalar_prefetch=1,
            grid=(aux // width,),
            in_specs=[piece] * 4 + [slab, on_left, on_right],
            out_specs=slab,
            scratch_shapes=[pltpu.VMEM((rows, rows), BF16)],
        ),
        out_shape=jax.ShapeDtypeStruct((rows, aux), BF16),
        compiler_params=params(32),
        cost_estimate=pl.CostEstimate(
            flops=2 * rows * rows * aux, bytes_accessed=8 * rows * aux, transcendentals=0
        ),
        name="late_gamma",
    )(info, *pieces, early, following, preceding)


def along_x(value, by):
    return lax.ppermute(
        value, "aux", [(a, a // X * X + (a + by) % X) for a in range(lax.axis_size("aux"))]
    )


def across_y(value):
    count = lax.axis_size("aux")
    return lax.ppermute(value, "aux", [(a, (a + X) % count) for a in range(count)])


def left_homes_to(value, forward, by=0, turn=0):
    aux, occ = lax.axis_size("aux"), lax.axis_size("occ")

    def aux_to(a):
        return (a // X * X + turn * X) % aux + (a + by) % X

    return lax.ppermute(
        value,
        ("aux", "occ"),
        [
            (a * occ + k, aux_to(a) * occ + (k + forward) % occ)
            for a in range(aux)
            for k in range(1, occ, 2)
        ],
    )


def swapped(value, axis, other):
    return lax.ppermute(value, axis, [(k, other(k)) for k in range(lax.axis_size(axis))])


def after(value, *earlier):
    return lax.optimization_barrier((value, *earlier))[0]


def gap(energy, virt_energy):
    return (energy.astype(F32)[:, None] - virt_energy.astype(F32)[None, :]).reshape(-1)


def body(orbital_slabs, occ_energy, virt_energy, pair_kept):
    occ_count, virt_count, aux_count = orbital_slabs.shape
    rows = occ_count * virt_count
    occ = lax.axis_size("occ")
    slabs = orbital_slabs.reshape(rows, aux_count)
    place = lax.axis_index("occ")
    core = lax.rem(place, 2)
    x = lax.rem(lax.axis_index("aux"), X)
    info = jnp.stack([core, x]).astype(jnp.int32)

    def outer_partner(k):
        return (k + 1) % occ if k % 2 else (k - 1) % occ

    following = lax.ppermute(slabs, "occ", [(k, (k - 1) % occ) for k in range(0, occ, 2)])
    other = swapped(slabs, "occ", lambda k: k ^ 1)
    inner_energy = swapped(occ_energy, "occ", lambda k: k ^ 1)
    outer_energy = swapped(occ_energy, "occ", outer_partner)

    own_gap = gap(occ_energy, virt_energy)
    inner_gap = gap(inner_energy, virt_energy)
    outer_gap = gap(outer_energy, virt_energy)
    first_core = core == 0

    def rows_of(values):
        return lax.dynamic_slice_in_dim(values, x * Q, Q, 0).reshape(Q, 1)

    gl_own, gr_own = rows_of(own_gap), own_gap.reshape(1, rows)
    gl_in = rows_of(jnp.where(first_core, own_gap, inner_gap))
    gr_in = jnp.where(first_core, inner_gap, own_gap).reshape(1, rows)
    gl_out = rows_of(jnp.where(first_core, outer_gap, own_gap))
    gr_out = jnp.where(first_core, own_gap, outer_gap).reshape(1, rows)
    keep_in = pair_kept[place - core].astype(F32)
    keep_out = pair_kept[lax.rem(place - 1 + core + occ, occ)].astype(F32)
    keep = jnp.stack([keep_in, keep_out])

    pieces = early_integrals(info, slabs, other)
    arrived = [along_x(pieces[d], d) for d in (1, 2, 3)]
    sums = pieces[0].astype(F32)
    for value in arrived:
        sums = sums + value.astype(F32)
    sums = sums.astype(BF16)
    sums = sums.astype(F32) + across_y(sums).astype(F32)
    inner_other = swapped(sums[Q:], "occ", lambda k: k ^ 1)
    tilde, density = early_tilde(info, keep, sums, inner_other, gl_own, gr_own, gl_in, gr_in)
    gathered = [tilde] + [along_x(tilde, d) for d in (1, 2, 3)]
    early = early_gamma(info, gathered, slabs, other)

    preceding = lax.ppermute(
        after(slabs, following), "occ", [(k, (k + 1) % occ) for k in range(1, occ, 2)]
    )
    pieces = late_integrals(info, slabs, following)
    arrived = [left_homes_to(pieces[d], 0, by=d) for d in (1, 2, 3)]
    sums = pieces[0].astype(F32)
    for value in arrived:
        sums = sums + value.astype(F32)
    sums = sums.astype(BF16)
    partner = left_homes_to(sums, 0, turn=1)
    near = left_homes_to(sums, 1)
    far = left_homes_to(sums, 1, turn=1)
    tilde, density = late_tilde(info, keep, sums, partner, near, far, density, gl_out, gr_out)
    gathered = [tilde] + [along_x(tilde, d) for d in (1, 2, 3)]

    count = lax.axis_size("aux")
    for bit in (1, 2):
        density = density + lax.ppermute(density, "aux", [(a, a ^ bit) for a in range(count)])
    bit = 1
    while bit < occ:
        density = density + swapped(density, "occ", lambda k, bit=bit: k ^ bit)
        bit *= 2
    virt_density = density / (4.0 * occ_count * occ_count * virt_count)

    gamma = late_gamma(info, gathered, early, following, preceding)
    return gamma.reshape(occ_count, virt_count, aux_count), virt_density


def solution(mesh):
    return jax.shard_map(
        body,
        mesh=mesh,
        in_specs=(P("occ", None, "aux"), P("occ"), P(), P()),
        out_specs=(P("occ", None, "aux"), P()),
        check_vma=False,
    )
```

time: 334 us -> 180 us (0.54)
  blocking collectives: 143 us -> 0 us
  starting transfers between devices: 13.5 us -> 42.9 us
  matrix products: 24.7 us -> 0 us
  Pallas kernels: 0 us -> 23.4 us
  local copies, waits for them, and re-layouts: 20.8 us -> 7.96 us
  between operations: 14.8 us -> 2.17 us
  other arithmetic: 14.4 us -> 3.58 us
    psum x1 -> x0, blocking collectives: 143 us -> none  [body(): total_density = lax.psum(local_density, 'occ')]
    psum x1 -> x0, waiting for transfers between devices: 72.3 us -> none  [pair_terms(): lax.psum(partial_value.astype(jnp.bfloat16), 'aux').astype(jnp.float32)]
    ppermute x3 -> x29, waiting for transfers between devices: 29.5 us -> 99.6 us  [the longest x9 48.1 us: swapped(): lax.ppermute(value, axis, [(k, other(k)) for k in range(lax.axis_size(axi...]
    ppermute x3 -> x29, starting transfers between devices: 13.5 us -> 42.9 us  [the longest x9 13.8 us: along_x(): lax.ppermute(value, 'aux', [(a, a // X * X + (a + by) % X) for a in range...]
    dot_general x8 -> x0, matrix products: 24.7 us -> none  [the longest x2 8.23 us: contract_rows(): lax.dot_general(left, right, (((1,), (1,)), ((), ())), preferred_element_...]
    pallas_call x0 -> x6, Pallas kernels: none -> 23.4 us  [the longest x1 7.2 us: early_integrals(): pl.pallas_call(early_integrals_kernel, grid_spec=pltpu.PrefetchScalarGrid...]
    convert_element_type x7 -> x6, other arithmetic: 12.2 us -> 2.64 us  [the longest x2 1.29 us: body(): sums = sums.astype(BF16)]
    reshape x5, local copies, waits for them, and re-layouts: 10.1 us -> 1.75 us  [rows_of(): return lax.dynamic_slice_in_dim(values, x * Q, Q, 0).reshape(Q, 1)]
  transfers between devices with their start and end apart: 4 -> 29, of which waited for: 2 -> 13; matrix products, arithmetic and copies ran while one was open for 9% -> 4% of each run, Pallas kernels for 0% -> 10%
where the time goes in v1:
time: 180 us
  waiting for transfers between devices  99.6 us (55%)
  starting transfers between devices  42.9 us (24%)
  Pallas kernels  23.4 us (13%)
  local copies, waits for them, and re-layouts  7.96 us (4%)
  other arithmetic  3.58 us (2%)
  between operations  2.17 us (1%)
    ppermute x9, waiting for transfers between devices, swapped(): lax.ppermute(value, axis, [(k, other(k)) for k in range(lax.axis_size(axi...  48.1 us
    ppermute x1, waiting for transfers between devices, body(): lax.ppermute(slabs, 'occ', [(k, (k - 1) % occ) for k in range(0, occ, 2)])  34.8 us
    ppermute x9, starting transfers between devices, along_x(): lax.ppermute(value, 'aux', [(a, a // X * X + (a + by) % X) for a in range...  13.8 us
    ppermute x1, starting transfers between devices, body(): lax.ppermute(slabs, 'occ', [(k, (k - 1) % occ) for k in range(0, occ, 2)])  10 us
    ppermute x9, starting transfers between devices, swapped(): lax.ppermute(value, axis, [(k, other(k)) for k in range(lax.axis_size(axi...  9.84 us
    ppermute x2, waiting for transfers between devices, body(): lax.ppermute(density, 'aux', [(a, a ^ bit) for a in range(count)])  7.51 us
    pallas_call x1, Pallas kernels, early_integrals(): pl.pallas_call(early_integrals_kernel, grid_spec=pltpu.PrefetchScalarGrid...  7.2 us
    pallas_call x1, Pallas kernels, early_gamma(): pl.pallas_call(early_gamma_kernel, grid_spec=pltpu.PrefetchScalarGridSpec...  6.51 us
  transfers between devices with their start and end apart: 29, of which 13 were waited for; matrix products, arithmetic and copies ran while one was open for 4% of the time, Pallas kernels for 10%

profile of v1, /device:TPU:2, one launch (start us, length us, event | category | flops | bytes accessed | tf_op | source)
XLA Modules:
  0.0 179.5 jit_solution(14015453555934112523)
XLA Ops:
  0.6 10.0 %collective-permute-start = (bf16[512,3072]{1,0:T(8,128)(2,1)}, bf16[512,3072]{1,0:T(8,128)(2,1)S(1)}, u32[]{:S(2)}, u32[]{:S(2)}) collective-permute-start(bf16[512,3072]{1,0:T(8,128)(2,1)} %bitcast.10), channel_id=1, source_target_pairs={{0,31},{2,1},{4,3},{6,5},{8,7},{10,9},{12,11},{14,13},{16,15},{18,... | collective-permute-start | bytes 9437192 | tf_op jit(solution)/shard_map/ppermute | solution.py:378
  10.8 34.8 %collective-permute-done.following = bf16[512,3072]{1,0:T(8,128)(2,1)S(1)} collective-permute-done((bf16[512,3072]{1,0:T(8,128)(2,1)}, bf16[512,3072]{1,0:T(8,128)(2,1)S(1)}, u32[]{:S(2)}, u32[]{:S(2)}) %collective-permute-start) | collective-permute-done | bytes 3145760 | tf_op jit(solution)/shard_map/ppermute | solution.py:378
  46.8 7.7 %collective-permute-start.14 = (bf16[8]{0:T(256)(128)(2,1)}, bf16[8]{0:T(256)(128)(2,1)S(1)}, u32[]{:S(2)}, u32[]{:S(2)}) collective-permute-start(bf16[8]{0:T(256)(128)(2,1)} %param.5), channel_id=1, source_target_pairs={{0,31},{1,2},{2,1},{3,4},{4,3},{5,6},{6,5},{7,8},{8,7},{9,10},{10,... | collective-permute-start | bytes 56 | tf_op jit(solution)/shard_map/ppermute | solution.py:354
  58.7 29.4 %collective-permute-done.14 = bf16[8]{0:T(256)(128)(2,1)S(1)} collective-permute-done((bf16[8]{0:T(256)(128)(2,1)}, bf16[8]{0:T(256)(128)(2,1)S(1)}, u32[]{:S(2)}, u32[]{:S(2)}) %collective-permute-start.14) | collective-permute-done | bytes 48 | tf_op jit(solution)/shard_map/ppermute | solution.py:354
  89.1 1.9 %copy-done = bf16[8,64,3072]{2,1,0:T(8,128)(2,1)S(1)} copy-done((bf16[8,64,3072]{2,1,0:T(8,128)(2,1)S(1)}, bf16[8,64,3072]{2,1,0:T(8,128)(2,1)}, u32[]{:S(2)}) %copy-start) | copy-done | bytes 3145752
  90.9 7.2 %early_integrals.1 = (bf16[192,512]{1,0:T(8,128)(2,1)S(1)}, bf16[192,512]{1,0:T(8,128)(2,1)}, bf16[192,512]{1,0:T(8,128)(2,1)}, bf16[192,512]{1,0:T(8,128)(2,1)}) custom-call(s32[2]{0:T(128)S(1)} %pad_add_fusion.info, bf16[512,3072]{1,0:T(8,128)(2,1)S(1)} %bitcast.13, bf16[512,3072]{1,0:T(8,128)(2,1)} %collective-permute-done.7.other), custom_call_target="tpu_custom_call" | custom-call | flops 2415919104 | bytes 6291456 | tf_op jit(solution)/shard_map/early_integrals/pallas_call | solution.py:69
  98.1 1.5 collective-permute-start.8
  100.8 2.2 %collective-permute-start.10 = (bf16[192,512]{1,0:T(8,128)(2,1)}, bf16[192,512]{1,0:T(8,128)(2,1)}, u32[]{:S(2)}, u32[]{:S(2)}) collective-permute-start(bf16[192,512]{1,0:T(8,128)(2,1)} %get-tuple-element.22), channel_id=1, source_target_pairs={{0,96},{32,0},{64,32},{96,64},{128,224},{160,128},{192,160},{224,1... | collective-permute-start | bytes 589832 | tf_op jit(solution)/shard_map/ppermute | solution.py:326
  104.8 1.9 %copy-done.1 = bf16[8,64,3072]{2,1,0:T(8,128)(2,1)S(1)} copy-done((bf16[8,64,3072]{2,1,0:T(8,128)(2,1)S(1)}, bf16[8,64,3072]{2,1,0:T(8,128)(2,1)}, u32[]{:S(2)}) %copy-start.1) | copy-done | bytes 3145752
  115.3 2.6 %collective-permute-done.11 = bf16[192,512]{1,0:T(8,128)(2,1)S(1)} collective-permute-done((bf16[192,512]{1,0:T(8,128)(2,1)S(1)}, bf16[192,512]{1,0:T(8,128)(2,1)S(1)}, u32[]{:S(2)}, u32[]{:S(2)}) %collective-permute-start.11) | collective-permute-done | bytes 196640 | tf_op jit(solution)/shard_map/ppermute | solution.py:333
  120.8 4.6 %collective-permute-done.6.far = bf16[128,512]{1,0:T(8,128)(2,1)S(1)} collective-permute-done((bf16[128,512]{1,0:T(8,128)(2,1)S(1)}, bf16[128,512]{1,0:T(8,128)(2,1)S(1)}, u32[]{:S(2)}, u32[]{:S(2)}) %collective-permute-start.6) | collective-permute-done | bytes 131104 | tf_op jit(solution)/shard_map/ppermute | solution.py:342
  125.4 1.6 collective-permute-done.5.near
  128.6 3.6 %collective-permute-done.22 = f32[64,64]{1,0:T(8,128)S(1)} collective-permute-done((f32[64,64]{1,0:T(8,128)S(1)}, f32[64,64]{1,0:T(8,128)S(1)}, u32[]{:S(2)}, u32[]{:S(2)}) %collective-permute-start.22) | collective-permute-done | bytes 16416 | tf_op jit(solution)/shard_map/ppermute | solution.py:429
  132.2 1.5 collective-permute-start.23
  133.7 3.9 %collective-permute-done.23 = f32[64,64]{1,0:T(8,128)S(1)} collective-permute-done((f32[64,64]{1,0:T(8,128)S(1)}, f32[64,64]{1,0:T(8,128)S(1)}, u32[]{:S(2)}, u32[]{:S(2)}) %collective-permute-start.23) | collective-permute-done | bytes 16416 | tf_op jit(solution)/shard_map/ppermute | solution.py:429
  138.9 5.4 %collective-permute-done.25 = f32[64,64]{1,0:T(8,128)S(1)} collective-permute-done((f32[64,64]{1,0:T(8,128)S(1)}, f32[64,64]{1,0:T(8,128)S(1)}, u32[]{:S(2)}, u32[]{:S(2)}) %collective-permute-start.25) | collective-permute-done | bytes 16416 | tf_op jit(solution)/shard_map/ppermute | solution.py:354
  146.3 2.4 %collective-permute-start.18 = (bf16[8,128,128]{2,1,0:T(8,128)(2,1)S(1)}, bf16[8,128,128]{2,1,0:T(8,128)(2,1)S(1)}, u32[]{:S(2)}, u32[]{:S(2)}) collective-permute-start(bf16[8,128,128]{2,1,0:T(8,128)(2,1)S(1)} %get-tuple-element.25.p0), channel_id=1, source_target_pairs={{0,32},{32,64},{64,96},{96,0},{128,160},{160,192},{192,224},{224,1... | collective-permute-start | bytes 786440 | tf_op jit(solution)/shard_map/ppermute | solution.py:326
  148.8 4.8 %collective-permute-done.27 = f32[64,64]{1,0:T(8,128)S(1)} collective-permute-done((f32[64,64]{1,0:T(8,128)S(1)}, f32[64,64]{1,0:T(8,128)S(1)}, u32[]{:S(2)}, u32[]{:S(2)}) %collective-permute-start.27) | collective-permute-done | bytes 16416 | tf_op jit(solution)/shard_map/ppermute | solution.py:354
  153.6 1.9 %collective-permute-start.28 = (f32[64,64]{1,0:T(8,128)S(1)}, f32[64,64]{1,0:T(8,128)S(1)}, u32[]{:S(2)}, u32[]{:S(2)}) collective-permute-start(f32[64,64]{1,0:T(8,128)S(1)} %add.77), channel_id=1, source_target_pairs={{0,16},{1,17},{2,18},{3,19},{4,20},{5,21},{6,22},{7,23},{8,24},{9,... | collective-permute-start | bytes 49160 | tf_op jit(solution)/shard_map/ppermute | solution.py:354
  155.5 5.9 %collective-permute-done.28 = f32[64,64]{1,0:T(8,128)S(1)} collective-permute-done((f32[64,64]{1,0:T(8,128)S(1)}, f32[64,64]{1,0:T(8,128)S(1)}, u32[]{:S(2)}, u32[]{:S(2)}) %collective-permute-start.28) | collective-permute-done | bytes 16416 | tf_op jit(solution)/shard_map/ppermute | solution.py:354
  162.1 2.0 %collective-permute-start.16 = (bf16[4,128,128]{2,1,0:T(8,128)(2,1)S(1)}, bf16[4,128,128]{2,1,0:T(8,128)(2,1)S(1)}, u32[]{:S(2)}, u32[]{:S(2)}) collective-permute-start(bf16[4,128,128]{2,1,0:T(8,128)(2,1)S(1)} %get-tuple-element.24.p0), channel_id=1, source_target_pairs={{0,64},{32,96},{64,0},{96,32},{128,192},{160,224},{192,128},{224,1... | collective-permute-start | bytes 393224 | tf_op jit(solution)/shard_map/ppermute | solution.py:326
  164.1 2.6 %collective-permute-start.15 = (bf16[4,128,128]{2,1,0:T(8,128)(2,1)S(1)}, bf16[4,128,128]{2,1,0:T(8,128)(2,1)S(1)}, u32[]{:S(2)}, u32[]{:S(2)}) collective-permute-start(bf16[4,128,128]{2,1,0:T(8,128)(2,1)S(1)} %get-tuple-element.24.p0), channel_id=1, source_target_pairs={{0,32},{32,64},{64,96},{96,0},{128,160},{160,192},{192,224},{224,1... | collective-permute-start | bytes 393224 | tf_op jit(solution)/shard_map/ppermute | solution.py:326
  166.7 6.5 %early_gamma.1.early = f32[512,3072]{1,0:T(8,128)S(1)} custom-call(s32[2]{0:T(128)S(1)} %pad_add_fusion.info, bf16[8,128,128]{2,1,0:T(8,128)(2,1)S(1)} %get-tuple-element.25.p0, bf16[8,128,128]{2,1,0:T(8,128)(2,1)S(1)} %collective-permute-done.18.p1, bf16[8,128,128]{2,1,0:T(8,128)(2,1)S(1)} %collective-permute-done.19.p2, ...), custom_call_target="tpu_custom_call" | custom-call | flops 3221225472 | bytes 12582912 | tf_op jit(solution)/shard_map/early_gamma/pallas_call | solution.py:256
  173.3 6.3 %late_gamma.1 = bf16[512,3072]{1,0:T(8,128)(2,1)} custom-call(s32[2]{0:T(128)S(1)} %pad_add_fusion.info, bf16[4,128,128]{2,1,0:T(8,128)(2,1)S(1)} %get-tuple-element.24.p0, bf16[4,128,128]{2,1,0:T(8,128)(2,1)S(1)} %collective-permute-done.15.p1, bf16[4,128,128]{2,1,0:T(8,128)(2,1)S(1)} %collective-permute-done.16.p2, ...), custom_call_target="tpu_custom_call" | custom-call | flops 1610612736 | bytes 12582912 | tf_op jit(solution)/shard_map/late_gamma/pallas_call | solution.py:307
  (80 shorter events, 25.1 us)
Async XLA Ops:
  0.6 44.9 %collective-permute-start = (bf16[512,3072]{1,0:T(8,128)(2,1)}, bf16[512,3072]{1,0:T(8,128)(2,1)S(1)}, u32[]{:S(2)}, u32[]{:S(2)}) collective-permute-start(bf16[512,3072]{1,0:T(8,128)(2,1)} %bitcast.10), channel_id=1, source_target_pairs={{0,31},{2,1},{4,3},{6,5},{8,7},{10,9},{12,11},{14,13},{16,15},{18,... | collective-permute-start | bytes 9437192 | tf_op jit(solution)/shard_map/ppermute | solution.py:378
  10.7 78.4 %collective-permute-start.7 = (bf16[512,3072]{1,0:T(8,128)(2,1)}, bf16[512,3072]{1,0:T(8,128)(2,1)}, u32[]{:S(2)}, u32[]{:S(2)}) collective-permute-start(bf16[512,3072]{1,0:T(8,128)(2,1)} %bitcast.11), channel_id=1, source_target_pairs={{0,1},{1,0},{2,3},{3,2},{4,5},{5,4},{6,7},{7,6},{8,9},{9,8},{10,11... | collective-permute-start | bytes 9437192 | tf_op jit(solution)/shard_map/ppermute | solution.py:354
  45.6 127.7 %collective-permute-start.21 = (bf16[512,3072]{1,0:T(8,128)(2,1)}, bf16[512,3072]{1,0:T(8,128)(2,1)}, u32[]{:S(2)}, u32[]{:S(2)}) collective-permute-start(bf16[512,3072]{1,0:T(8,128)(2,1)} %bitcast.12), channel_id=1, source_target_pairs={{1,2},{3,4},{5,6},{7,8},{9,10},{11,12},{13,14},{15,16},{17,18},{19... | collective-permute-start | bytes 9437192 | tf_op jit(solution)/shard_map/ppermute | solution.py:412
  46.8 41.2 %collective-permute-start.14 = (bf16[8]{0:T(256)(128)(2,1)}, bf16[8]{0:T(256)(128)(2,1)S(1)}, u32[]{:S(2)}, u32[]{:S(2)}) collective-permute-start(bf16[8]{0:T(256)(128)(2,1)} %param.5), channel_id=1, source_target_pairs={{0,31},{1,2},{2,1},{3,4},{4,3},{5,6},{6,5},{7,8},{8,7},{9,10},{10,... | collective-permute-start | bytes 56 | tf_op jit(solution)/shard_map/ppermute | solution.py:354
  54.5 33.6 %collective-permute-start.13 = (bf16[8]{0:T(256)(128)(2,1)}, bf16[8]{0:T(256)(128)(2,1)S(1)}, u32[]{:S(2)}, u32[]{:S(2)}) collective-permute-start(bf16[8]{0:T(256)(128)(2,1)} %param.5), channel_id=1, source_target_pairs={{0,1},{1,0},{2,3},{3,2},{4,5},{5,4},{6,7},{7,6},{8,9},{9,8},{10,11... | collective-permute-start | bytes 56 | tf_op jit(solution)/shard_map/ppermute | solution.py:354
  98.1 10.3 %collective-permute-start.8 = (bf16[192,512]{1,0:T(8,128)(2,1)}, bf16[192,512]{1,0:T(8,128)(2,1)}, u32[]{:S(2)}, u32[]{:S(2)}) collective-permute-start(bf16[192,512]{1,0:T(8,128)(2,1)} %get-tuple-element.20), channel_id=1, source_target_pairs={{0,32},{32,64},{64,96},{96,0},{128,160},{160,192},{192,224},{224,1... | collective-permute-start | bytes 589832 | tf_op jit(solution)/shard_map/ppermute | solution.py:326
  99.7 9.6 %collective-permute-start.9 = (bf16[192,512]{1,0:T(8,128)(2,1)}, bf16[192,512]{1,0:T(8,128)(2,1)}, u32[]{:S(2)}, u32[]{:S(2)}) collective-permute-start(bf16[192,512]{1,0:T(8,128)(2,1)} %get-tuple-element.21), channel_id=1, source_target_pairs={{0,64},{32,96},{64,0},{96,32},{128,192},{160,224},{192,128},{224,1... | collective-permute-start | bytes 589832 | tf_op jit(solution)/shard_map/ppermute | solution.py:326
  100.8 9.5 %collective-permute-start.10 = (bf16[192,512]{1,0:T(8,128)(2,1)}, bf16[192,512]{1,0:T(8,128)(2,1)}, u32[]{:S(2)}, u32[]{:S(2)}) collective-permute-start(bf16[192,512]{1,0:T(8,128)(2,1)} %get-tuple-element.22), channel_id=1, source_target_pairs={{0,96},{32,0},{64,32},{96,64},{128,224},{160,128},{192,160},{224,1... | collective-permute-start | bytes 589832 | tf_op jit(solution)/shard_map/ppermute | solution.py:326
  107.6 4.3 %collective-permute-start.1 = (bf16[128,512]{1,0:T(8,128)(2,1)S(1)}, bf16[128,512]{1,0:T(8,128)(2,1)S(1)}, u32[]{:S(2)}, u32[]{:S(2)}) collective-permute-start(bf16[128,512]{1,0:T(8,128)(2,1)S(1)} %get-tuple-element.16), channel_id=1, source_target_pairs={{1,33},{3,35},{5,37},{7,39},{9,41},{11,43},{13,45},{15,47},{17,49}... | collective-permute-start | bytes 393224 | tf_op jit(solution)/shard_map/ppermute | solution.py:342
  111.5 6.4 %collective-permute-start.11 = (bf16[192,512]{1,0:T(8,128)(2,1)S(1)}, bf16[192,512]{1,0:T(8,128)(2,1)S(1)}, u32[]{:S(2)}, u32[]{:S(2)}) collective-permute-start(bf16[192,512]{1,0:T(8,128)(2,1)S(1)} %add_convert_fusion), channel_id=1, source_target_pairs={{0,128},{32,160},{64,192},{96,224},{128,0},{160,32},{192,64},{224,... | collective-permute-start | bytes 589832 | tf_op jit(solution)/shard_map/ppermute | solution.py:333
  112.0 13.4 %collective-permute-start.6 = (bf16[128,512]{1,0:T(8,128)(2,1)S(1)}, bf16[128,512]{1,0:T(8,128)(2,1)S(1)}, u32[]{:S(2)}, u32[]{:S(2)}) collective-permute-start(bf16[128,512]{1,0:T(8,128)(2,1)S(1)} %add_convert_fusion.1.mine), channel_id=1, source_target_pairs={{1,130},{3,132},{5,134},{7,136},{9,138},{11,140},{13,142},{15,144}... | collective-permute-start | bytes 393224 | tf_op jit(solution)/shard_map/ppermute | solution.py:342
  113.3 13.7 %collective-permute-start.5 = (bf16[128,512]{1,0:T(8,128)(2,1)S(1)}, bf16[128,512]{1,0:T(8,128)(2,1)S(1)}, u32[]{:S(2)}, u32[]{:S(2)}) collective-permute-start(bf16[128,512]{1,0:T(8,128)(2,1)S(1)} %add_convert_fusion.1.mine), channel_id=1, source_target_pairs={{1,2},{3,4},{5,6},{7,8},{9,10},{11,12},{13,14},{15,16},{17,18},{19... | collective-permute-start | bytes 393224 | tf_op jit(solution)/shard_map/ppermute | solution.py:342
  114.6 12.4 %collective-permute-start.4 = (bf16[128,512]{1,0:T(8,128)(2,1)S(1)}, bf16[128,512]{1,0:T(8,128)(2,1)S(1)}, u32[]{:S(2)}, u32[]{:S(2)}) collective-permute-start(bf16[128,512]{1,0:T(8,128)(2,1)S(1)} %add_convert_fusion.1.mine), channel_id=1, source_target_pairs={{1,129},{3,131},{5,133},{7,135},{9,137},{11,139},{13,141},{15,143}... | collective-permute-start | bytes 393224 | tf_op jit(solution)/shard_map/ppermute | solution.py:342
  132.2 5.4 %collective-permute-start.23 = (f32[64,64]{1,0:T(8,128)S(1)}, f32[64,64]{1,0:T(8,128)S(1)}, u32[]{:S(2)}, u32[]{:S(2)}) collective-permute-start(f32[64,64]{1,0:T(8,128)S(1)} %add.72), channel_id=1, source_target_pairs={{0,64},{32,96},{64,0},{96,32},{128,192},{160,224},{192,128},{224,1... | collective-permute-start | bytes 49160 | tf_op jit(solution)/shard_map/ppermute | solution.py:429
  138.8 5.4 %collective-permute-start.25 = (f32[64,64]{1,0:T(8,128)S(1)}, f32[64,64]{1,0:T(8,128)S(1)}, u32[]{:S(2)}, u32[]{:S(2)}) collective-permute-start(f32[64,64]{1,0:T(8,128)S(1)} %add.74), channel_id=1, source_target_pairs={{0,2},{1,3},{2,0},{3,1},{4,6},{5,7},{6,4},{7,5},{8,10},{9,11},{10,... | collective-permute-start | bytes 49160 | tf_op jit(solution)/shard_map/ppermute | solution.py:354
  144.3 4.4 %collective-permute-start.26 = (f32[64,64]{1,0:T(8,128)S(1)}, f32[64,64]{1,0:T(8,128)S(1)}, u32[]{:S(2)}, u32[]{:S(2)}) collective-permute-start(f32[64,64]{1,0:T(8,128)S(1)} %add.75), channel_id=1, source_target_pairs={{0,4},{1,5},{2,6},{3,7},{4,0},{5,1},{6,2},{7,3},{8,12},{9,13},{10,... | collective-permute-start | bytes 49160 | tf_op jit(solution)/shard_map/ppermute | solution.py:354
  144.3 17.8 %collective-permute-start.20 = (bf16[8,128,128]{2,1,0:T(8,128)(2,1)S(1)}, bf16[8,128,128]{2,1,0:T(8,128)(2,1)S(1)}, u32[]{:S(2)}, u32[]{:S(2)}) collective-permute-start(bf16[8,128,128]{2,1,0:T(8,128)(2,1)S(1)} %get-tuple-element.25.p0), channel_id=1, source_target_pairs={{0,96},{32,0},{64,32},{96,64},{128,224},{160,128},{192,160},{224,1... | collective-permute-start | bytes 786440 | tf_op jit(solution)/shard_map/ppermute | solution.py:326
  144.8 19.2 %collective-permute-start.19 = (bf16[8,128,128]{2,1,0:T(8,128)(2,1)S(1)}, bf16[8,128,128]{2,1,0:T(8,128)(2,1)S(1)}, u32[]{:S(2)}, u32[]{:S(2)}) collective-permute-start(bf16[8,128,128]{2,1,0:T(8,128)(2,1)S(1)} %get-tuple-element.25.p0), channel_id=1, source_target_pairs={{0,64},{32,96},{64,0},{96,32},{128,192},{160,224},{192,128},{224,1... | collective-permute-start | bytes 786440 | tf_op jit(solution)/shard_map/ppermute | solution.py:326
  146.3 20.4 %collective-permute-start.18 = (bf16[8,128,128]{2,1,0:T(8,128)(2,1)S(1)}, bf16[8,128,128]{2,1,0:T(8,128)(2,1)S(1)}, u32[]{:S(2)}, u32[]{:S(2)}) collective-permute-start(bf16[8,128,128]{2,1,0:T(8,128)(2,1)S(1)} %get-tuple-element.25.p0), channel_id=1, source_target_pairs={{0,32},{32,64},{64,96},{96,0},{128,160},{160,192},{192,224},{224,1... | collective-permute-start | bytes 786440 | tf_op jit(solution)/shard_map/ppermute | solution.py:326
  148.7 4.9 %collective-permute-start.27 = (f32[64,64]{1,0:T(8,128)S(1)}, f32[64,64]{1,0:T(8,128)S(1)}, u32[]{:S(2)}, u32[]{:S(2)}) collective-permute-start(f32[64,64]{1,0:T(8,128)S(1)} %add.76), channel_id=1, source_target_pairs={{0,8},{1,9},{2,10},{3,11},{4,12},{5,13},{6,14},{7,15},{8,0},{9,1},... | collective-permute-start | bytes 49160 | tf_op jit(solution)/shard_map/ppermute | solution.py:354
  153.6 7.8 %collective-permute-start.28 = (f32[64,64]{1,0:T(8,128)S(1)}, f32[64,64]{1,0:T(8,128)S(1)}, u32[]{:S(2)}, u32[]{:S(2)}) collective-permute-start(f32[64,64]{1,0:T(8,128)S(1)} %add.77), channel_id=1, source_target_pairs={{0,16},{1,17},{2,18},{3,19},{4,20},{5,21},{6,22},{7,23},{8,24},{9,... | collective-permute-start | bytes 49160 | tf_op jit(solution)/shard_map/ppermute | solution.py:354
  161.4 11.8 %collective-permute-start.17 = (bf16[4,128,128]{2,1,0:T(8,128)(2,1)S(1)}, bf16[4,128,128]{2,1,0:T(8,128)(2,1)S(1)}, u32[]{:S(2)}, u32[]{:S(2)}) collective-permute-start(bf16[4,128,128]{2,1,0:T(8,128)(2,1)S(1)} %get-tuple-element.24.p0), channel_id=1, source_target_pairs={{0,96},{32,0},{64,32},{96,64},{128,224},{160,128},{192,160},{224,1... | collective-permute-start | bytes 393224 | tf_op jit(solution)/shard_map/ppermute | solution.py:326
  162.1 11.2 %collective-permute-start.16 = (bf16[4,128,128]{2,1,0:T(8,128)(2,1)S(1)}, bf16[4,128,128]{2,1,0:T(8,128)(2,1)S(1)}, u32[]{:S(2)}, u32[]{:S(2)}) collective-permute-start(bf16[4,128,128]{2,1,0:T(8,128)(2,1)S(1)} %get-tuple-element.24.p0), channel_id=1, source_target_pairs={{0,64},{32,96},{64,0},{96,32},{128,192},{160,224},{192,128},{224,1... | collective-permute-start | bytes 393224 | tf_op jit(solution)/shard_map/ppermute | solution.py:326
  164.1 9.2 %collective-permute-start.15 = (bf16[4,128,128]{2,1,0:T(8,128)(2,1)S(1)}, bf16[4,128,128]{2,1,0:T(8,128)(2,1)S(1)}, u32[]{:S(2)}, u32[]{:S(2)}) collective-permute-start(bf16[4,128,128]{2,1,0:T(8,128)(2,1)S(1)} %get-tuple-element.24.p0), channel_id=1, source_target_pairs={{0,32},{32,64},{64,96},{96,0},{128,160},{160,192},{192,224},{224,1... | collective-permute-start | bytes 393224 | tf_op jit(solution)/shard_map/ppermute | solution.py:326
  (9 other events, 87.0 us)

commit v2 on v0

v2 whole, which is shorter than its diff:
```python
import functools

import jax
import jax.numpy as jnp
from jax import lax
from jax.experimental import pallas as pl
from jax.experimental.pallas import tpu as pltpu
from jax.sharding import PartitionSpec as P

F32 = jnp.float32
BF16 = jnp.bfloat16
MIB = 1 << 20
X = 4
CHUNKS = 4
SMEM = pl.BlockSpec(memory_space=pltpu.SMEM)
VMEM = pl.BlockSpec(memory_space=pltpu.VMEM)
ANY = pl.BlockSpec(memory_space=pl.ANY)
Q = 128


def params(mib):
    return pltpu.CompilerParams(vmem_limit_bytes=mib * MIB)


def rows_product(left, right):
    return lax.dot_general(left, right, (((1,), (1,)), ((), ())), preferred_element_type=F32)


def product(left, right):
    return lax.dot_general(left, right, (((1,), (0,)), ((), ())), preferred_element_type=F32)


def owned(info, x):
    return x ^ info[2]


def owned_late(info, x):
    return x ^ info[2] ^ (2 - 2 * info[0])


KEEP = 24


def chunks(aux):
    width = aux // CHUNKS
    return [slice(c * width, (c + 1) * width) for c in range(CHUNKS)]


def fetched(source, target, semaphores):
    return [
        pltpu.make_async_copy(source.at[:, at], target.at[:, at], semaphores.at[c])
        for c, at in enumerate(chunks(source.shape[1]))
    ]


def early_integrals_kernel(
    info, own, other, o0, o1, o2, o3, mine, theirs, total_own, total_inner, sem_mine, sem_theirs
):
    own_copies = fetched(own, mine, sem_mine)
    other_copies = fetched(other, theirs, sem_theirs)
    for copy in own_copies + other_copies:
        copy.start()

    def add(total, value, first):
        if first:
            total[...] = value
        else:
            total[...] += value

    for c, at in enumerate(chunks(own.shape[1])):
        own_copies[c].wait()
        add(total_own, rows_product(mine[:, at], mine[:, at]), c == 0)

    def half(block, at, parity):
        return jnp.concatenate(
            [block[(2 * q + parity) * 64 : (2 * q + parity + 1) * 64, at] for q in range(4)], axis=0
        )

    for c, at in enumerate(chunks(own.shape[1])):
        other_copies[c].wait()

        @pl.when(info[0] == 0)
        def _():
            add(total_inner, rows_product(half(mine, at, 0), theirs[:, at]), c == 0)

        @pl.when(info[0] == 1)
        def _():
            add(total_inner, rows_product(half(theirs, at, 1), mine[:, at]), c == 0)

    for d, out in enumerate((o0, o1, o2, o3)):
        q = owned(info, lax.rem(info[1] + d, X))
        out[0:128, :] = total_own[pl.ds(pl.multiple_of(q * 128, 128), 128), :].astype(BF16)
        out[128:192, :] = total_inner[pl.ds(pl.multiple_of(q * 64, 64), 64), :].astype(BF16)


def early_integrals(info, own, other):
    rows, aux = own.shape
    return pl.pallas_call(
        early_integrals_kernel,
        in_specs=[SMEM, ANY, ANY],
        out_specs=[VMEM] * 4,
        out_shape=[jax.ShapeDtypeStruct((192, rows), BF16)] * 4,
        scratch_shapes=[
            pltpu.VMEM((rows, aux), BF16),
            pltpu.VMEM((rows, aux), BF16),
            pltpu.VMEM((rows, rows), F32),
            pltpu.VMEM((rows // 2, rows), F32),
            pltpu.SemaphoreType.DMA((CHUNKS,)),
            pltpu.SemaphoreType.DMA((CHUNKS,)),
        ],
        compiler_params=params(40),
        cost_estimate=pl.CostEstimate(flops=0, bytes_accessed=0, transcendentals=0),
        name="early_integrals",
    )(info, own, other)


def late_integrals_kernel(
    info, own, following, o0, o1, o2, o3, mine, theirs, total, sem_mine, sem_theirs
):
    @pl.when(info[0] == 1)
    def _():
        own_copies = fetched(own, mine, sem_mine)
        other_copies = fetched(following, theirs, sem_theirs)
        for pair in zip(own_copies, other_copies):
            for copy in pair:
                copy.start()
        for c, at in enumerate(chunks(own.shape[1])):
            own_copies[c].wait()
            other_copies[c].wait()
            value = rows_product(mine[:, at], theirs[:, at])
            if c == 0:
                total[...] = value
            else:
                total[...] += value
        for d, out in enumerate((o0, o1, o2, o3)):
            q = owned(info, lax.rem(info[1] + d, X))
            out[...] = total[pl.ds(pl.multiple_of(q * 128, 128), 128), :].astype(BF16)

    @pl.when(info[0] == 0)
    def _():
        for out in (o0, o1, o2, o3):
            out[...] = jnp.zeros_like(out)


def late_integrals(info, own, following):
    rows, aux = own.shape
    return pl.pallas_call(
        late_integrals_kernel,
        in_specs=[SMEM, ANY, ANY],
        out_specs=[VMEM] * 4,
        out_shape=[jax.ShapeDtypeStruct((Q, rows), BF16)] * 4,
        scratch_shapes=[
            pltpu.VMEM((rows, aux), BF16),
            pltpu.VMEM((rows, aux), BF16),
            pltpu.VMEM((rows, rows), F32),
            pltpu.SemaphoreType.DMA((CHUNKS,)),
            pltpu.SemaphoreType.DMA((CHUNKS,)),
        ],
        compiler_params=params(40),
        cost_estimate=pl.CostEstimate(flops=0, bytes_accessed=0, transcendentals=0),
        name="late_integrals",
    )(info, own, following)


def block_transposed(wide):
    turned = wide.T
    top, bottom = turned[:64], turned[64:]
    low = lax.broadcasted_iota(jnp.int32, (64, 128), 1) < 64
    first = jnp.where(low, top, pltpu.roll(bottom, 64, 1))
    second = jnp.where(low, pltpu.roll(top, 64, 1), bottom)
    return jnp.concatenate([first, second], axis=0), turned


def diagonal_blocks(square):
    return square[:64, :64] + pltpu.roll(square[64:, :], 64, 1)[:, :64]


def tilde_rows(integrals, q, left, right, along, keep, store):
    first = jnp.zeros((128, 128), F32)
    second = jnp.zeros((128, 128), F32)
    upper = lax.broadcasted_iota(jnp.int32, (128, 1), 0) < 64
    lower = lax.broadcasted_iota(jnp.int32, (1, 128), 1) < 64
    down = jnp.broadcast_to(along, (128, 128)).T
    gap_left = jnp.where(upper, left(2 * q), left(2 * q + 1)) - down
    for J in range(4):
        at = slice(J * 128, (J + 1) * 128)
        gap_right = jnp.where(lower, right(2 * J), right(2 * J + 1)) - along
        amp = (keep * integrals(at) / (gap_left + gap_right)).astype(BF16)
        wide = amp.astype(F32)
        swapped, turned = block_transposed(wide)
        tilde_wide = (2.0 * wide - swapped).astype(BF16).astype(F32)
        tilde = tilde_wide.astype(BF16)
        tilde_turned = tilde_wide.T.astype(BF16)
        first += rows_product(tilde, amp)
        second += rows_product(tilde_turned, turned.astype(BF16))
        store(J, tilde, tilde_turned)
    return diagonal_blocks(first), diagonal_blocks(second)


def early_tilde_kernel(info, table, sums, inner_other, along, out, density):
    q = owned(info, info[1])
    left_home = info[0] == 0

    def own(i):
        return table[i]

    def left(i):
        return table[8 * info[0] + i]

    def right(j):
        return table[8 - 8 * info[0] + j]

    def store_own(J, tilde, turned):
        out[J] = tilde

    own_first, _ = tilde_rows(
        lambda at: sums[0:128, at], q, own, own, along[...], 1.0, store_own
    )

    def inner(at):
        mine, theirs = sums[128:192, at], inner_other[:, at]
        return jnp.concatenate(
            [jnp.where(left_home, mine, theirs), jnp.where(left_home, theirs, mine)], axis=0
        )

    def store_inner(J, tilde, turned):
        out[4 + J] = jnp.where(left_home, tilde, turned)

    first, second = tilde_rows(
        inner, q, left, right, along[...], table[KEEP], store_inner
    )
    density[...] = own_first + jnp.where(left_home, first + second, 0.0)


def early_tilde(info, table, *rest):
    return pl.pallas_call(
        early_tilde_kernel,
        in_specs=[SMEM] * 2 + [VMEM] * 3,
        out_specs=[VMEM, VMEM],
        out_shape=[jax.ShapeDtypeStruct((8, 128, 128), BF16), jax.ShapeDtypeStruct((64, 64), F32)],
        compiler_params=pltpu.CompilerParams(vmem_limit_bytes=32 * MIB),
        cost_estimate=pl.CostEstimate(flops=0, bytes_accessed=0, transcendentals=0),
        name="early_tilde",
    )(info, table, *rest)


def folded(square):
    return jnp.concatenate([square[:32], square[32:]], axis=1)


def late_tilde_kernel(info, table, near, far, partner, mine, early, along, out):
    left_home = info[0] == 1

    def left(i):
        return table[16 - 16 * info[0] + i]

    def right(j):
        return table[16 * info[0] + j]

    def outer(at):
        here = mine[:, at].astype(F32) + partner[:, at].astype(F32)
        there = near[:, at].astype(F32) + far[:, at].astype(F32)
        return jnp.where(left_home, here, there)

    def store(J, tilde, turned):
        out[J * 128 : (J + 1) * 128, :] = jnp.where(left_home, tilde, turned)

    first, second = tilde_rows(
        outer, owned_late(info, info[1]), left, right, along[...], table[KEEP + 1], store
    )
    total = early[...] + jnp.where(left_home, 0.0, first + second)
    high = total.astype(BF16)
    out[512:544, :] = folded(high)
    out[544:576, :] = folded((total - high.astype(F32)).astype(BF16))


def late_tilde(info, table, *rest):
    return pl.pallas_call(
        late_tilde_kernel,
        in_specs=[SMEM] * 2 + [VMEM] * 6,
        out_specs=VMEM,
        out_shape=jax.ShapeDtypeStruct((576, 128), BF16),
        compiler_params=pltpu.CompilerParams(vmem_limit_bytes=32 * MIB),
        cost_estimate=pl.CostEstimate(flops=0, bytes_accessed=0, transcendentals=0),
        name="late_tilde",
    )(info, table, *rest)


def gamma_kernel(
    info, e0, e1, e2, e3, p0, p1, p2, p3, own, other, following, preceding, out,
    slab, result, factors, sem_own, sem_other, sem_outer, sem_out,
):
    rows = own.shape[0]
    left_home = info[0] == 1
    own_copies = fetched(own, slab.at[:rows], sem_own)
    other_copies = fetched(other, slab.at[rows : 2 * rows], sem_other)
    left_copies = fetched(following, slab.at[2 * rows :], sem_outer)
    right_copies = fetched(preceding, slab.at[2 * rows :], sem_outer)
    for c in range(CHUNKS):
        own_copies[c].start()
        other_copies[c].start()

        @pl.when(left_home)
        def _():
            left_copies[c].start()

        @pl.when(jnp.logical_not(left_home))
        def _():
            right_copies[c].start()

    for d, (early, late) in enumerate(((e0, p0), (e1, p1), (e2, p2), (e3, p3))):
        q = owned(info, lax.rem(info[1] + X - d, X))
        here = pl.ds(pl.multiple_of(q * 128, 128), 128)
        for J in range(4):
            factors[here, J * 128 : (J + 1) * 128] = early[J]

        q_late = owned_late(info, lax.rem(info[1] + X - d, X))
        here_late = pl.ds(pl.multiple_of(q_late * 128, 128), 128)

        @pl.when(jnp.logical_not(left_home))
        def _():
            column = pl.ds(pl.multiple_of(2 * rows + q_late * 128, 128), 128)
            for J in range(4):
                factors[here, rows + J * 128 : rows + (J + 1) * 128] = early[4 + J]
                factors[J * 128 : (J + 1) * 128, column] = late[J * 128 : (J + 1) * 128]

        @pl.when(left_home)
        def _():
            column = pl.ds(pl.multiple_of(rows + q * 128, 128), 128)
            for J in range(4):
                factors[J * 128 : (J + 1) * 128, column] = early[4 + J]
                factors[here_late, 2 * rows + J * 128 : 2 * rows + (J + 1) * 128] = late[
                    J * 128 : (J + 1) * 128
                ]

    written = fetched(result, out, sem_out)
    for c, at in enumerate(chunks(own.shape[1])):
        own_copies[c].wait()
        other_copies[c].wait()

        @pl.when(left_home)
        def _():
            left_copies[c].wait()

        @pl.when(jnp.logical_not(left_home))
        def _():
            right_copies[c].wait()

        result[:, at] = product(factors[...], slab[:, at]).astype(BF16)
        written[c].start()
    for copy in written:
        copy.wait()


def gamma_block(info, early, late, own, other, following, preceding):
    rows, aux = own.shape
    return pl.pallas_call(
        gamma_kernel,
        in_specs=[SMEM] + [VMEM] * 8 + [ANY] * 4,
        out_specs=ANY,
        out_shape=jax.ShapeDtypeStruct((rows, aux), BF16),
        scratch_shapes=[
            pltpu.VMEM((3 * rows, aux), BF16),
            pltpu.VMEM((rows, aux), BF16),
            pltpu.VMEM((rows, 3 * rows), BF16),
            *[pltpu.SemaphoreType.DMA((CHUNKS,))] * 4,
        ],
        compiler_params=params(56),
        cost_estimate=pl.CostEstimate(flops=0, bytes_accessed=0, transcendentals=0),
        name="gamma_block",
    )(info, *early, *late, own, other, following, preceding)


def density_kernel(p0, p1, p2, p3, out):
    def unfolded(piece):
        wide = piece[512:544].astype(F32) + piece[544:576].astype(F32)
        turned = pltpu.roll(wide, 64, 1)
        return jnp.concatenate([wide[:, :64], turned[:, :64]], axis=0)

    out[...] = (unfolded(p0) + unfolded(p2)) + (unfolded(p1) + unfolded(p3))


def density_over_x(pieces):
    return pl.pallas_call(
        density_kernel,
        in_specs=[VMEM] * 4,
        out_specs=VMEM,
        out_shape=jax.ShapeDtypeStruct((64, 64), F32),
        compiler_params=params(8),
        cost_estimate=pl.CostEstimate(flops=0, bytes_accessed=0, transcendentals=0),
        name="density_over_x",
    )(*pieces)


def along_x(value, by):
    return lax.ppermute(
        value, "aux", [(a, a // X * X + (a + by) % X) for a in range(lax.axis_size("aux"))]
    )


def across_y(value):
    return lax.ppermute(value, "aux", [(a, a ^ X ^ 1) for a in range(lax.axis_size("aux"))])


def from_cores(core, value, occ_to, aux_to=lambda a: a):
    aux, occ = lax.axis_size("aux"), lax.axis_size("occ")
    return lax.ppermute(
        value,
        ("aux", "occ"),
        [
            (a * occ + k, aux_to(a) * occ + occ_to(k) % occ)
            for a in range(aux)
            for k in range(core, occ, 2)
        ],
    )


def swapped(value, axis, other):
    return lax.ppermute(value, axis, [(k, other(k)) for k in range(lax.axis_size(axis))])


def together(values):
    return lax.optimization_barrier(tuple(values))


def after(value, *earlier):
    return lax.optimization_barrier((value, *earlier))[0]


def body(orbital_slabs, occ_energy, virt_energy, pair_kept):
    occ_count, virt_count, aux_count = orbital_slabs.shape
    rows = occ_count * virt_count
    occ = lax.axis_size("occ")
    slabs = orbital_slabs.reshape(rows, aux_count)
    place = lax.axis_index("occ")
    core = lax.rem(place, 2)
    aux_place = lax.axis_index("aux")
    x = lax.rem(aux_place, X)
    info = jnp.stack([core, x, aux_place // X]).astype(jnp.int32)

    following = lax.ppermute(slabs, "occ", [(k, (k - 1) % occ) for k in range(0, occ, 2)])
    other = swapped(slabs, "occ", lambda k: k ^ 1)
    inner_energy = swapped(occ_energy, "occ", lambda k: k ^ 1)
    aux = lax.axis_size("aux")
    outer_energy = lax.ppermute(
        inner_energy,
        ("aux", "occ"),
        [
            (a * occ + k, (a ^ 1) * occ + (k + (2 if k % 2 == 0 else -2)) % occ)
            for a in range(aux)
            for k in range(occ)
        ],
    )
    along = jnp.tile(virt_energy.astype(F32), 2).reshape(1, Q)
    keep_in = pair_kept[place - core].astype(F32)
    keep_out = pair_kept[lax.rem(place - 1 + core + occ, occ)].astype(F32)

    pieces = early_integrals(info, after(slabs, inner_energy, along), other)
    *arrived, outer_energy = together([*(along_x(pieces[d], d) for d in (1, 2, 3)), outer_energy])
    table = jnp.concatenate(
        [occ_energy, inner_energy, outer_energy, jnp.stack([keep_in, keep_out]).astype(BF16)]
    ).astype(F32)
    sums = pieces[0].astype(F32)
    for value in arrived:
        sums = sums + value.astype(F32)
    scattered = sums.astype(BF16)
    sums = scattered.astype(F32) + across_y(scattered).astype(F32)
    inner_other = swapped(sums[Q:], "occ", lambda k: k ^ 1)
    tilde, density = early_tilde(info, table, sums, inner_other, along)
    early = [tilde, *together(along_x(tilde, d) for d in (1, 2, 3))]

    following = after(following, sums)
    preceding = lax.ppermute(
        after(slabs, following), "occ", [(k, (k + 1) % occ) for k in range(1, occ, 2)]
    )
    pieces = late_integrals(info, slabs, following)
    arrived = together(
        from_cores(1, pieces[d], lambda k: k - 1, lambda a, d=d: a // X * X + (a + d) % X)
        for d in range(X)
    )
    sums = arrived[0].astype(F32)
    for value in arrived[1:]:
        sums = sums + value.astype(F32)
    sums = sums.astype(BF16)
    shares = together(
        [
            from_cores(0, sums, lambda k: k + 2, lambda a: a ^ 2),
            from_cores(0, sums, lambda k: k + 2, lambda a: a ^ X ^ 3),
            from_cores(0, sums, lambda k: k + 1, lambda a: a ^ X ^ 1),
            from_cores(0, sums, lambda k: k + 1),
        ]
    )
    tilde = late_tilde(info, table, *shares, density, along)
    late = [tilde, *together(along_x(tilde, d) for d in (1, 2, 3))]

    density = density_over_x(late)
    for bit in (4, 8, 16, 2, 1):
        if bit == 16:
            density = after(density, preceding)
        density = density + swapped(density, "occ", lambda k, bit=bit: k ^ bit)
    virt_density = density / (4.0 * occ_count * occ_count * virt_count)

    gamma = gamma_block(info, early, late, slabs, other, following, preceding)
    return gamma.reshape(occ_count, virt_count, aux_count), virt_density


def solution(mesh):
    return jax.shard_map(
        body,
        mesh=mesh,
        in_specs=(P("occ", None, "aux"), P("occ"), P(), P()),
        out_specs=(P("occ", None, "aux"), P()),
        check_vma=False,
    )
```

time: 334 us -> 144 us (0.43)
  blocking collectives: 143 us -> 0 us
  waiting for transfers between devices: 102 us -> 46.6 us
  starting transfers between devices: 13.5 us -> 68 us
  matrix products: 24.7 us -> 0 us
  Pallas kernels: 0 us -> 20.9 us
  local copies, waits for them, and re-layouts: 20.8 us -> 2.98 us
  other arithmetic: 14.4 us -> 0.94 us
  between operations: 14.8 us -> 2.32 us
    psum x1 -> x0, blocking collectives: 143 us -> none  [body(): total_density = lax.psum(local_density, 'occ')]
    psum x1 -> x0, waiting for transfers between devices: 72.3 us -> none  [pair_terms(): lax.psum(partial_value.astype(jnp.bfloat16), 'aux').astype(jnp.float32)]
    ppermute x3 -> x29, starting transfers between devices: 13.5 us -> 68 us  [the longest x8 18.9 us: swapped(): lax.ppermute(value, axis, [(k, other(k)) for k in range(lax.axis_size(axi...]
    dot_general x8 -> x0, matrix products: 24.7 us -> none  [the longest x2 8.23 us: contract_rows(): lax.dot_general(left, right, (((1,), (1,)), ((), ())), preferred_element_...]
    pallas_call x0 -> x6, Pallas kernels: none -> 20.9 us  [the longest x1 11.1 us: gamma_block(): pl.pallas_call(gamma_kernel, in_specs=[SMEM] + [VMEM] * 8 + [ANY] * 4, ou...]
    ppermute x3 -> x29, waiting for transfers between devices: 29.5 us -> 46.6 us  [the longest x1 10.1 us: across_y(): lax.ppermute(value, 'aux', [(a, a ^ X ^ 1) for a in range(lax.axis_size('...]
    convert_element_type x7 -> x3, other arithmetic: 12.2 us -> 0.18 us  [the longest x1 0.1 us: body(): scattered = sums.astype(BF16)]
    reshape x5 -> x0, local copies, waits for them, and re-layouts: 10.1 us -> none  [the longest x2 5.1 us: pair_terms(): return (amplitude, tilde.reshape(rows, rows))]
  transfers between devices with their start and end apart: 4 -> 29, of which waited for: 2 -> 14; matrix products, arithmetic and copies ran while one was open for 9% -> 1% of each run, Pallas kernels for 0% -> 15%
where the time goes in v2:
time: 144 us; the launch traced here: 142 us
  starting transfers between devices  68 us (47%)
  waiting for transfers between devices  46.6 us (32%)
  Pallas kernels  20.9 us (15%)
  local copies, waits for them, and re-layouts  2.98 us (2%)
  between operations  2.32 us (2%)
    ppermute x8, starting transfers between devices, swapped(): lax.ppermute(value, axis, [(k, other(k)) for k in range(lax.axis_size(axi...  18.9 us
    ppermute x9, starting transfers between devices, along_x(): lax.ppermute(value, 'aux', [(a, a // X * X + (a + by) % X) for a in range...  17.8 us
    ppermute x8, starting transfers between devices, from_cores(): lax.ppermute(value, ('aux', 'occ'), [(a * occ + k, aux_to(a) * occ + occ_...  16.7 us
    ppermute x1, starting transfers between devices, body(): lax.ppermute(slabs, 'occ', [(k, (k - 1) % occ) for k in range(0, occ, 2)])  12.1 us
    pallas_call x1, Pallas kernels, gamma_block(): pl.pallas_call(gamma_kernel, in_specs=[SMEM] + [VMEM] * 8 + [ANY] * 4, ou...  11.1 us
    ppermute x1, waiting for transfers between devices, across_y(): lax.ppermute(value, 'aux', [(a, a ^ X ^ 1) for a in range(lax.axis_size('...  10.1 us
    ppermute x8, waiting for transfers between devices, swapped(): lax.ppermute(value, axis, [(k, other(k)) for k in range(lax.axis_size(axi...  9.48 us
    ppermute x1, waiting for transfers between devices, body(): lax.ppermute(inner_energy, ('aux', 'occ'), [(a * occ + k, (a ^ 1) * occ +...  8.15 us
  transfers between devices with their start and end apart: 29, of which 14 were waited for; matrix products, arithmetic and copies ran while one was open for 1% of the time, Pallas kernels for 15%

profile of v2, /device:TPU:2, one launch (start us, length us, event | category | flops | bytes accessed | tf_op | source)
XLA Modules:
  0.0 141.8 jit_solution(488058331109807171)
XLA Ops:
  0.7 12.1 %collective-permute-start.11 = (bf16[512,3072]{1,0:T(8,128)(2,1)}, bf16[512,3072]{1,0:T(8,128)(2,1)}, u32[]{:S(2)}, u32[]{:S(2)}) collective-permute-start(bf16[512,3072]{1,0:T(8,128)(2,1)} %bitcast.3.own), channel_id=1, source_target_pairs={{0,31},{2,1},{4,3},{6,5},{8,7},{10,9},{12,11},{14,13},{16,15},{18,... | collective-permute-start | bytes 9437192 | tf_op jit(solution)/shard_map/ppermute | solution.py:441
  14.1 6.1 %early_integrals.1 = (bf16[192,512]{1,0:T(8,128)(2,1)S(1)}, bf16[192,512]{1,0:T(8,128)(2,1)S(1)}, bf16[192,512]{1,0:T(8,128)(2,1)S(1)}, bf16[192,512]{1,0:T(8,128)(2,1)S(1)}) custom-call(s32[3]{0:T(128)S(1)} %pad_add_fusion.info, bf16[512,3072]{1,0:T(8,128)(2,1)} %bitcast.3.own, bf16[512,3072]{1,0:T(8,128)(2,1)S(1)} %collective-permute-done.1.other), custom_call_target="tpu_custom_call" | custom-call | tf_op jit(solution)/shard_map/early_integrals/pallas_call | solution.py:98
  22.9 2.2 %collective-permute-start.4 = (bf16[192,512]{1,0:T(8,128)(2,1)S(1)}, bf16[192,512]{1,0:T(8,128)(2,1)S(1)}, u32[]{:S(2)}, u32[]{:S(2)}) collective-permute-start(bf16[192,512]{1,0:T(8,128)(2,1)S(1)} %get-tuple-element.37), channel_id=1, source_target_pairs={{0,96},{32,0},{64,32},{96,64},{128,224},{160,128},{192,160},{224,1... | collective-permute-start | bytes 589832 | tf_op jit(solution)/shard_map/ppermute | solution.py:396
  25.1 8.2 %collective-permute-done.5 = bf16[8]{0:T(256)(128)(2,1)S(1)} collective-permute-done((bf16[8]{0:T(256)(128)(2,1)S(1)}, bf16[8]{0:T(256)(128)(2,1)S(1)}, u32[]{:S(2)}, u32[]{:S(2)}) %collective-permute-start.5) | collective-permute-done | bytes 48 | tf_op jit(solution)/shard_map/ppermute | solution.py:445
  34.9 10.1 %collective-permute-done.6 = bf16[192,512]{1,0:T(8,128)(2,1)S(1)} collective-permute-done((bf16[192,512]{1,0:T(8,128)(2,1)S(1)}, bf16[192,512]{1,0:T(8,128)(2,1)S(1)}, u32[]{:S(2)}, u32[]{:S(2)}) %collective-permute-start.6) | collective-permute-done | bytes 196640 | tf_op jit(solution)/shard_map/ppermute | solution.py:402
  45.1 5.4 %collective-permute-done.11.following = bf16[512,3072]{1,0:T(8,128)(2,1)} collective-permute-done((bf16[512,3072]{1,0:T(8,128)(2,1)}, bf16[512,3072]{1,0:T(8,128)(2,1)}, u32[]{:S(2)}, u32[]{:S(2)}) %collective-permute-start.11) | collective-permute-done | bytes 3145760 | tf_op jit(solution)/shard_map/ppermute | solution.py:441
  57.7 3.0 %collective-permute-start.7 = (f32[64,512]{1,0:T(8,128)S(1)}, f32[64,512]{1,0:T(8,128)S(1)}, u32[]{:S(2)}, u32[]{:S(2)}) collective-permute-start(f32[64,512]{1,0:T(8,128)S(1)} %slice.4), channel_id=1, source_target_pairs={{0,1},{1,0},{2,3},{3,2},{4,5},{5,4},{6,7},{7,6},{8,9},{9,8},{10,11... | collective-permute-start | bytes 393224 | tf_op jit(solution)/shard_map/ppermute | solution.py:419
  60.6 2.3 %collective-permute-done.14 = bf16[128,512]{1,0:T(8,128)(2,1)S(1)} collective-permute-done((bf16[128,512]{1,0:T(8,128)(2,1)S(1)}, bf16[128,512]{1,0:T(8,128)(2,1)S(1)}, u32[]{:S(2)}, u32[]{:S(2)}) %collective-permute-start.14) | collective-permute-done | bytes 131104 | tf_op jit(solution)/shard_map/ppermute | solution.py:407
  64.3 5.7 %collective-permute-start.16 = (bf16[128,512]{1,0:T(8,128)(2,1)S(1)}, bf16[128,512]{1,0:T(8,128)(2,1)S(1)}, u32[]{:S(2)}, u32[]{:S(2)}) collective-permute-start(bf16[128,512]{1,0:T(8,128)(2,1)S(1)} %add_convert_fusion.1), channel_id=1, source_target_pairs={{0,66},{2,68},{4,70},{6,72},{8,74},{10,76},{12,78},{14,80},{16,82}... | collective-permute-start | bytes 393224 | tf_op jit(solution)/shard_map/ppermute | solution.py:407
  70.0 3.1 %collective-permute-start.17 = (bf16[128,512]{1,0:T(8,128)(2,1)S(1)}, bf16[128,512]{1,0:T(8,128)(2,1)S(1)}, u32[]{:S(2)}, u32[]{:S(2)}) collective-permute-start(bf16[128,512]{1,0:T(8,128)(2,1)S(1)} %add_convert_fusion.1), channel_id=1, source_target_pairs={{0,226},{2,228},{4,230},{6,232},{8,234},{10,236},{12,238},{14,240}... | collective-permute-start | bytes 393224 | tf_op jit(solution)/shard_map/ppermute | solution.py:407
  79.6 1.8 %collective-permute-done.16.near = bf16[128,512]{1,0:T(8,128)(2,1)S(1)} collective-permute-done((bf16[128,512]{1,0:T(8,128)(2,1)S(1)}, bf16[128,512]{1,0:T(8,128)(2,1)S(1)}, u32[]{:S(2)}, u32[]{:S(2)}) %collective-permute-start.16) | collective-permute-done | bytes 131104 | tf_op jit(solution)/shard_map/ppermute | solution.py:407
  86.0 3.5 %collective-permute-start.21 = (bf16[576,128]{1,0:T(8,128)(2,1)S(1)}, bf16[576,128]{1,0:T(8,128)(2,1)S(1)}, u32[]{:S(2)}, u32[]{:S(2)}) collective-permute-start(bf16[576,128]{1,0:T(8,128)(2,1)S(1)} %late_tilde.1.p0), channel_id=1, source_target_pairs={{0,64},{32,96},{64,0},{96,32},{128,192},{160,224},{192,128},{224,1... | collective-permute-start | bytes 442376 | tf_op jit(solution)/shard_map/ppermute | solution.py:396
  89.5 3.6 %collective-permute-start.9 = (bf16[8,128,128]{2,1,0:T(8,128)(2,1)S(1)}, bf16[8,128,128]{2,1,0:T(8,128)(2,1)S(1)}, u32[]{:S(2)}, u32[]{:S(2)}) collective-permute-start(bf16[8,128,128]{2,1,0:T(8,128)(2,1)S(1)} %get-tuple-element.43.e0), channel_id=1, source_target_pairs={{0,64},{32,96},{64,0},{96,32},{128,192},{160,224},{192,128},{224,1... | collective-permute-start | bytes 786440 | tf_op jit(solution)/shard_map/ppermute | solution.py:396
  93.1 4.2 %collective-permute-start.10 = (bf16[8,128,128]{2,1,0:T(8,128)(2,1)S(1)}, bf16[8,128,128]{2,1,0:T(8,128)(2,1)S(1)}, u32[]{:S(2)}, u32[]{:S(2)}) collective-permute-start(bf16[8,128,128]{2,1,0:T(8,128)(2,1)S(1)} %get-tuple-element.43.e0), channel_id=1, source_target_pairs={{0,96},{32,0},{64,32},{96,64},{128,224},{160,128},{192,160},{224,1... | collective-permute-start | bytes 786440 | tf_op jit(solution)/shard_map/ppermute | solution.py:396
  97.4 6.1 %collective-permute-done.22.p3 = bf16[576,128]{1,0:T(8,128)(2,1)S(1)} collective-permute-done((bf16[576,128]{1,0:T(8,128)(2,1)S(1)}, bf16[576,128]{1,0:T(8,128)(2,1)S(1)}, u32[]{:S(2)}, u32[]{:S(2)}) %collective-permute-start.22) | collective-permute-done | bytes 147488 | tf_op jit(solution)/shard_map/ppermute | solution.py:396
  103.6 2.0 %collective-permute-start.24 = (f32[64,64]{1,0:T(8,128)S(1)}, f32[64,64]{1,0:T(8,128)S(1)}, u32[]{:S(2)}, u32[]{:S(2)}) collective-permute-start(f32[64,64]{1,0:T(8,128)S(1)} %density_over_x.1), channel_id=1, source_target_pairs={{0,4},{1,5},{2,6},{3,7},{4,0},{5,1},{6,2},{7,3},{8,12},{9,13},{10,... | collective-permute-start | bytes 49160 | tf_op jit(solution)/shard_map/ppermute | solution.py:419
  105.6 2.0 %collective-permute-done.24 = f32[64,64]{1,0:T(8,128)S(1)} collective-permute-done((f32[64,64]{1,0:T(8,128)S(1)}, f32[64,64]{1,0:T(8,128)S(1)}, u32[]{:S(2)}, u32[]{:S(2)}) %collective-permute-start.24) | collective-permute-done | bytes 16416 | tf_op jit(solution)/shard_map/ppermute | solution.py:419
  107.6 4.7 %collective-permute-start.25 = (f32[64,64]{1,0:T(8,128)S(1)}, f32[64,64]{1,0:T(8,128)S(1)}, u32[]{:S(2)}, u32[]{:S(2)}) collective-permute-start(f32[64,64]{1,0:T(8,128)S(1)} %add.61), channel_id=1, source_target_pairs={{0,8},{1,9},{2,10},{3,11},{4,12},{5,13},{6,14},{7,15},{8,0},{9,1},... | collective-permute-start | bytes 49160 | tf_op jit(solution)/shard_map/ppermute | solution.py:419
  112.3 1.9 %collective-permute-done.25 = f32[64,64]{1,0:T(8,128)S(1)} collective-permute-done((f32[64,64]{1,0:T(8,128)S(1)}, f32[64,64]{1,0:T(8,128)S(1)}, u32[]{:S(2)}, u32[]{:S(2)}) %collective-permute-start.25) | collective-permute-done | bytes 16416 | tf_op jit(solution)/shard_map/ppermute | solution.py:419
  114.2 4.6 %collective-permute-start.26 = (f32[64,64]{1,0:T(8,128)S(1)}, f32[64,64]{1,0:T(8,128)S(1)}, u32[]{:S(2)}, u32[]{:S(2)}) collective-permute-start(f32[64,64]{1,0:T(8,128)S(1)} %add.62), channel_id=1, source_target_pairs={{0,16},{1,17},{2,18},{3,19},{4,20},{5,21},{6,22},{7,23},{8,24},{9,... | collective-permute-start | bytes 49160 | tf_op jit(solution)/shard_map/ppermute | solution.py:419
  118.8 3.3 %collective-permute-done.26 = f32[64,64]{1,0:T(8,128)S(1)} collective-permute-done((f32[64,64]{1,0:T(8,128)S(1)}, f32[64,64]{1,0:T(8,128)S(1)}, u32[]{:S(2)}, u32[]{:S(2)}) %collective-permute-start.26) | collective-permute-done | bytes 16416 | tf_op jit(solution)/shard_map/ppermute | solution.py:419
  122.1 4.5 %collective-permute-start.27 = (f32[64,64]{1,0:T(8,128)S(1)}, f32[64,64]{1,0:T(8,128)S(1)}, u32[]{:S(2)}, u32[]{:S(2)}) collective-permute-start(f32[64,64]{1,0:T(8,128)S(1)} %add.63), channel_id=1, source_target_pairs={{0,2},{1,3},{2,0},{3,1},{4,6},{5,7},{6,4},{7,5},{8,10},{9,11},{10,... | collective-permute-start | bytes 49160 | tf_op jit(solution)/shard_map/ppermute | solution.py:419
  126.5 1.9 %collective-permute-done.27 = f32[64,64]{1,0:T(8,128)S(1)} collective-permute-done((f32[64,64]{1,0:T(8,128)S(1)}, f32[64,64]{1,0:T(8,128)S(1)}, u32[]{:S(2)}, u32[]{:S(2)}) %collective-permute-start.27) | collective-permute-done | bytes 16416 | tf_op jit(solution)/shard_map/ppermute | solution.py:419
  130.0 11.1 %gamma_block.1 = bf16[512,3072]{1,0:T(8,128)(2,1)} custom-call(s32[3]{0:T(128)} %copy-done.6, bf16[8,128,128]{2,1,0:T(8,128)(2,1)} %copy-done.5, bf16[8,128,128]{2,1,0:T(8,128)(2,1)} %copy-done.7, bf16[8,128,128]{2,1,0:T(8,128)(2,1)} %copy-done.8, bf16[8,128,128]{2,1,0:T(8,128)(2,1)} %copy-done.9, bf16[576,128]{1,0:T(8,128)(2,1)} %copy-done.1, ...), custom_call_target="tpu_custom_call" | custom-call | tf_op jit(solution)/shard_map/gamma_block/pallas_call | solution.py:357
  (79 shorter events, 26.2 us)
Async XLA Ops:
  0.6 13.5 %collective-permute-start.1 = (bf16[512,3072]{1,0:T(8,128)(2,1)}, bf16[512,3072]{1,0:T(8,128)(2,1)S(1)}, u32[]{:S(2)}, u32[]{:S(2)}) collective-permute-start(bf16[512,3072]{1,0:T(8,128)(2,1)} %bitcast.3.own), channel_id=1, source_target_pairs={{0,1},{1,0},{2,3},{3,2},{4,5},{5,4},{6,7},{7,6},{8,9},{9,8},{10,11... | collective-permute-start | bytes 9437192 | tf_op jit(solution)/shard_map/ppermute | solution.py:419
  0.7 49.7 %collective-permute-start.11 = (bf16[512,3072]{1,0:T(8,128)(2,1)}, bf16[512,3072]{1,0:T(8,128)(2,1)}, u32[]{:S(2)}, u32[]{:S(2)}) collective-permute-start(bf16[512,3072]{1,0:T(8,128)(2,1)} %bitcast.3.own), channel_id=1, source_target_pairs={{0,31},{2,1},{4,3},{6,5},{8,7},{10,9},{12,11},{14,13},{16,15},{18,... | collective-permute-start | bytes 9437192 | tf_op jit(solution)/shard_map/ppermute | solution.py:441
  20.2 13.0 %collective-permute-start.2 = (bf16[192,512]{1,0:T(8,128)(2,1)S(1)}, bf16[192,512]{1,0:T(8,128)(2,1)S(1)}, u32[]{:S(2)}, u32[]{:S(2)}) collective-permute-start(bf16[192,512]{1,0:T(8,128)(2,1)S(1)} %get-tuple-element.35), channel_id=1, source_target_pairs={{0,32},{32,64},{64,96},{96,0},{128,160},{160,192},{192,224},{224,1... | collective-permute-start | bytes 589832 | tf_op jit(solution)/shard_map/ppermute | solution.py:396
  21.8 11.4 %collective-permute-start.3 = (bf16[192,512]{1,0:T(8,128)(2,1)S(1)}, bf16[192,512]{1,0:T(8,128)(2,1)S(1)}, u32[]{:S(2)}, u32[]{:S(2)}) collective-permute-start(bf16[192,512]{1,0:T(8,128)(2,1)S(1)} %get-tuple-element.36), channel_id=1, source_target_pairs={{0,64},{32,96},{64,0},{96,32},{128,192},{160,224},{192,128},{224,1... | collective-permute-start | bytes 589832 | tf_op jit(solution)/shard_map/ppermute | solution.py:396
  22.9 10.7 %collective-permute-start.4 = (bf16[192,512]{1,0:T(8,128)(2,1)S(1)}, bf16[192,512]{1,0:T(8,128)(2,1)S(1)}, u32[]{:S(2)}, u32[]{:S(2)}) collective-permute-start(bf16[192,512]{1,0:T(8,128)(2,1)S(1)} %get-tuple-element.37), channel_id=1, source_target_pairs={{0,96},{32,0},{64,32},{96,64},{128,224},{160,128},{192,160},{224,1... | collective-permute-start | bytes 589832 | tf_op jit(solution)/shard_map/ppermute | solution.py:396
  25.1 8.2 %collective-permute-start.5 = (bf16[8]{0:T(256)(128)(2,1)S(1)}, bf16[8]{0:T(256)(128)(2,1)S(1)}, u32[]{:S(2)}, u32[]{:S(2)}) collective-permute-start(bf16[8]{0:T(256)(128)(2,1)S(1)} %collective-permute-done), channel_id=1, source_target_pairs={{0,34},{1,63},{2,36},{3,33},{4,38},{5,35},{6,40},{7,37},{8,42},{9,... | collective-permute-start | bytes 56 | tf_op jit(solution)/shard_map/ppermute | solution.py:445
  33.7 11.3 %collective-permute-start.6 = (bf16[192,512]{1,0:T(8,128)(2,1)S(1)}, bf16[192,512]{1,0:T(8,128)(2,1)S(1)}, u32[]{:S(2)}, u32[]{:S(2)}) collective-permute-start(bf16[192,512]{1,0:T(8,128)(2,1)S(1)} %add_convert_fusion), channel_id=1, source_target_pairs={{0,160},{32,128},{64,224},{96,192},{128,32},{160,0},{192,96},{224,... | collective-permute-start | bytes 589832 | tf_op jit(solution)/shard_map/ppermute | solution.py:402
  50.5 63.7 %collective-permute-start.23 = (bf16[512,3072]{1,0:T(8,128)(2,1)}, bf16[512,3072]{1,0:T(8,128)(2,1)}, u32[]{:S(2)}, u32[]{:S(2)}) collective-permute-start(bf16[512,3072]{1,0:T(8,128)(2,1)} %bitcast.3.own), channel_id=1, source_target_pairs={{1,2},{3,4},{5,6},{7,8},{9,10},{11,12},{13,14},{15,16},{17,18},{19... | collective-permute-start | bytes 9437192 | tf_op jit(solution)/shard_map/ppermute | solution.py:473
  53.7 6.9 %collective-permute-start.13 = (bf16[128,512]{1,0:T(8,128)(2,1)S(1)}, bf16[128,512]{1,0:T(8,128)(2,1)S(1)}, u32[]{:S(2)}, u32[]{:S(2)}) collective-permute-start(bf16[128,512]{1,0:T(8,128)(2,1)S(1)} %get-tuple-element.49), channel_id=1, source_target_pairs={{1,32},{3,34},{5,36},{7,38},{9,40},{11,42},{13,44},{15,46},{17,48}... | collective-permute-start | bytes 393224 | tf_op jit(solution)/shard_map/ppermute | solution.py:407
  55.0 7.9 %collective-permute-start.14 = (bf16[128,512]{1,0:T(8,128)(2,1)S(1)}, bf16[128,512]{1,0:T(8,128)(2,1)S(1)}, u32[]{:S(2)}, u32[]{:S(2)}) collective-permute-start(bf16[128,512]{1,0:T(8,128)(2,1)S(1)} %get-tuple-element.50), channel_id=1, source_target_pairs={{1,64},{3,66},{5,68},{7,70},{9,72},{11,74},{13,76},{15,78},{17,80}... | collective-permute-start | bytes 393224 | tf_op jit(solution)/shard_map/ppermute | solution.py:407
  56.3 7.9 %collective-permute-start.15 = (bf16[128,512]{1,0:T(8,128)(2,1)S(1)}, bf16[128,512]{1,0:T(8,128)(2,1)S(1)}, u32[]{:S(2)}, u32[]{:S(2)}) collective-permute-start(bf16[128,512]{1,0:T(8,128)(2,1)S(1)} %get-tuple-element.51), channel_id=1, source_target_pairs={{1,96},{3,98},{5,100},{7,102},{9,104},{11,106},{13,108},{15,110},{... | collective-permute-start | bytes 393224 | tf_op jit(solution)/shard_map/ppermute | solution.py:407
  57.7 16.7 %collective-permute-start.7 = (f32[64,512]{1,0:T(8,128)S(1)}, f32[64,512]{1,0:T(8,128)S(1)}, u32[]{:S(2)}, u32[]{:S(2)}) collective-permute-start(f32[64,512]{1,0:T(8,128)S(1)} %slice.4), channel_id=1, source_target_pairs={{0,1},{1,0},{2,3},{3,2},{4,5},{5,4},{6,7},{7,6},{8,9},{9,8},{10,11... | collective-permute-start | bytes 393224 | tf_op jit(solution)/shard_map/ppermute | solution.py:419
  64.3 17.1 %collective-permute-start.16 = (bf16[128,512]{1,0:T(8,128)(2,1)S(1)}, bf16[128,512]{1,0:T(8,128)(2,1)S(1)}, u32[]{:S(2)}, u32[]{:S(2)}) collective-permute-start(bf16[128,512]{1,0:T(8,128)(2,1)S(1)} %add_convert_fusion.1), channel_id=1, source_target_pairs={{0,66},{2,68},{4,70},{6,72},{8,74},{10,76},{12,78},{14,80},{16,82}... | collective-permute-start | bytes 393224 | tf_op jit(solution)/shard_map/ppermute | solution.py:407
  70.0 13.1 %collective-permute-start.17 = (bf16[128,512]{1,0:T(8,128)(2,1)S(1)}, bf16[128,512]{1,0:T(8,128)(2,1)S(1)}, u32[]{:S(2)}, u32[]{:S(2)}) collective-permute-start(bf16[128,512]{1,0:T(8,128)(2,1)S(1)} %add_convert_fusion.1), channel_id=1, source_target_pairs={{0,226},{2,228},{4,230},{6,232},{8,234},{10,236},{12,238},{14,240}... | collective-permute-start | bytes 393224 | tf_op jit(solution)/shard_map/ppermute | solution.py:407
  73.1 10.0 %collective-permute-start.18 = (bf16[128,512]{1,0:T(8,128)(2,1)S(1)}, bf16[128,512]{1,0:T(8,128)(2,1)S(1)}, u32[]{:S(2)}, u32[]{:S(2)}) collective-permute-start(bf16[128,512]{1,0:T(8,128)(2,1)S(1)} %add_convert_fusion.1), channel_id=1, source_target_pairs={{0,161},{2,163},{4,165},{6,167},{8,169},{10,171},{12,173},{14,175}... | collective-permute-start | bytes 393224 | tf_op jit(solution)/shard_map/ppermute | solution.py:407
  74.4 8.6 %collective-permute-start.19 = (bf16[128,512]{1,0:T(8,128)(2,1)S(1)}, bf16[128,512]{1,0:T(8,128)(2,1)S(1)}, u32[]{:S(2)}, u32[]{:S(2)}) collective-permute-start(bf16[128,512]{1,0:T(8,128)(2,1)S(1)} %add_convert_fusion.1), channel_id=1, source_target_pairs={{0,1},{2,3},{4,5},{6,7},{8,9},{10,11},{12,13},{14,15},{16,17},{18,... | collective-permute-start | bytes 393224 | tf_op jit(solution)/shard_map/ppermute | solution.py:407
  84.4 8.7 %collective-permute-start.20 = (bf16[576,128]{1,0:T(8,128)(2,1)S(1)}, bf16[576,128]{1,0:T(8,128)(2,1)S(1)}, u32[]{:S(2)}, u32[]{:S(2)}) collective-permute-start(bf16[576,128]{1,0:T(8,128)(2,1)S(1)} %late_tilde.1.p0), channel_id=1, source_target_pairs={{0,32},{32,64},{64,96},{96,0},{128,160},{160,192},{192,224},{224,1... | collective-permute-start | bytes 442376 | tf_op jit(solution)/shard_map/ppermute | solution.py:396
  86.0 11.3 %collective-permute-start.21 = (bf16[576,128]{1,0:T(8,128)(2,1)S(1)}, bf16[576,128]{1,0:T(8,128)(2,1)S(1)}, u32[]{:S(2)}, u32[]{:S(2)}) collective-permute-start(bf16[576,128]{1,0:T(8,128)(2,1)S(1)} %late_tilde.1.p0), channel_id=1, source_target_pairs={{0,64},{32,96},{64,0},{96,32},{128,192},{160,224},{192,128},{224,1... | collective-permute-start | bytes 442376 | tf_op jit(solution)/shard_map/ppermute | solution.py:396
  89.5 38.9 %collective-permute-start.8 = (bf16[8,128,128]{2,1,0:T(8,128)(2,1)S(1)}, bf16[8,128,128]{2,1,0:T(8,128)(2,1)S(1)}, u32[]{:S(2)}, u32[]{:S(2)}) collective-permute-start(bf16[8,128,128]{2,1,0:T(8,128)(2,1)S(1)} %get-tuple-element.43.e0), channel_id=1, source_target_pairs={{0,32},{32,64},{64,96},{96,0},{128,160},{160,192},{192,224},{224,1... | collective-permute-start | bytes 786440 | tf_op jit(solution)/shard_map/ppermute | solution.py:396
  89.5 39.0 %collective-permute-start.9 = (bf16[8,128,128]{2,1,0:T(8,128)(2,1)S(1)}, bf16[8,128,128]{2,1,0:T(8,128)(2,1)S(1)}, u32[]{:S(2)}, u32[]{:S(2)}) collective-permute-start(bf16[8,128,128]{2,1,0:T(8,128)(2,1)S(1)} %get-tuple-element.43.e0), channel_id=1, source_target_pairs={{0,64},{32,96},{64,0},{96,32},{128,192},{160,224},{192,128},{224,1... | collective-permute-start | bytes 786440 | tf_op jit(solution)/shard_map/ppermute | solution.py:396
  93.1 35.4 %collective-permute-start.10 = (bf16[8,128,128]{2,1,0:T(8,128)(2,1)S(1)}, bf16[8,128,128]{2,1,0:T(8,128)(2,1)S(1)}, u32[]{:S(2)}, u32[]{:S(2)}) collective-permute-start(bf16[8,128,128]{2,1,0:T(8,128)(2,1)S(1)} %get-tuple-element.43.e0), channel_id=1, source_target_pairs={{0,96},{32,0},{64,32},{96,64},{128,224},{160,128},{192,160},{224,1... | collective-permute-start | bytes 786440 | tf_op jit(solution)/shard_map/ppermute | solution.py:396
  107.6 6.6 %collective-permute-start.25 = (f32[64,64]{1,0:T(8,128)S(1)}, f32[64,64]{1,0:T(8,128)S(1)}, u32[]{:S(2)}, u32[]{:S(2)}) collective-permute-start(f32[64,64]{1,0:T(8,128)S(1)} %add.61), channel_id=1, source_target_pairs={{0,8},{1,9},{2,10},{3,11},{4,12},{5,13},{6,14},{7,15},{8,0},{9,1},... | collective-permute-start | bytes 49160 | tf_op jit(solution)/shard_map/ppermute | solution.py:419
  114.2 7.9 %collective-permute-start.26 = (f32[64,64]{1,0:T(8,128)S(1)}, f32[64,64]{1,0:T(8,128)S(1)}, u32[]{:S(2)}, u32[]{:S(2)}) collective-permute-start(f32[64,64]{1,0:T(8,128)S(1)} %add.62), channel_id=1, source_target_pairs={{0,16},{1,17},{2,18},{3,19},{4,20},{5,21},{6,22},{7,23},{8,24},{9,... | collective-permute-start | bytes 49160 | tf_op jit(solution)/shard_map/ppermute | solution.py:419
  128.4 12.7 %collective-permute-start.28 = (f32[64,64]{1,0:T(8,128)S(1)}, f32[64,64]{1,0:T(8,128)S(1)}, u32[]{:S(2)}, u32[]{:S(2)}) collective-permute-start(f32[64,64]{1,0:T(8,128)S(1)} %add.64), channel_id=1, source_target_pairs={{0,1},{1,0},{2,3},{3,2},{4,5},{5,4},{6,7},{7,6},{8,9},{9,8},{10,11... | collective-permute-start | bytes 49160 | tf_op jit(solution)/shard_map/ppermute | solution.py:419
  (17 other events, 349.2 us)

commit v3 on v2

--- a/solution.py
+++ b/solution.py
@@ -35,10 +35,7 @@
 
 
 def owned_late(info, x):
-    return x ^ info[2] ^ (2 - 2 * info[0])
-
-
-KEEP = 24
+    return x ^ info[2] ^ (1 - info[0])
 
 
 def chunks(aux):
@@ -108,7 +105,7 @@
             pltpu.SemaphoreType.DMA((CHUNKS,)),
             pltpu.SemaphoreType.DMA((CHUNKS,)),
         ],
-        compiler_params=params(40),
+        compiler_params=params(60),
         cost_estimate=pl.CostEstimate(flops=0, bytes_accessed=0, transcendentals=0),
         name="early_integrals",
     )(info, own, other)
@@ -156,7 +153,7 @@
             pltpu.SemaphoreType.DMA((CHUNKS,)),
             pltpu.SemaphoreType.DMA((CHUNKS,)),
         ],
-        compiler_params=params(40),
+        compiler_params=params(56),
         cost_estimate=pl.CostEstimate(flops=0, bytes_accessed=0, transcendentals=0),
         name="late_integrals",
     )(info, own, following)
@@ -175,11 +172,12 @@
     return square[:64, :64] + pltpu.roll(square[64:, :], 64, 1)[:, :64]
 
 
-def tilde_rows(integrals, q, left, right, along, keep, store):
+def tilde_rows(integrals, q, left, right, virt, keep, store):
     first = jnp.zeros((128, 128), F32)
     second = jnp.zeros((128, 128), F32)
     upper = lax.broadcasted_iota(jnp.int32, (128, 1), 0) < 64
     lower = lax.broadcasted_iota(jnp.int32, (1, 128), 1) < 64
+    along = jnp.concatenate([virt, virt], axis=1).astype(F32)
     down = jnp.broadcast_to(along, (128, 128)).T
     gap_left = jnp.where(upper, left(2 * q), left(2 * q + 1)) - down
     for J in range(4):
@@ -197,28 +195,30 @@
     return diagonal_blocks(first), diagonal_blocks(second)
 
 
-def early_tilde_kernel(info, table, sums, inner_other, along, out, density):
+def early_tilde_kernel(
+    info, kept, own_energy, inner_energy, here, there, inner_mine, inner_other, virt, out, density
+):
     q = owned(info, info[1])
     left_home = info[0] == 0
 
     def own(i):
-        return table[i]
+        return own_energy[i]
 
     def left(i):
-        return table[8 * info[0] + i]
+        return jnp.where(left_home, own_energy[i], inner_energy[i])
 
     def right(j):
-        return table[8 - 8 * info[0] + j]
+        return jnp.where(left_home, inner_energy[j], own_energy[j])
 
     def store_own(J, tilde, turned):
         out[J] = tilde
 
     own_first, _ = tilde_rows(
-        lambda at: sums[0:128, at], q, own, own, along[...], 1.0, store_own
+        lambda at: here[0:128, at].astype(F32) + there[0:128, at].astype(F32), q, own, own, virt[...], 1.0, store_own
     )
 
     def inner(at):
-        mine, theirs = sums[128:192, at], inner_other[:, at]
+        mine, theirs = inner_mine[:, at], inner_other[:, at]
         return jnp.concatenate(
             [jnp.where(left_home, mine, theirs), jnp.where(left_home, theirs, mine)], axis=0
         )
@@ -227,63 +227,59 @@
         out[4 + J] = jnp.where(left_home, tilde, turned)
 
     first, second = tilde_rows(
-        inner, q, left, right, along[...], table[KEEP], store_inner
+        inner, q, left, right, virt[...], kept[info[3] - info[0]].astype(F32), store_inner
     )
     density[...] = own_first + jnp.where(left_home, first + second, 0.0)
 
 
-def early_tilde(info, table, *rest):
+def early_tilde(*operands):
     return pl.pallas_call(
         early_tilde_kernel,
-        in_specs=[SMEM] * 2 + [VMEM] * 3,
+        in_specs=[SMEM] * 4 + [VMEM] * 5,
         out_specs=[VMEM, VMEM],
         out_shape=[jax.ShapeDtypeStruct((8, 128, 128), BF16), jax.ShapeDtypeStruct((64, 64), F32)],
         compiler_params=pltpu.CompilerParams(vmem_limit_bytes=32 * MIB),
         cost_estimate=pl.CostEstimate(flops=0, bytes_accessed=0, transcendentals=0),
         name="early_tilde",
-    )(info, table, *rest)
-
-
-def folded(square):
-    return jnp.concatenate([square[:32], square[32:]], axis=1)
-
-
-def late_tilde_kernel(info, table, near, far, partner, mine, early, along, out):
-    left_home = info[0] == 1
+    )(*operands)
+
+
+def late_tilde_kernel(
+    info, kept, left_energy, right_energy, mine, partner, early, virt, straight, turned, density
+):
+    def outer(at):
+        return mine[:, at].astype(F32) + partner[:, at].astype(F32)
 
     def left(i):
-        return table[16 - 16 * info[0] + i]
+        return left_energy[i]
 
     def right(j):
-        return table[16 * info[0] + j]
-
-    def outer(at):
-        here = mine[:, at].astype(F32) + partner[:, at].astype(F32)
-        there = near[:, at].astype(F32) + far[:, at].astype(F32)
-        return jnp.where(left_home, here, there)
-
-    def store(J, tilde, turned):
-        out[J * 128 : (J + 1) * 128, :] = jnp.where(left_home, tilde, turned)
+        return right_energy[j]
+
+    def store(J, tilde, tilde_turned):
+        straight[J * 128 : (J + 1) * 128, :] = tilde
+        turned[J * 128 : (J + 1) * 128, :] = tilde_turned
 
     first, second = tilde_rows(
-        outer, owned_late(info, info[1]), left, right, along[...], table[KEEP + 1], store
-    )
-    total = early[...] + jnp.where(left_home, 0.0, first + second)
-    high = total.astype(BF16)
-    out[512:544, :] = folded(high)
-    out[544:576, :] = folded((total - high.astype(F32)).astype(BF16))
-
-
-def late_tilde(info, table, *rest):
+        outer, owned(info, info[1]), left, right, virt[...], kept[info[3] - info[0] + 1].astype(F32), store
+    )
+    density[...] = early[...] + jnp.where(info[0] == 0, first + second, 0.0)
+
+
+def late_tilde(*operands):
     return pl.pallas_call(
         late_tilde_kernel,
-        in_specs=[SMEM] * 2 + [VMEM] * 6,
-        out_specs=VMEM,
-        out_shape=jax.ShapeDtypeStruct((576, 128), BF16),
-        compiler_params=pltpu.CompilerParams(vmem_limit_bytes=32 * MIB),
+        in_specs=[SMEM] * 4 + [VMEM] * 4,
+        out_specs=[VMEM] * 3,
+        out_shape=[
+            jax.ShapeDtypeStruct((512, 128), BF16),
+            jax.ShapeDtypeStruct((512, 128), BF16),
+            jax.ShapeDtypeStruct((64, 64), F32),
+        ],
+        compiler_params=params(32),
         cost_estimate=pl.CostEstimate(flops=0, bytes_accessed=0, transcendentals=0),
         name="late_tilde",
-    )(info, table, *rest)
+    )(*operands)
 
 
 def gamma_kernel(
@@ -371,27 +367,6 @@
     )(info, *early, *late, own, other, following, preceding)
 
 
-def density_kernel(p0, p1, p2, p3, out):
-    def unfolded(piece):
-        wide = piece[512:544].astype(F32) + piece[544:576].astype(F32)
-        turned = pltpu.roll(wide, 64, 1)
-        return jnp.concatenate([wide[:, :64], turned[:, :64]], axis=0)
-
-    out[...] = (unfolded(p0) + unfolded(p2)) + (unfolded(p1) + unfolded(p3))
-
-
-def density_over_x(pieces):
-    return pl.pallas_call(
-        density_kernel,
-        in_specs=[VMEM] * 4,
-        out_specs=VMEM,
-        out_shape=jax.ShapeDtypeStruct((64, 64), F32),
-        compiler_params=params(8),
-        cost_estimate=pl.CostEstimate(flops=0, bytes_accessed=0, transcendentals=0),
-        name="density_over_x",
-    )(*pieces)
-
-
 def along_x(value, by):
     return lax.ppermute(
         value, "aux", [(a, a // X * X + (a + by) % X) for a in range(lax.axis_size("aux"))]
@@ -436,44 +411,34 @@
     core = lax.rem(place, 2)
     aux_place = lax.axis_index("aux")
     x = lax.rem(aux_place, X)
-    info = jnp.stack([core, x, aux_place // X]).astype(jnp.int32)
+    info = jnp.stack([core, x, aux_place // X, place]).astype(jnp.int32)
+    energy = occ_energy.astype(F32)
 
     following = lax.ppermute(slabs, "occ", [(k, (k - 1) % occ) for k in range(0, occ, 2)])
     other = swapped(slabs, "occ", lambda k: k ^ 1)
-    inner_energy = swapped(occ_energy, "occ", lambda k: k ^ 1)
-    aux = lax.axis_size("aux")
-    outer_energy = lax.ppermute(
-        inner_energy,
-        ("aux", "occ"),
-        [
-            (a * occ + k, (a ^ 1) * occ + (k + (2 if k % 2 == 0 else -2)) % occ)
-            for a in range(aux)
-            for k in range(occ)
-        ],
-    )
-    along = jnp.tile(virt_energy.astype(F32), 2).reshape(1, Q)
-    keep_in = pair_kept[place - core].astype(F32)
-    keep_out = pair_kept[lax.rem(place - 1 + core + occ, occ)].astype(F32)
-
-    pieces = early_integrals(info, after(slabs, inner_energy, along), other)
-    *arrived, outer_energy = together([*(along_x(pieces[d], d) for d in (1, 2, 3)), outer_energy])
-    table = jnp.concatenate(
-        [occ_energy, inner_energy, outer_energy, jnp.stack([keep_in, keep_out]).astype(BF16)]
-    ).astype(F32)
+    inner_energy = swapped(energy, "occ", lambda k: k ^ 1)
+    outer_energy = from_cores(1, inner_energy, lambda k: k - 3, lambda a: a ^ 1)
+    virt = virt_energy.reshape(1, virt_count)
+
+    pieces = early_integrals(info, slabs, other)
+    arrived = together(along_x(pieces[d], d) for d in (1, 2, 3))
     sums = pieces[0].astype(F32)
     for value in arrived:
         sums = sums + value.astype(F32)
     scattered = sums.astype(BF16)
-    sums = scattered.astype(F32) + across_y(scattered).astype(F32)
-    inner_other = swapped(sums[Q:], "occ", lambda k: k ^ 1)
-    tilde, density = early_tilde(info, table, sums, inner_other, along)
-    early = [tilde, *together(along_x(tilde, d) for d in (1, 2, 3))]
-
-    following = after(following, sums)
+    there, outer_energy = together([across_y(scattered), outer_energy])
+    inner = scattered[Q:].astype(F32) + there[Q:].astype(F32)
+    inner_other = swapped(inner, "occ", lambda k: k ^ 1)
+    tilde, density = early_tilde(
+        info, pair_kept, energy, inner_energy, scattered, there, inner, inner_other, virt
+    )
+    own_tilde = tilde
+
+    following = after(following, tilde)
+    pieces = late_integrals(info, slabs, following)
     preceding = lax.ppermute(
-        after(slabs, following), "occ", [(k, (k + 1) % occ) for k in range(1, occ, 2)]
-    )
-    pieces = late_integrals(info, slabs, following)
+        after(slabs, pieces[0]), "occ", [(k, (k + 1) % occ) for k in range(1, occ, 2)]
+    )
     arrived = together(
         from_cores(1, pieces[d], lambda k: k - 1, lambda a, d=d: a // X * X + (a + d) % X)
         for d in range(X)
@@ -482,25 +447,27 @@
     for value in arrived[1:]:
         sums = sums + value.astype(F32)
     sums = sums.astype(BF16)
-    shares = together(
-        [
-            from_cores(0, sums, lambda k: k + 2, lambda a: a ^ 2),
-            from_cores(0, sums, lambda k: k + 2, lambda a: a ^ X ^ 3),
-            from_cores(0, sums, lambda k: k + 1, lambda a: a ^ X ^ 1),
-            from_cores(0, sums, lambda k: k + 1),
-        ]
-    )
-    tilde = late_tilde(info, table, *shares, density, along)
+    partner = from_cores(0, sums, lambda k: k, lambda a: a ^ X ^ 1)
+    straight, turned, density = late_tilde(
+        info, pair_kept, inner_energy, outer_energy, sums, partner, density, virt
+    )
+    left = from_cores(0, straight, lambda k: k + 1)
+    right = from_cores(0, turned, lambda k: k + 2, lambda a: a ^ 1)
+
+    tilde = jnp.where(core == 1, left, right)
+    own_tilde = after(own_tilde, left)
+    early = [own_tilde, *together(along_x(own_tilde, d) for d in (1, 2, 3))]
     late = [tilde, *together(along_x(tilde, d) for d in (1, 2, 3))]
-
-    density = density_over_x(late)
-    for bit in (4, 8, 16, 2, 1):
-        if bit == 16:
-            density = after(density, preceding)
-        density = density + swapped(density, "occ", lambda k, bit=bit: k ^ bit)
+    gamma = gamma_block(info, early, late, slabs, other, following, preceding)
+
+    for flip, earlier in ((4, ()), (8, (left,)), (16, (early[1],)), (2, (preceding, tilde))):
+        density = after(density, *earlier)
+        density = density + swapped(density, "occ", lambda k, flip=flip: k ^ flip)
+    parts = [along_x(density, d) for d in range(1, X)]
+    gamma, density, *parts = together([gamma, density, *parts])
+    density = (density + parts[1]) + (parts[0] + parts[2])
+    density = density + swapped(density, "occ", lambda k: k ^ 1)
     virt_density = density / (4.0 * occ_count * occ_count * virt_count)
-
-    gamma = gamma_block(info, early, late, slabs, other, following, preceding)
     return gamma.reshape(occ_count, virt_count, aux_count), virt_density
 
 

time: 144 us -> 135 us (0.938)
  starting transfers between devices: 68 us -> 55.1 us
  waiting for transfers between devices: 46.6 us -> 49.2 us
  other arithmetic: 0.94 us -> 2.39 us
    ppermute x8, waiting for transfers between devices: 7.01 us -> 21.6 us  [from_cores(): lax.ppermute(value, ('aux', 'occ'), [(a * occ + k, aux_to(a) * occ + occ_...]
    ppermute x8, starting transfers between devices: 18.9 us -> 5.7 us  [swapped(): lax.ppermute(value, axis, [(k, other(k)) for k in range(lax.axis_size(axi...]
    ppermute x1, waiting for transfers between devices: 10.1 us -> 0.01 us  [across_y(): lax.ppermute(value, 'aux', [(a, a ^ X ^ 1) for a in range(lax.axis_size('...]
    ppermute x8, waiting for transfers between devices: 9.48 us -> 18.6 us  [swapped(): lax.ppermute(value, axis, [(k, other(k)) for k in range(lax.axis_size(axi...]
    ppermute x2 -> x1, waiting for transfers between devices: 8.16 us -> 0.01 us  [body(): lax.ppermute(after(slabs, pieces[0]), 'occ', [(k, (k + 1) % occ) for k in...]
    ppermute x1, waiting for transfers between devices: 5.36 us -> 3.26 us  [body(): lax.ppermute(slabs, 'occ', [(k, (k - 1) % occ) for k in range(0, occ, 2)])]
    unnamed x24 -> x28, local copies, waits for them, and re-layouts: 1.48 us -> 2.94 us
    ppermute x9 -> x12, waiting for transfers between devices: 6.48 us -> 5.86 us  [along_x(): lax.ppermute(value, 'aux', [(a, a // X * X + (a + by) % X) for a in range...]
  transfers between devices with their start and end apart: 29 -> 31, of which waited for: 14 -> 16; matrix products, arithmetic and copies ran while one was open for 1% -> 1% of each run, Pallas kernels for 15% -> 16%
where the time goes in v3:
time: 135 us; the launch traced here: 133 us
  starting transfers between devices  55.1 us (41%)
  waiting for transfers between devices  49.2 us (36%)
  Pallas kernels  22.3 us (17%)
  local copies, waits for them, and re-layouts  2.94 us (2%)
  other arithmetic  2.39 us (2%)
    ppermute x8, waiting for transfers between devices, from_cores(): lax.ppermute(value, ('aux', 'occ'), [(a * occ + k, aux_to(a) * occ + occ_...  21.6 us
    ppermute x8, waiting for transfers between devices, swapped(): lax.ppermute(value, axis, [(k, other(k)) for k in range(lax.axis_size(axi...  18.6 us
    ppermute x12, starting transfers between devices, along_x(): lax.ppermute(value, 'aux', [(a, a // X * X + (a + by) % X) for a in range...  18.2 us
    ppermute x8, starting transfers between devices, from_cores(): lax.ppermute(value, ('aux', 'occ'), [(a * occ + k, aux_to(a) * occ + occ_...  15.6 us
    ppermute x1, starting transfers between devices, body(): lax.ppermute(slabs, 'occ', [(k, (k - 1) % occ) for k in range(0, occ, 2)])  12.1 us
    pallas_call x1, Pallas kernels, gamma_block(): pl.pallas_call(gamma_kernel, in_specs=[SMEM] + [VMEM] * 8 + [ANY] * 4, ou...  11.1 us
    pallas_call x1, Pallas kernels, early_integrals(): pl.pallas_call(early_integrals_kernel, in_specs=[SMEM, ANY, ANY], out_spe...  6.55 us
    ppermute x12, waiting for transfers between devices, along_x(): lax.ppermute(value, 'aux', [(a, a // X * X + (a + by) % X) for a in range...  5.86 us
  transfers between devices with their start and end apart: 31, of which 16 were waited for; matrix products, arithmetic and copies ran while one was open for 1% of the time, Pallas kernels for 16%

profile of v3, /device:TPU:2, one launch (start us, length us, event | category | flops | bytes accessed | tf_op | source)
XLA Modules:
  0.0 132.9 jit_solution(9684060131259048125)
XLA Ops:
  0.7 12.1 %collective-permute-start.8 = (bf16[512,3072]{1,0:T(8,128)(2,1)}, bf16[512,3072]{1,0:T(8,128)(2,1)}, u32[]{:S(2)}, u32[]{:S(2)}) collective-permute-start(bf16[512,3072]{1,0:T(8,128)(2,1)} %bitcast.4.own), channel_id=1, source_target_pairs={{0,31},{2,1},{4,3},{6,5},{8,7},{10,9},{12,11},{14,13},{16,15},{18,... | collective-permute-start | bytes 9437192 | tf_op jit(solution)/shard_map/ppermute | solution.py:417
  13.5 1.7 %copy-done.5 = bf16[512,3072]{1,0:T(8,128)(2,1)} copy-done((bf16[512,3072]{1,0:T(8,128)(2,1)}, bf16[512,3072]{1,0:T(8,128)(2,1)S(1)}, u32[]{:S(2)}) %copy-start.5) | copy-done | bytes 3145752
  15.2 6.5 %early_integrals.1 = (bf16[192,512]{1,0:T(8,128)(2,1)}, bf16[192,512]{1,0:T(8,128)(2,1)}, bf16[192,512]{1,0:T(8,128)(2,1)}, bf16[192,512]{1,0:T(8,128)(2,1)}) custom-call(s32[4]{0:T(128)} %pad_add_fusion.info, bf16[512,3072]{1,0:T(8,128)(2,1)} %bitcast.4.own, bf16[512,3072]{1,0:T(8,128)(2,1)} %copy-done.5), custom_call_target="tpu_custom_call" | custom-call | tf_op jit(solution)/shard_map/early_integrals/pallas_call | solution.py:95
  24.4 2.1 %collective-permute-start.4 = (bf16[192,512]{1,0:T(8,128)(2,1)}, bf16[192,512]{1,0:T(8,128)(2,1)S(1)}, u32[]{:S(2)}, u32[]{:S(2)}) collective-permute-start(bf16[192,512]{1,0:T(8,128)(2,1)} %get-tuple-element.44), channel_id=1, source_target_pairs={{0,96},{32,0},{64,32},{96,64},{128,224},{160,128},{192,160},{224,1... | collective-permute-start | bytes 589832 | tf_op jit(solution)/shard_map/ppermute | solution.py:371
  27.7 4.3 %collective-permute-done.3 = bf16[192,512]{1,0:T(8,128)(2,1)S(1)} collective-permute-done((bf16[192,512]{1,0:T(8,128)(2,1)}, bf16[192,512]{1,0:T(8,128)(2,1)S(1)}, u32[]{:S(2)}, u32[]{:S(2)}) %collective-permute-start.3) | collective-permute-done | bytes 196640 | tf_op jit(solution)/shard_map/ppermute | solution.py:371
  33.4 2.2 %collective-permute-start.5 = (bf16[192,512]{1,0:T(8,128)(2,1)S(1)}, bf16[192,512]{1,0:T(8,128)(2,1)S(1)}, u32[]{:S(2)}, u32[]{:S(2)}) collective-permute-start(bf16[192,512]{1,0:T(8,128)(2,1)S(1)} %add_convert_fusion.here), channel_id=1, source_target_pairs={{0,160},{32,128},{64,224},{96,192},{128,32},{160,0},{192,96},{224,... | collective-permute-start | bytes 589832 | tf_op jit(solution)/shard_map/ppermute | solution.py:377
  38.0 6.0 %collective-permute-done.6.right_energy = f32[8]{0:T(128)S(1)} collective-permute-done((f32[8]{0:T(128)S(1)}, f32[8]{0:T(128)S(1)}, u32[]{:S(2)}, u32[]{:S(2)}) %collective-permute-start.6) | collective-permute-done | bytes 64 | tf_op jit(solution)/shard_map/ppermute | solution.py:382
  45.5 1.7 %early_tilde.1 = (bf16[8,128,128]{2,1,0:T(8,128)(2,1)S(1)}, f32[64,64]{1,0:T(8,128)S(1)}) custom-call(s32[4]{0:T(128)S(1)} %copy-done.1, s32[32]{0:T(128)S(1)} %copy-done.3, f32[8]{0:T(128)S(1)} %convert_element_type.39.own_energy, f32[8]{0:T(128)S(1)} %collective-permute-done.inner_energy.left_energy, bf16[192,512]{1,0:T(8,128)(2,1)S(1)} %add_convert_fusion.here, ...), custom_call_target="tpu_custom_call" | custom-call | tf_op jit(solution)/shard_map/early_tilde/pallas_call | solution.py:236
  47.2 3.3 %collective-permute-done.8.following = bf16[512,3072]{1,0:T(8,128)(2,1)} collective-permute-done((bf16[512,3072]{1,0:T(8,128)(2,1)}, bf16[512,3072]{1,0:T(8,128)(2,1)}, u32[]{:S(2)}, u32[]{:S(2)}) %collective-permute-start.8) | collective-permute-done | bytes 3145760 | tf_op jit(solution)/shard_map/ppermute | solution.py:417
  50.5 1.6 %late_integrals.1 = (bf16[128,512]{1,0:T(8,128)(2,1)}, bf16[128,512]{1,0:T(8,128)(2,1)}, bf16[128,512]{1,0:T(8,128)(2,1)}, bf16[128,512]{1,0:T(8,128)(2,1)}) custom-call(s32[4]{0:T(128)} %pad_add_fusion.info, bf16[512,3072]{1,0:T(8,128)(2,1)} %bitcast.4.own, bf16[512,3072]{1,0:T(8,128)(2,1)} %collective-permute-done.8.following), custom_call_target="tpu_custom_call" | custom-call | tf_op jit(solution)/shard_map/late_integrals/pallas_call | solution.py:144
  60.0 3.3 %collective-permute-done.11 = bf16[128,512]{1,0:T(8,128)(2,1)S(1)} collective-permute-done((bf16[128,512]{1,0:T(8,128)(2,1)}, bf16[128,512]{1,0:T(8,128)(2,1)S(1)}, u32[]{:S(2)}, u32[]{:S(2)}) %collective-permute-start.11) | collective-permute-done | bytes 131104 | tf_op jit(solution)/shard_map/ppermute | solution.py:382
  64.6 2.6 %collective-permute-start.13 = (bf16[128,512]{1,0:T(8,128)(2,1)S(1)}, bf16[128,512]{1,0:T(8,128)(2,1)S(1)}, u32[]{:S(2)}, u32[]{:S(2)}) collective-permute-start(bf16[128,512]{1,0:T(8,128)(2,1)S(1)} %add_convert_fusion.1.mine), channel_id=1, source_target_pairs={{0,160},{2,162},{4,164},{6,166},{8,168},{10,170},{12,172},{14,174}... | collective-permute-start | bytes 393224 | tf_op jit(solution)/shard_map/ppermute | solution.py:382
  67.2 5.3 %collective-permute-done.13.partner = bf16[128,512]{1,0:T(8,128)(2,1)S(1)} collective-permute-done((bf16[128,512]{1,0:T(8,128)(2,1)S(1)}, bf16[128,512]{1,0:T(8,128)(2,1)S(1)}, u32[]{:S(2)}, u32[]{:S(2)}) %collective-permute-start.13) | collective-permute-done | bytes 131104 | tf_op jit(solution)/shard_map/ppermute | solution.py:382
  75.1 5.3 %collective-permute-start.18 = (bf16[512,128]{1,0:T(8,128)(2,1)S(1)}, bf16[512,128]{1,0:T(8,128)(2,1)S(1)}, u32[]{:S(2)}, u32[]{:S(2)}) collective-permute-start(bf16[512,128]{1,0:T(8,128)(2,1)S(1)} %get-tuple-element.66), channel_id=1, source_target_pairs={{0,34},{2,36},{4,38},{6,40},{8,42},{10,44},{12,46},{14,48},{16,50}... | collective-permute-start | bytes 393224 | tf_op jit(solution)/shard_map/ppermute | solution.py:382
  80.4 1.8 %collective-permute-start.23 = (f32[64,64]{1,0:T(8,128)S(1)}, f32[64,64]{1,0:T(8,128)S(1)}, u32[]{:S(2)}, u32[]{:S(2)}) collective-permute-start(f32[64,64]{1,0:T(8,128)S(1)} %get-tuple-element.71), channel_id=1, source_target_pairs={{0,4},{1,5},{2,6},{3,7},{4,0},{5,1},{6,2},{7,3},{8,12},{9,13},{10,... | collective-permute-start | bytes 49160 | tf_op jit(solution)/shard_map/ppermute | solution.py:394
  82.2 1.9 %collective-permute-start.17 = (bf16[8,128,128]{2,1,0:T(8,128)(2,1)S(1)}, bf16[8,128,128]{2,1,0:T(8,128)(2,1)S(1)}, u32[]{:S(2)}, u32[]{:S(2)}) collective-permute-start(bf16[8,128,128]{2,1,0:T(8,128)(2,1)S(1)} %get-tuple-element.62.e0), channel_id=1, source_target_pairs={{0,96},{32,0},{64,32},{96,64},{128,224},{160,128},{192,160},{224,1... | collective-permute-start | bytes 786440 | tf_op jit(solution)/shard_map/ppermute | solution.py:371
  86.8 4.4 %collective-permute-done.18 = bf16[512,128]{1,0:T(8,128)(2,1)S(1)} collective-permute-done((bf16[512,128]{1,0:T(8,128)(2,1)S(1)}, bf16[512,128]{1,0:T(8,128)(2,1)S(1)}, u32[]{:S(2)}, u32[]{:S(2)}) %collective-permute-start.18) | collective-permute-done | bytes 131104 | tf_op jit(solution)/shard_map/ppermute | solution.py:382
  91.3 5.0 %collective-permute-done.24 = f32[64,64]{1,0:T(8,128)S(1)} collective-permute-done((f32[64,64]{1,0:T(8,128)S(1)}, f32[64,64]{1,0:T(8,128)S(1)}, u32[]{:S(2)}, u32[]{:S(2)}) %collective-permute-start.24) | collective-permute-done | bytes 16416 | tf_op jit(solution)/shard_map/ppermute | solution.py:394
  96.3 1.9 %collective-permute-start.21 = (bf16[512,128]{1,0:T(8,128)(2,1)S(1)}, bf16[512,128]{1,0:T(8,128)(2,1)S(1)}, u32[]{:S(2)}, u32[]{:S(2)}) collective-permute-start(bf16[512,128]{1,0:T(8,128)(2,1)S(1)} %broadcast_select_fusion.p0), channel_id=1, source_target_pairs={{0,96},{32,0},{64,32},{96,64},{128,224},{160,128},{192,160},{224,1... | collective-permute-start | bytes 393224 | tf_op jit(solution)/shard_map/ppermute | solution.py:371
  100.3 3.4 %collective-permute-start.25 = (f32[64,64]{1,0:T(8,128)S(1)}, f32[64,64]{1,0:T(8,128)S(1)}, u32[]{:S(2)}, u32[]{:S(2)}) collective-permute-start(f32[64,64]{1,0:T(8,128)S(1)} %add.54), channel_id=1, source_target_pairs={{0,16},{1,17},{2,18},{3,19},{4,20},{5,21},{6,22},{7,23},{8,24},{9,... | collective-permute-start | bytes 49160 | tf_op jit(solution)/shard_map/ppermute | solution.py:394
  103.7 4.5 %collective-permute-done.25 = f32[64,64]{1,0:T(8,128)S(1)} collective-permute-done((f32[64,64]{1,0:T(8,128)S(1)}, f32[64,64]{1,0:T(8,128)S(1)}, u32[]{:S(2)}, u32[]{:S(2)}) %collective-permute-start.25) | collective-permute-done | bytes 16416 | tf_op jit(solution)/shard_map/ppermute | solution.py:394
  108.3 5.4 %collective-permute-done.26 = f32[64,64]{1,0:T(8,128)S(1)} collective-permute-done((f32[64,64]{1,0:T(8,128)S(1)}, f32[64,64]{1,0:T(8,128)S(1)}, u32[]{:S(2)}, u32[]{:S(2)}) %collective-permute-start.26) | collective-permute-done | bytes 16416 | tf_op jit(solution)/shard_map/ppermute | solution.py:394
  114.9 2.4 %collective-permute-start.28 = (f32[64,64]{1,0:T(8,128)S(1)}, f32[64,64]{1,0:T(8,128)S(1)}, u32[]{:S(2)}, u32[]{:S(2)}) collective-permute-start(f32[64,64]{1,0:T(8,128)S(1)} %add.56), channel_id=1, source_target_pairs={{0,64},{32,96},{64,0},{96,32},{128,192},{160,224},{192,128},{224,1... | collective-permute-start | bytes 49160 | tf_op jit(solution)/shard_map/ppermute | solution.py:371
  119.9 11.1 %gamma_block.1 = bf16[512,3072]{1,0:T(8,128)(2,1)} custom-call(s32[4]{0:T(128)} %pad_add_fusion.info, bf16[8,128,128]{2,1,0:T(8,128)(2,1)} %copy-done, bf16[8,128,128]{2,1,0:T(8,128)(2,1)} %copy-done.9, bf16[8,128,128]{2,1,0:T(8,128)(2,1)} %copy-done.8, bf16[8,128,128]{2,1,0:T(8,128)(2,1)} %copy-done.7, bf16[512,128]{1,0:T(8,128)(2,1)} %copy-done.6, ...), custom_call_target="tpu_custom_call" | custom-call | tf_op jit(solution)/shard_map/gamma_block/pallas_call | solution.py:353
  (83 shorter events, 32.3 us)
Async XLA Ops:
  0.6 12.9 %collective-permute-start.1 = (bf16[512,3072]{1,0:T(8,128)(2,1)}, bf16[512,3072]{1,0:T(8,128)(2,1)S(1)}, u32[]{:S(2)}, u32[]{:S(2)}) collective-permute-start(bf16[512,3072]{1,0:T(8,128)(2,1)} %bitcast.4.own), channel_id=1, source_target_pairs={{0,1},{1,0},{2,3},{3,2},{4,5},{5,4},{6,7},{7,6},{8,9},{9,8},{10,11... | collective-permute-start | bytes 9437192 | tf_op jit(solution)/shard_map/ppermute | solution.py:394
  0.7 49.7 %collective-permute-start.8 = (bf16[512,3072]{1,0:T(8,128)(2,1)}, bf16[512,3072]{1,0:T(8,128)(2,1)}, u32[]{:S(2)}, u32[]{:S(2)}) collective-permute-start(bf16[512,3072]{1,0:T(8,128)(2,1)} %bitcast.4.own), channel_id=1, source_target_pairs={{0,31},{2,1},{4,3},{6,5},{8,7},{10,9},{12,11},{14,13},{16,15},{18,... | collective-permute-start | bytes 9437192 | tf_op jit(solution)/shard_map/ppermute | solution.py:417
  23.3 8.7 %collective-permute-start.3 = (bf16[192,512]{1,0:T(8,128)(2,1)}, bf16[192,512]{1,0:T(8,128)(2,1)S(1)}, u32[]{:S(2)}, u32[]{:S(2)}) collective-permute-start(bf16[192,512]{1,0:T(8,128)(2,1)} %get-tuple-element.43), channel_id=1, source_target_pairs={{0,64},{32,96},{64,0},{96,32},{128,192},{160,224},{192,128},{224,1... | collective-permute-start | bytes 589832 | tf_op jit(solution)/shard_map/ppermute | solution.py:371
  24.4 8.0 %collective-permute-start.4 = (bf16[192,512]{1,0:T(8,128)(2,1)}, bf16[192,512]{1,0:T(8,128)(2,1)S(1)}, u32[]{:S(2)}, u32[]{:S(2)}) collective-permute-start(bf16[192,512]{1,0:T(8,128)(2,1)} %get-tuple-element.44), channel_id=1, source_target_pairs={{0,96},{32,0},{64,32},{96,64},{128,224},{160,128},{192,160},{224,1... | collective-permute-start | bytes 589832 | tf_op jit(solution)/shard_map/ppermute | solution.py:371
  33.4 10.6 %collective-permute-start.5 = (bf16[192,512]{1,0:T(8,128)(2,1)S(1)}, bf16[192,512]{1,0:T(8,128)(2,1)S(1)}, u32[]{:S(2)}, u32[]{:S(2)}) collective-permute-start(bf16[192,512]{1,0:T(8,128)(2,1)S(1)} %add_convert_fusion.here), channel_id=1, source_target_pairs={{0,160},{32,128},{64,224},{96,192},{128,32},{160,0},{192,96},{224,... | collective-permute-start | bytes 589832 | tf_op jit(solution)/shard_map/ppermute | solution.py:377
  36.8 7.3 %collective-permute-start.6 = (f32[8]{0:T(128)S(1)}, f32[8]{0:T(128)S(1)}, u32[]{:S(2)}, u32[]{:S(2)}) collective-permute-start(f32[8]{0:T(128)S(1)} %collective-permute-done.inner_energy.left_energy), channel_id=1, source_target_pairs={{1,62},{3,32},{5,34},{7,36},{9,38},{11,40},{13,42},{15,44},{17,46}... | collective-permute-start | bytes 104 | tf_op jit(solution)/shard_map/ppermute | solution.py:382
  52.1 56.1 %collective-permute-start.22 = (bf16[512,3072]{1,0:T(8,128)(2,1)}, bf16[512,3072]{1,0:T(8,128)(2,1)}, u32[]{:S(2)}, u32[]{:S(2)}) collective-permute-start(bf16[512,3072]{1,0:T(8,128)(2,1)} %bitcast.4.own), channel_id=1, source_target_pairs={{1,2},{3,4},{5,6},{7,8},{9,10},{11,12},{13,14},{15,16},{17,18},{19... | collective-permute-start | bytes 9437192 | tf_op jit(solution)/shard_map/ppermute | solution.py:439
  53.4 6.5 %collective-permute-start.10 = (bf16[128,512]{1,0:T(8,128)(2,1)}, bf16[128,512]{1,0:T(8,128)(2,1)S(1)}, u32[]{:S(2)}, u32[]{:S(2)}) collective-permute-start(bf16[128,512]{1,0:T(8,128)(2,1)} %get-tuple-element.53), channel_id=1, source_target_pairs={{1,32},{3,34},{5,36},{7,38},{9,40},{11,42},{13,44},{15,46},{17,48}... | collective-permute-start | bytes 393224 | tf_op jit(solution)/shard_map/ppermute | solution.py:382
  54.7 8.5 %collective-permute-start.11 = (bf16[128,512]{1,0:T(8,128)(2,1)}, bf16[128,512]{1,0:T(8,128)(2,1)S(1)}, u32[]{:S(2)}, u32[]{:S(2)}) collective-permute-start(bf16[128,512]{1,0:T(8,128)(2,1)} %get-tuple-element.54), channel_id=1, source_target_pairs={{1,64},{3,66},{5,68},{7,70},{9,72},{11,74},{13,76},{15,78},{17,80}... | collective-permute-start | bytes 393224 | tf_op jit(solution)/shard_map/ppermute | solution.py:382
  56.0 8.5 %collective-permute-start.12 = (bf16[128,512]{1,0:T(8,128)(2,1)}, bf16[128,512]{1,0:T(8,128)(2,1)S(1)}, u32[]{:S(2)}, u32[]{:S(2)}) collective-permute-start(bf16[128,512]{1,0:T(8,128)(2,1)} %get-tuple-element.55), channel_id=1, source_target_pairs={{1,96},{3,98},{5,100},{7,102},{9,104},{11,106},{13,108},{15,110},{... | collective-permute-start | bytes 393224 | tf_op jit(solution)/shard_map/ppermute | solution.py:382
  57.3 7.2 %collective-permute-start.9 = (bf16[128,512]{1,0:T(8,128)(2,1)}, bf16[128,512]{1,0:T(8,128)(2,1)S(1)}, u32[]{:S(2)}, u32[]{:S(2)}) collective-permute-start(bf16[128,512]{1,0:T(8,128)(2,1)} %get-tuple-element.52), channel_id=1, source_target_pairs={{1,0},{3,2},{5,4},{7,6},{9,8},{11,10},{13,12},{15,14},{17,16},{19,... | collective-permute-start | bytes 393224 | tf_op jit(solution)/shard_map/ppermute | solution.py:382
  64.6 7.9 %collective-permute-start.13 = (bf16[128,512]{1,0:T(8,128)(2,1)S(1)}, bf16[128,512]{1,0:T(8,128)(2,1)S(1)}, u32[]{:S(2)}, u32[]{:S(2)}) collective-permute-start(bf16[128,512]{1,0:T(8,128)(2,1)S(1)} %add_convert_fusion.1.mine), channel_id=1, source_target_pairs={{0,160},{2,162},{4,164},{6,166},{8,168},{10,170},{12,172},{14,174}... | collective-permute-start | bytes 393224 | tf_op jit(solution)/shard_map/ppermute | solution.py:382
  73.8 8.4 %collective-permute-start.14 = (bf16[512,128]{1,0:T(8,128)(2,1)S(1)}, bf16[512,128]{1,0:T(8,128)(2,1)S(1)}, u32[]{:S(2)}, u32[]{:S(2)}) collective-permute-start(bf16[512,128]{1,0:T(8,128)(2,1)S(1)} %get-tuple-element.61), channel_id=1, source_target_pairs={{0,1},{2,3},{4,5},{6,7},{8,9},{10,11},{12,13},{14,15},{16,17},{18,... | collective-permute-start | bytes 393224 | tf_op jit(solution)/shard_map/ppermute | solution.py:382
  75.1 16.0 %collective-permute-start.18 = (bf16[512,128]{1,0:T(8,128)(2,1)S(1)}, bf16[512,128]{1,0:T(8,128)(2,1)S(1)}, u32[]{:S(2)}, u32[]{:S(2)}) collective-permute-start(bf16[512,128]{1,0:T(8,128)(2,1)S(1)} %get-tuple-element.66), channel_id=1, source_target_pairs={{0,34},{2,36},{4,38},{6,40},{8,42},{10,44},{12,46},{14,48},{16,50}... | collective-permute-start | bytes 393224 | tf_op jit(solution)/shard_map/ppermute | solution.py:382
  82.2 16.1 %collective-permute-start.17 = (bf16[8,128,128]{2,1,0:T(8,128)(2,1)S(1)}, bf16[8,128,128]{2,1,0:T(8,128)(2,1)S(1)}, u32[]{:S(2)}, u32[]{:S(2)}) collective-permute-start(bf16[8,128,128]{2,1,0:T(8,128)(2,1)S(1)} %get-tuple-element.62.e0), channel_id=1, source_target_pairs={{0,96},{32,0},{64,32},{96,64},{128,224},{160,128},{192,160},{224,1... | collective-permute-start | bytes 786440 | tf_op jit(solution)/shard_map/ppermute | solution.py:371
  84.0 15.4 %collective-permute-start.16 = (bf16[8,128,128]{2,1,0:T(8,128)(2,1)S(1)}, bf16[8,128,128]{2,1,0:T(8,128)(2,1)S(1)}, u32[]{:S(2)}, u32[]{:S(2)}) collective-permute-start(bf16[8,128,128]{2,1,0:T(8,128)(2,1)S(1)} %get-tuple-element.62.e0), channel_id=1, source_target_pairs={{0,64},{32,96},{64,0},{96,32},{128,192},{160,224},{192,128},{224,1... | collective-permute-start | bytes 786440 | tf_op jit(solution)/shard_map/ppermute | solution.py:371
  85.5 14.8 %collective-permute-start.15 = (bf16[8,128,128]{2,1,0:T(8,128)(2,1)S(1)}, bf16[8,128,128]{2,1,0:T(8,128)(2,1)S(1)}, u32[]{:S(2)}, u32[]{:S(2)}) collective-permute-start(bf16[8,128,128]{2,1,0:T(8,128)(2,1)S(1)} %get-tuple-element.62.e0), channel_id=1, source_target_pairs={{0,32},{32,64},{64,96},{96,0},{128,160},{160,192},{192,224},{224,1... | collective-permute-start | bytes 786440 | tf_op jit(solution)/shard_map/ppermute | solution.py:371
  96.3 21.0 %collective-permute-start.21 = (bf16[512,128]{1,0:T(8,128)(2,1)S(1)}, bf16[512,128]{1,0:T(8,128)(2,1)S(1)}, u32[]{:S(2)}, u32[]{:S(2)}) collective-permute-start(bf16[512,128]{1,0:T(8,128)(2,1)S(1)} %broadcast_select_fusion.p0), channel_id=1, source_target_pairs={{0,96},{32,0},{64,32},{96,64},{128,224},{160,128},{192,160},{224,1... | collective-permute-start | bytes 393224 | tf_op jit(solution)/shard_map/ppermute | solution.py:371
  98.2 20.3 %collective-permute-start.20 = (bf16[512,128]{1,0:T(8,128)(2,1)S(1)}, bf16[512,128]{1,0:T(8,128)(2,1)S(1)}, u32[]{:S(2)}, u32[]{:S(2)}) collective-permute-start(bf16[512,128]{1,0:T(8,128)(2,1)S(1)} %broadcast_select_fusion.p0), channel_id=1, source_target_pairs={{0,64},{32,96},{64,0},{96,32},{128,192},{160,224},{192,128},{224,1... | collective-permute-start | bytes 393224 | tf_op jit(solution)/shard_map/ppermute | solution.py:371
  99.4 19.2 %collective-permute-start.19 = (bf16[512,128]{1,0:T(8,128)(2,1)S(1)}, bf16[512,128]{1,0:T(8,128)(2,1)S(1)}, u32[]{:S(2)}, u32[]{:S(2)}) collective-permute-start(bf16[512,128]{1,0:T(8,128)(2,1)S(1)} %broadcast_select_fusion.p0), channel_id=1, source_target_pairs={{0,32},{32,64},{64,96},{96,0},{128,160},{160,192},{192,224},{224,1... | collective-permute-start | bytes 393224 | tf_op jit(solution)/shard_map/ppermute | solution.py:371
  100.3 7.9 %collective-permute-start.25 = (f32[64,64]{1,0:T(8,128)S(1)}, f32[64,64]{1,0:T(8,128)S(1)}, u32[]{:S(2)}, u32[]{:S(2)}) collective-permute-start(f32[64,64]{1,0:T(8,128)S(1)} %add.54), channel_id=1, source_target_pairs={{0,16},{1,17},{2,18},{3,19},{4,20},{5,21},{6,22},{7,23},{8,24},{9,... | collective-permute-start | bytes 49160 | tf_op jit(solution)/shard_map/ppermute | solution.py:394
  113.7 17.3 %collective-permute-start.29 = (f32[64,64]{1,0:T(8,128)S(1)}, f32[64,64]{1,0:T(8,128)S(1)}, u32[]{:S(2)}, u32[]{:S(2)}) collective-permute-start(f32[64,64]{1,0:T(8,128)S(1)} %add.56), channel_id=1, source_target_pairs={{0,96},{32,0},{64,32},{96,64},{128,224},{160,128},{192,160},{224,1... | collective-permute-start | bytes 49160 | tf_op jit(solution)/shard_map/ppermute | solution.py:371
  114.9 16.1 %collective-permute-start.28 = (f32[64,64]{1,0:T(8,128)S(1)}, f32[64,64]{1,0:T(8,128)S(1)}, u32[]{:S(2)}, u32[]{:S(2)}) collective-permute-start(f32[64,64]{1,0:T(8,128)S(1)} %add.56), channel_id=1, source_target_pairs={{0,64},{32,96},{64,0},{96,32},{128,192},{160,224},{192,128},{224,1... | collective-permute-start | bytes 49160 | tf_op jit(solution)/shard_map/ppermute | solution.py:371
  117.3 13.7 %collective-permute-start.27 = (f32[64,64]{1,0:T(8,128)S(1)}, f32[64,64]{1,0:T(8,128)S(1)}, u32[]{:S(2)}, u32[]{:S(2)}) collective-permute-start(f32[64,64]{1,0:T(8,128)S(1)} %add.56), channel_id=1, source_target_pairs={{0,32},{32,64},{64,96},{96,0},{128,160},{160,192},{192,224},{224,1... | collective-permute-start | bytes 49160 | tf_op jit(solution)/shard_map/ppermute | solution.py:371
  (21 other events, 293.5 us)

commit v4 on v3

--- a/solution.py
+++ b/solution.py
@@ -11,7 +11,7 @@
 BF16 = jnp.bfloat16
 MIB = 1 << 20
 X = 4
-CHUNKS = 4
+CHUNKS = 3
 SMEM = pl.BlockSpec(memory_space=pltpu.SMEM)
 VMEM = pl.BlockSpec(memory_space=pltpu.VMEM)
 ANY = pl.BlockSpec(memory_space=pl.ANY)

time: 135 us -> 134 us (level)
  Pallas kernels: 22.3 us -> 20.7 us
    pallas_call x1, Pallas kernels: 11.1 us -> 9.67 us  [gamma_block(): pl.pallas_call(gamma_kernel, in_specs=[SMEM] + [VMEM] * 8 + [ANY] * 4, ou...]
  transfers between devices with their start and end apart: 31 -> 31, of which waited for: 16 -> 16; matrix products, arithmetic and copies ran while one was open for 1% -> 1% of each run, Pallas kernels for 16% -> 14%
where the time goes in v4:
time: 134 us; the launch traced here: 131 us
  starting transfers between devices  54.5 us (41%)
  waiting for transfers between devices  50 us (37%)
  Pallas kernels  20.7 us (15%)
  local copies, waits for them, and re-layouts  2.94 us (2%)
  other arithmetic  2.39 us (2%)
    ppermute x8, waiting for transfers between devices, from_cores(): lax.ppermute(value, ('aux', 'occ'), [(a * occ + k, aux_to(a) * occ + occ_...  21.6 us
    ppermute x8, waiting for transfers between devices, swapped(): lax.ppermute(value, axis, [(k, other(k)) for k in range(lax.axis_size(axi...  19.1 us
    ppermute x12, starting transfers between devices, along_x(): lax.ppermute(value, 'aux', [(a, a // X * X + (a + by) % X) for a in range...  18.2 us
    ppermute x8, starting transfers between devices, from_cores(): lax.ppermute(value, ('aux', 'occ'), [(a * occ + k, aux_to(a) * occ + occ_...  15.8 us
    ppermute x1, starting transfers between devices, body(): lax.ppermute(slabs, 'occ', [(k, (k - 1) % occ) for k in range(0, occ, 2)])  12.1 us
    pallas_call x1, Pallas kernels, gamma_block(): pl.pallas_call(gamma_kernel, in_specs=[SMEM] + [VMEM] * 8 + [ANY] * 4, ou...  9.67 us
    pallas_call x1, Pallas kernels, early_integrals(): pl.pallas_call(early_integrals_kernel, in_specs=[SMEM, ANY, ANY], out_spe...  6.36 us
    ppermute x12, waiting for transfers between devices, along_x(): lax.ppermute(value, 'aux', [(a, a // X * X + (a + by) % X) for a in range...  5.85 us
  transfers between devices with their start and end apart: 31, of which 16 were waited for; matrix products, arithmetic and copies ran while one was open for 1% of the time, Pallas kernels for 14%

profile of v4, /device:TPU:2, one launch (start us, length us, event | category | flops | bytes accessed | tf_op | source)
XLA Modules:
  0.0 131.5 jit_solution(11603949718164521694)
XLA Ops:
  0.7 12.1 %collective-permute-start.8 = (bf16[512,3072]{1,0:T(8,128)(2,1)}, bf16[512,3072]{1,0:T(8,128)(2,1)}, u32[]{:S(2)}, u32[]{:S(2)}) collective-permute-start(bf16[512,3072]{1,0:T(8,128)(2,1)} %bitcast.4.own), channel_id=1, source_target_pairs={{0,31},{2,1},{4,3},{6,5},{8,7},{10,9},{12,11},{14,13},{16,15},{18,... | collective-permute-start | bytes 9437192 | tf_op jit(solution)/shard_map/ppermute | solution.py:417
  13.5 1.7 %copy-done.5 = bf16[512,3072]{1,0:T(8,128)(2,1)} copy-done((bf16[512,3072]{1,0:T(8,128)(2,1)}, bf16[512,3072]{1,0:T(8,128)(2,1)S(1)}, u32[]{:S(2)}) %copy-start.5) | copy-done | bytes 3145752
  15.2 6.4 %early_integrals.1 = (bf16[192,512]{1,0:T(8,128)(2,1)}, bf16[192,512]{1,0:T(8,128)(2,1)}, bf16[192,512]{1,0:T(8,128)(2,1)}, bf16[192,512]{1,0:T(8,128)(2,1)}) custom-call(s32[4]{0:T(128)} %pad_add_fusion.info, bf16[512,3072]{1,0:T(8,128)(2,1)} %bitcast.4.own, bf16[512,3072]{1,0:T(8,128)(2,1)} %copy-done.5), custom_call_target="tpu_custom_call" | custom-call | tf_op jit(solution)/shard_map/early_integrals/pallas_call | solution.py:95
  24.2 2.2 %collective-permute-start.4 = (bf16[192,512]{1,0:T(8,128)(2,1)}, bf16[192,512]{1,0:T(8,128)(2,1)S(1)}, u32[]{:S(2)}, u32[]{:S(2)}) collective-permute-start(bf16[192,512]{1,0:T(8,128)(2,1)} %get-tuple-element.44), channel_id=1, source_target_pairs={{0,96},{32,0},{64,32},{96,64},{128,224},{160,128},{192,160},{224,1... | collective-permute-start | bytes 589832 | tf_op jit(solution)/shard_map/ppermute | solution.py:371
  27.5 4.3 %collective-permute-done.3 = bf16[192,512]{1,0:T(8,128)(2,1)S(1)} collective-permute-done((bf16[192,512]{1,0:T(8,128)(2,1)}, bf16[192,512]{1,0:T(8,128)(2,1)S(1)}, u32[]{:S(2)}, u32[]{:S(2)}) %collective-permute-start.3) | collective-permute-done | bytes 196640 | tf_op jit(solution)/shard_map/ppermute | solution.py:371
  33.2 2.2 %collective-permute-start.5 = (bf16[192,512]{1,0:T(8,128)(2,1)S(1)}, bf16[192,512]{1,0:T(8,128)(2,1)S(1)}, u32[]{:S(2)}, u32[]{:S(2)}) collective-permute-start(bf16[192,512]{1,0:T(8,128)(2,1)S(1)} %add_convert_fusion.here), channel_id=1, source_target_pairs={{0,160},{32,128},{64,224},{96,192},{128,32},{160,0},{192,96},{224,... | collective-permute-start | bytes 589832 | tf_op jit(solution)/shard_map/ppermute | solution.py:377
  37.9 6.0 %collective-permute-done.6.right_energy = f32[8]{0:T(128)S(1)} collective-permute-done((f32[8]{0:T(128)S(1)}, f32[8]{0:T(128)S(1)}, u32[]{:S(2)}, u32[]{:S(2)}) %collective-permute-start.6) | collective-permute-done | bytes 64 | tf_op jit(solution)/shard_map/ppermute | solution.py:382
  45.3 1.7 %early_tilde.1 = (bf16[8,128,128]{2,1,0:T(8,128)(2,1)S(1)}, f32[64,64]{1,0:T(8,128)S(1)}) custom-call(s32[4]{0:T(128)S(1)} %copy-done.1, s32[32]{0:T(128)S(1)} %copy-done.3, f32[8]{0:T(128)S(1)} %convert_element_type.39.own_energy, f32[8]{0:T(128)S(1)} %collective-permute-done.inner_energy.left_energy, bf16[192,512]{1,0:T(8,128)(2,1)S(1)} %add_convert_fusion.here, ...), custom_call_target="tpu_custom_call" | custom-call | tf_op jit(solution)/shard_map/early_tilde/pallas_call | solution.py:236
  47.0 3.4 %collective-permute-done.8.following = bf16[512,3072]{1,0:T(8,128)(2,1)} collective-permute-done((bf16[512,3072]{1,0:T(8,128)(2,1)}, bf16[512,3072]{1,0:T(8,128)(2,1)}, u32[]{:S(2)}, u32[]{:S(2)}) %collective-permute-start.8) | collective-permute-done | bytes 3145760 | tf_op jit(solution)/shard_map/ppermute | solution.py:417
  50.5 1.6 %late_integrals.1 = (bf16[128,512]{1,0:T(8,128)(2,1)}, bf16[128,512]{1,0:T(8,128)(2,1)}, bf16[128,512]{1,0:T(8,128)(2,1)}, bf16[128,512]{1,0:T(8,128)(2,1)}) custom-call(s32[4]{0:T(128)} %pad_add_fusion.info, bf16[512,3072]{1,0:T(8,128)(2,1)} %bitcast.4.own, bf16[512,3072]{1,0:T(8,128)(2,1)} %collective-permute-done.8.following), custom_call_target="tpu_custom_call" | custom-call | tf_op jit(solution)/shard_map/late_integrals/pallas_call | solution.py:144
  60.1 3.1 %collective-permute-done.11 = bf16[128,512]{1,0:T(8,128)(2,1)S(1)} collective-permute-done((bf16[128,512]{1,0:T(8,128)(2,1)}, bf16[128,512]{1,0:T(8,128)(2,1)S(1)}, u32[]{:S(2)}, u32[]{:S(2)}) %collective-permute-start.11) | collective-permute-done | bytes 131104 | tf_op jit(solution)/shard_map/ppermute | solution.py:382
  64.5 2.6 %collective-permute-start.13 = (bf16[128,512]{1,0:T(8,128)(2,1)S(1)}, bf16[128,512]{1,0:T(8,128)(2,1)S(1)}, u32[]{:S(2)}, u32[]{:S(2)}) collective-permute-start(bf16[128,512]{1,0:T(8,128)(2,1)S(1)} %add_convert_fusion.1.mine), channel_id=1, source_target_pairs={{0,160},{2,162},{4,164},{6,166},{8,168},{10,170},{12,172},{14,174}... | collective-permute-start | bytes 393224 | tf_op jit(solution)/shard_map/ppermute | solution.py:382
  67.1 5.3 %collective-permute-done.13.partner = bf16[128,512]{1,0:T(8,128)(2,1)S(1)} collective-permute-done((bf16[128,512]{1,0:T(8,128)(2,1)S(1)}, bf16[128,512]{1,0:T(8,128)(2,1)S(1)}, u32[]{:S(2)}, u32[]{:S(2)}) %collective-permute-start.13) | collective-permute-done | bytes 131104 | tf_op jit(solution)/shard_map/ppermute | solution.py:382
  75.0 5.5 %collective-permute-start.18 = (bf16[512,128]{1,0:T(8,128)(2,1)S(1)}, bf16[512,128]{1,0:T(8,128)(2,1)S(1)}, u32[]{:S(2)}, u32[]{:S(2)}) collective-permute-start(bf16[512,128]{1,0:T(8,128)(2,1)S(1)} %get-tuple-element.66), channel_id=1, source_target_pairs={{0,34},{2,36},{4,38},{6,40},{8,42},{10,44},{12,46},{14,48},{16,50}... | collective-permute-start | bytes 393224 | tf_op jit(solution)/shard_map/ppermute | solution.py:382
  80.4 1.6 %collective-permute-start.23 = (f32[64,64]{1,0:T(8,128)S(1)}, f32[64,64]{1,0:T(8,128)S(1)}, u32[]{:S(2)}, u32[]{:S(2)}) collective-permute-start(f32[64,64]{1,0:T(8,128)S(1)} %get-tuple-element.71), channel_id=1, source_target_pairs={{0,4},{1,5},{2,6},{3,7},{4,0},{5,1},{6,2},{7,3},{8,12},{9,13},{10,... | collective-permute-start | bytes 49160 | tf_op jit(solution)/shard_map/ppermute | solution.py:394
  82.1 1.9 %collective-permute-start.17 = (bf16[8,128,128]{2,1,0:T(8,128)(2,1)S(1)}, bf16[8,128,128]{2,1,0:T(8,128)(2,1)S(1)}, u32[]{:S(2)}, u32[]{:S(2)}) collective-permute-start(bf16[8,128,128]{2,1,0:T(8,128)(2,1)S(1)} %get-tuple-element.62.e0), channel_id=1, source_target_pairs={{0,96},{32,0},{64,32},{96,64},{128,224},{160,128},{192,160},{224,1... | collective-permute-start | bytes 786440 | tf_op jit(solution)/shard_map/ppermute | solution.py:371
  86.7 4.5 %collective-permute-done.18 = bf16[512,128]{1,0:T(8,128)(2,1)S(1)} collective-permute-done((bf16[512,128]{1,0:T(8,128)(2,1)S(1)}, bf16[512,128]{1,0:T(8,128)(2,1)S(1)}, u32[]{:S(2)}, u32[]{:S(2)}) %collective-permute-start.18) | collective-permute-done | bytes 131104 | tf_op jit(solution)/shard_map/ppermute | solution.py:382
  91.3 5.0 %collective-permute-done.24 = f32[64,64]{1,0:T(8,128)S(1)} collective-permute-done((f32[64,64]{1,0:T(8,128)S(1)}, f32[64,64]{1,0:T(8,128)S(1)}, u32[]{:S(2)}, u32[]{:S(2)}) %collective-permute-start.24) | collective-permute-done | bytes 16416 | tf_op jit(solution)/shard_map/ppermute | solution.py:394
  96.3 2.0 %collective-permute-start.21 = (bf16[512,128]{1,0:T(8,128)(2,1)S(1)}, bf16[512,128]{1,0:T(8,128)(2,1)S(1)}, u32[]{:S(2)}, u32[]{:S(2)}) collective-permute-start(bf16[512,128]{1,0:T(8,128)(2,1)S(1)} %broadcast_select_fusion.p0), channel_id=1, source_target_pairs={{0,96},{32,0},{64,32},{96,64},{128,224},{160,128},{192,160},{224,1... | collective-permute-start | bytes 393224 | tf_op jit(solution)/shard_map/ppermute | solution.py:371
  100.7 2.9 %collective-permute-start.25 = (f32[64,64]{1,0:T(8,128)S(1)}, f32[64,64]{1,0:T(8,128)S(1)}, u32[]{:S(2)}, u32[]{:S(2)}) collective-permute-start(f32[64,64]{1,0:T(8,128)S(1)} %add.54), channel_id=1, source_target_pairs={{0,16},{1,17},{2,18},{3,19},{4,20},{5,21},{6,22},{7,23},{8,24},{9,... | collective-permute-start | bytes 49160 | tf_op jit(solution)/shard_map/ppermute | solution.py:394
  103.6 5.0 %collective-permute-done.25 = f32[64,64]{1,0:T(8,128)S(1)} collective-permute-done((f32[64,64]{1,0:T(8,128)S(1)}, f32[64,64]{1,0:T(8,128)S(1)}, u32[]{:S(2)}, u32[]{:S(2)}) %collective-permute-start.25) | collective-permute-done | bytes 16416 | tf_op jit(solution)/shard_map/ppermute | solution.py:394
  108.8 5.4 %collective-permute-done.26 = f32[64,64]{1,0:T(8,128)S(1)} collective-permute-done((f32[64,64]{1,0:T(8,128)S(1)}, f32[64,64]{1,0:T(8,128)S(1)}, u32[]{:S(2)}, u32[]{:S(2)}) %collective-permute-start.26) | collective-permute-done | bytes 16416 | tf_op jit(solution)/shard_map/ppermute | solution.py:394
  115.0 2.7 %collective-permute-start.28 = (f32[64,64]{1,0:T(8,128)S(1)}, f32[64,64]{1,0:T(8,128)S(1)}, u32[]{:S(2)}, u32[]{:S(2)}) collective-permute-start(f32[64,64]{1,0:T(8,128)S(1)} %add.56), channel_id=1, source_target_pairs={{0,64},{32,96},{64,0},{96,32},{128,192},{160,224},{192,128},{224,1... | collective-permute-start | bytes 49160 | tf_op jit(solution)/shard_map/ppermute | solution.py:371
  119.8 9.7 %gamma_block.1 = bf16[512,3072]{1,0:T(8,128)(2,1)} custom-call(s32[4]{0:T(128)} %pad_add_fusion.info, bf16[8,128,128]{2,1,0:T(8,128)(2,1)} %copy-done, bf16[8,128,128]{2,1,0:T(8,128)(2,1)} %copy-done.9, bf16[8,128,128]{2,1,0:T(8,128)(2,1)} %copy-done.8, bf16[8,128,128]{2,1,0:T(8,128)(2,1)} %copy-done.7, bf16[512,128]{1,0:T(8,128)(2,1)} %copy-done.6, ...), custom_call_target="tpu_custom_call" | custom-call | tf_op jit(solution)/shard_map/gamma_block/pallas_call | solution.py:353
  (83 shorter events, 31.8 us)
Async XLA Ops:
  0.6 12.9 %collective-permute-start.1 = (bf16[512,3072]{1,0:T(8,128)(2,1)}, bf16[512,3072]{1,0:T(8,128)(2,1)S(1)}, u32[]{:S(2)}, u32[]{:S(2)}) collective-permute-start(bf16[512,3072]{1,0:T(8,128)(2,1)} %bitcast.4.own), channel_id=1, source_target_pairs={{0,1},{1,0},{2,3},{3,2},{4,5},{5,4},{6,7},{7,6},{8,9},{9,8},{10,11... | collective-permute-start | bytes 9437192 | tf_op jit(solution)/shard_map/ppermute | solution.py:394
  0.7 49.7 %collective-permute-start.8 = (bf16[512,3072]{1,0:T(8,128)(2,1)}, bf16[512,3072]{1,0:T(8,128)(2,1)}, u32[]{:S(2)}, u32[]{:S(2)}) collective-permute-start(bf16[512,3072]{1,0:T(8,128)(2,1)} %bitcast.4.own), channel_id=1, source_target_pairs={{0,31},{2,1},{4,3},{6,5},{8,7},{10,9},{12,11},{14,13},{16,15},{18,... | collective-permute-start | bytes 9437192 | tf_op jit(solution)/shard_map/ppermute | solution.py:417
  23.1 8.7 %collective-permute-start.3 = (bf16[192,512]{1,0:T(8,128)(2,1)}, bf16[192,512]{1,0:T(8,128)(2,1)S(1)}, u32[]{:S(2)}, u32[]{:S(2)}) collective-permute-start(bf16[192,512]{1,0:T(8,128)(2,1)} %get-tuple-element.43), channel_id=1, source_target_pairs={{0,64},{32,96},{64,0},{96,32},{128,192},{160,224},{192,128},{224,1... | collective-permute-start | bytes 589832 | tf_op jit(solution)/shard_map/ppermute | solution.py:371
  24.2 8.0 %collective-permute-start.4 = (bf16[192,512]{1,0:T(8,128)(2,1)}, bf16[192,512]{1,0:T(8,128)(2,1)S(1)}, u32[]{:S(2)}, u32[]{:S(2)}) collective-permute-start(bf16[192,512]{1,0:T(8,128)(2,1)} %get-tuple-element.44), channel_id=1, source_target_pairs={{0,96},{32,0},{64,32},{96,64},{128,224},{160,128},{192,160},{224,1... | collective-permute-start | bytes 589832 | tf_op jit(solution)/shard_map/ppermute | solution.py:371
  33.2 10.6 %collective-permute-start.5 = (bf16[192,512]{1,0:T(8,128)(2,1)S(1)}, bf16[192,512]{1,0:T(8,128)(2,1)S(1)}, u32[]{:S(2)}, u32[]{:S(2)}) collective-permute-start(bf16[192,512]{1,0:T(8,128)(2,1)S(1)} %add_convert_fusion.here), channel_id=1, source_target_pairs={{0,160},{32,128},{64,224},{96,192},{128,32},{160,0},{192,96},{224,... | collective-permute-start | bytes 589832 | tf_op jit(solution)/shard_map/ppermute | solution.py:377
  36.6 7.3 %collective-permute-start.6 = (f32[8]{0:T(128)S(1)}, f32[8]{0:T(128)S(1)}, u32[]{:S(2)}, u32[]{:S(2)}) collective-permute-start(f32[8]{0:T(128)S(1)} %collective-permute-done.inner_energy.left_energy), channel_id=1, source_target_pairs={{1,62},{3,32},{5,34},{7,36},{9,38},{11,40},{13,42},{15,44},{17,46}... | collective-permute-start | bytes 104 | tf_op jit(solution)/shard_map/ppermute | solution.py:382
  52.1 56.5 %collective-permute-start.22 = (bf16[512,3072]{1,0:T(8,128)(2,1)}, bf16[512,3072]{1,0:T(8,128)(2,1)}, u32[]{:S(2)}, u32[]{:S(2)}) collective-permute-start(bf16[512,3072]{1,0:T(8,128)(2,1)} %bitcast.4.own), channel_id=1, source_target_pairs={{1,2},{3,4},{5,6},{7,8},{9,10},{11,12},{13,14},{15,16},{17,18},{19... | collective-permute-start | bytes 9437192 | tf_op jit(solution)/shard_map/ppermute | solution.py:439
  53.4 6.7 %collective-permute-start.10 = (bf16[128,512]{1,0:T(8,128)(2,1)}, bf16[128,512]{1,0:T(8,128)(2,1)S(1)}, u32[]{:S(2)}, u32[]{:S(2)}) collective-permute-start(bf16[128,512]{1,0:T(8,128)(2,1)} %get-tuple-element.53), channel_id=1, source_target_pairs={{1,32},{3,34},{5,36},{7,38},{9,40},{11,42},{13,44},{15,46},{17,48}... | collective-permute-start | bytes 393224 | tf_op jit(solution)/shard_map/ppermute | solution.py:382
  54.7 8.4 %collective-permute-start.11 = (bf16[128,512]{1,0:T(8,128)(2,1)}, bf16[128,512]{1,0:T(8,128)(2,1)S(1)}, u32[]{:S(2)}, u32[]{:S(2)}) collective-permute-start(bf16[128,512]{1,0:T(8,128)(2,1)} %get-tuple-element.54), channel_id=1, source_target_pairs={{1,64},{3,66},{5,68},{7,70},{9,72},{11,74},{13,76},{15,78},{17,80}... | collective-permute-start | bytes 393224 | tf_op jit(solution)/shard_map/ppermute | solution.py:382
  56.0 8.4 %collective-permute-start.12 = (bf16[128,512]{1,0:T(8,128)(2,1)}, bf16[128,512]{1,0:T(8,128)(2,1)S(1)}, u32[]{:S(2)}, u32[]{:S(2)}) collective-permute-start(bf16[128,512]{1,0:T(8,128)(2,1)} %get-tuple-element.55), channel_id=1, source_target_pairs={{1,96},{3,98},{5,100},{7,102},{9,104},{11,106},{13,108},{15,110},{... | collective-permute-start | bytes 393224 | tf_op jit(solution)/shard_map/ppermute | solution.py:382
  57.3 7.1 %collective-permute-start.9 = (bf16[128,512]{1,0:T(8,128)(2,1)}, bf16[128,512]{1,0:T(8,128)(2,1)S(1)}, u32[]{:S(2)}, u32[]{:S(2)}) collective-permute-start(bf16[128,512]{1,0:T(8,128)(2,1)} %get-tuple-element.52), channel_id=1, source_target_pairs={{1,0},{3,2},{5,4},{7,6},{9,8},{11,10},{13,12},{15,14},{17,16},{19,... | collective-permute-start | bytes 393224 | tf_op jit(solution)/shard_map/ppermute | solution.py:382
  64.5 7.9 %collective-permute-start.13 = (bf16[128,512]{1,0:T(8,128)(2,1)S(1)}, bf16[128,512]{1,0:T(8,128)(2,1)S(1)}, u32[]{:S(2)}, u32[]{:S(2)}) collective-permute-start(bf16[128,512]{1,0:T(8,128)(2,1)S(1)} %add_convert_fusion.1.mine), channel_id=1, source_target_pairs={{0,160},{2,162},{4,164},{6,166},{8,168},{10,170},{12,172},{14,174}... | collective-permute-start | bytes 393224 | tf_op jit(solution)/shard_map/ppermute | solution.py:382
  73.7 8.4 %collective-permute-start.14 = (bf16[512,128]{1,0:T(8,128)(2,1)S(1)}, bf16[512,128]{1,0:T(8,128)(2,1)S(1)}, u32[]{:S(2)}, u32[]{:S(2)}) collective-permute-start(bf16[512,128]{1,0:T(8,128)(2,1)S(1)} %get-tuple-element.61), channel_id=1, source_target_pairs={{0,1},{2,3},{4,5},{6,7},{8,9},{10,11},{12,13},{14,15},{16,17},{18,... | collective-permute-start | bytes 393224 | tf_op jit(solution)/shard_map/ppermute | solution.py:382
  75.0 16.3 %collective-permute-start.18 = (bf16[512,128]{1,0:T(8,128)(2,1)S(1)}, bf16[512,128]{1,0:T(8,128)(2,1)S(1)}, u32[]{:S(2)}, u32[]{:S(2)}) collective-permute-start(bf16[512,128]{1,0:T(8,128)(2,1)S(1)} %get-tuple-element.66), channel_id=1, source_target_pairs={{0,34},{2,36},{4,38},{6,40},{8,42},{10,44},{12,46},{14,48},{16,50}... | collective-permute-start | bytes 393224 | tf_op jit(solution)/shard_map/ppermute | solution.py:382
  82.1 16.3 %collective-permute-start.17 = (bf16[8,128,128]{2,1,0:T(8,128)(2,1)S(1)}, bf16[8,128,128]{2,1,0:T(8,128)(2,1)S(1)}, u32[]{:S(2)}, u32[]{:S(2)}) collective-permute-start(bf16[8,128,128]{2,1,0:T(8,128)(2,1)S(1)} %get-tuple-element.62.e0), channel_id=1, source_target_pairs={{0,96},{32,0},{64,32},{96,64},{128,224},{160,128},{192,160},{224,1... | collective-permute-start | bytes 786440 | tf_op jit(solution)/shard_map/ppermute | solution.py:371
  84.0 15.5 %collective-permute-start.16 = (bf16[8,128,128]{2,1,0:T(8,128)(2,1)S(1)}, bf16[8,128,128]{2,1,0:T(8,128)(2,1)S(1)}, u32[]{:S(2)}, u32[]{:S(2)}) collective-permute-start(bf16[8,128,128]{2,1,0:T(8,128)(2,1)S(1)} %get-tuple-element.62.e0), channel_id=1, source_target_pairs={{0,64},{32,96},{64,0},{96,32},{128,192},{160,224},{192,128},{224,1... | collective-permute-start | bytes 786440 | tf_op jit(solution)/shard_map/ppermute | solution.py:371
  85.4 15.3 %collective-permute-start.15 = (bf16[8,128,128]{2,1,0:T(8,128)(2,1)S(1)}, bf16[8,128,128]{2,1,0:T(8,128)(2,1)S(1)}, u32[]{:S(2)}, u32[]{:S(2)}) collective-permute-start(bf16[8,128,128]{2,1,0:T(8,128)(2,1)S(1)} %get-tuple-element.62.e0), channel_id=1, source_target_pairs={{0,32},{32,64},{64,96},{96,0},{128,160},{160,192},{192,224},{224,1... | collective-permute-start | bytes 786440 | tf_op jit(solution)/shard_map/ppermute | solution.py:371
  96.3 21.4 %collective-permute-start.21 = (bf16[512,128]{1,0:T(8,128)(2,1)S(1)}, bf16[512,128]{1,0:T(8,128)(2,1)S(1)}, u32[]{:S(2)}, u32[]{:S(2)}) collective-permute-start(bf16[512,128]{1,0:T(8,128)(2,1)S(1)} %broadcast_select_fusion.p0), channel_id=1, source_target_pairs={{0,96},{32,0},{64,32},{96,64},{128,224},{160,128},{192,160},{224,1... | collective-permute-start | bytes 393224 | tf_op jit(solution)/shard_map/ppermute | solution.py:371
  98.3 20.2 %collective-permute-start.20 = (bf16[512,128]{1,0:T(8,128)(2,1)S(1)}, bf16[512,128]{1,0:T(8,128)(2,1)S(1)}, u32[]{:S(2)}, u32[]{:S(2)}) collective-permute-start(bf16[512,128]{1,0:T(8,128)(2,1)S(1)} %broadcast_select_fusion.p0), channel_id=1, source_target_pairs={{0,64},{32,96},{64,0},{96,32},{128,192},{160,224},{192,128},{224,1... | collective-permute-start | bytes 393224 | tf_op jit(solution)/shard_map/ppermute | solution.py:371
  99.5 19.1 %collective-permute-start.19 = (bf16[512,128]{1,0:T(8,128)(2,1)S(1)}, bf16[512,128]{1,0:T(8,128)(2,1)S(1)}, u32[]{:S(2)}, u32[]{:S(2)}) collective-permute-start(bf16[512,128]{1,0:T(8,128)(2,1)S(1)} %broadcast_select_fusion.p0), channel_id=1, source_target_pairs={{0,32},{32,64},{64,96},{96,0},{128,160},{160,192},{192,224},{224,1... | collective-permute-start | bytes 393224 | tf_op jit(solution)/shard_map/ppermute | solution.py:371
  100.7 7.9 %collective-permute-start.25 = (f32[64,64]{1,0:T(8,128)S(1)}, f32[64,64]{1,0:T(8,128)S(1)}, u32[]{:S(2)}, u32[]{:S(2)}) collective-permute-start(f32[64,64]{1,0:T(8,128)S(1)} %add.54), channel_id=1, source_target_pairs={{0,16},{1,17},{2,18},{3,19},{4,20},{5,21},{6,22},{7,23},{8,24},{9,... | collective-permute-start | bytes 49160 | tf_op jit(solution)/shard_map/ppermute | solution.py:394
  114.2 15.4 %collective-permute-start.29 = (f32[64,64]{1,0:T(8,128)S(1)}, f32[64,64]{1,0:T(8,128)S(1)}, u32[]{:S(2)}, u32[]{:S(2)}) collective-permute-start(f32[64,64]{1,0:T(8,128)S(1)} %add.56), channel_id=1, source_target_pairs={{0,96},{32,0},{64,32},{96,64},{128,224},{160,128},{192,160},{224,1... | collective-permute-start | bytes 49160 | tf_op jit(solution)/shard_map/ppermute | solution.py:371
  115.0 14.6 %collective-permute-start.28 = (f32[64,64]{1,0:T(8,128)S(1)}, f32[64,64]{1,0:T(8,128)S(1)}, u32[]{:S(2)}, u32[]{:S(2)}) collective-permute-start(f32[64,64]{1,0:T(8,128)S(1)} %add.56), channel_id=1, source_target_pairs={{0,64},{32,96},{64,0},{96,32},{128,192},{160,224},{192,128},{224,1... | collective-permute-start | bytes 49160 | tf_op jit(solution)/shard_map/ppermute | solution.py:371
  117.7 11.8 %collective-permute-start.27 = (f32[64,64]{1,0:T(8,128)S(1)}, f32[64,64]{1,0:T(8,128)S(1)}, u32[]{:S(2)}, u32[]{:S(2)}) collective-permute-start(f32[64,64]{1,0:T(8,128)S(1)} %add.56), channel_id=1, source_target_pairs={{0,32},{32,64},{64,96},{96,0},{128,160},{160,192},{192,224},{224,1... | collective-permute-start | bytes 49160 | tf_op jit(solution)/shard_map/ppermute | solution.py:371
  (21 other events, 291.3 us)

commit v5 on v4

--- a/solution.py
+++ b/solution.py
@@ -153,7 +153,7 @@
             pltpu.SemaphoreType.DMA((CHUNKS,)),
             pltpu.SemaphoreType.DMA((CHUNKS,)),
         ],
-        compiler_params=params(56),
+        compiler_params=params(40),
         cost_estimate=pl.CostEstimate(flops=0, bytes_accessed=0, transcendentals=0),
         name="late_integrals",
     )(info, own, following)

time: 134 us -> 133 us (level)
  waiting for transfers between devices: 50 us -> 48.4 us
  starting transfers between devices: 54.5 us -> 55.9 us
    ppermute x8, waiting for transfers between devices: 19.1 us -> 17.4 us  [swapped(): lax.ppermute(value, axis, [(k, other(k)) for k in range(lax.axis_size(axi...]
    unnamed x28 -> x24, local copies, waits for them, and re-layouts: 2.94 us -> 1.94 us
  transfers between devices with their start and end apart: 31 -> 31, of which waited for: 16 -> 16; matrix products, arithmetic and copies ran while one was open for 1% -> 2% of each run, Pallas kernels for 14% -> 15%
where the time goes in v5:
time: 133 us; the launch traced here: 131 us
  starting transfers between devices  55.9 us (42%)
  waiting for transfers between devices  48.4 us (36%)
  Pallas kernels  20.4 us (15%)
  other arithmetic  3.35 us (3%)
  local copies, waits for them, and re-layouts  1.94 us (1%)
    ppermute x8, waiting for transfers between devices, from_cores(): lax.ppermute(value, ('aux', 'occ'), [(a * occ + k, aux_to(a) * occ + occ_...  20.5 us
    ppermute x12, starting transfers between devices, along_x(): lax.ppermute(value, 'aux', [(a, a // X * X + (a + by) % X) for a in range...  18.2 us
    ppermute x8, waiting for transfers between devices, swapped(): lax.ppermute(value, axis, [(k, other(k)) for k in range(lax.axis_size(axi...  17.4 us
    ppermute x8, starting transfers between devices, from_cores(): lax.ppermute(value, ('aux', 'occ'), [(a * occ + k, aux_to(a) * occ + occ_...  16 us
    ppermute x1, starting transfers between devices, body(): lax.ppermute(slabs, 'occ', [(k, (k - 1) % occ) for k in range(0, occ, 2)])  12.2 us
    pallas_call x1, Pallas kernels, gamma_block(): pl.pallas_call(gamma_kernel, in_specs=[SMEM] + [VMEM] * 8 + [ANY] * 4, ou...  9.67 us
    pallas_call x1, Pallas kernels, early_integrals(): pl.pallas_call(early_integrals_kernel, in_specs=[SMEM, ANY, ANY], out_spe...  6.64 us
    ppermute x8, starting transfers between devices, swapped(): lax.ppermute(value, axis, [(k, other(k)) for k in range(lax.axis_size(axi...  5.92 us
  transfers between devices with their start and end apart: 31, of which 16 were waited for; matrix products, arithmetic and copies ran while one was open for 2% of the time, Pallas kernels for 15%

profile of v5, /device:TPU:2, one launch (start us, length us, event | category | flops | bytes accessed | tf_op | source)
XLA Modules:
  0.0 131.0 jit_solution(6543258189963523723)
XLA Ops:
  0.7 12.2 %collective-permute-start.8 = (bf16[512,3072]{1,0:T(8,128)(2,1)}, bf16[512,3072]{1,0:T(8,128)(2,1)}, u32[]{:S(2)}, u32[]{:S(2)}) collective-permute-start(bf16[512,3072]{1,0:T(8,128)(2,1)} %bitcast.8), channel_id=1, source_target_pairs={{0,31},{2,1},{4,3},{6,5},{8,7},{10,9},{12,11},{14,13},{16,15},{18,... | collective-permute-start | bytes 9437192 | tf_op jit(solution)/shard_map/ppermute | solution.py:417
  13.6 6.6 %early_integrals.1 = (bf16[192,512]{1,0:T(8,128)(2,1)}, bf16[192,512]{1,0:T(8,128)(2,1)}, bf16[192,512]{1,0:T(8,128)(2,1)}, bf16[192,512]{1,0:T(8,128)(2,1)}) custom-call(s32[4]{0:T(128)} %pad_add_fusion.info, bf16[512,3072]{1,0:T(8,128)(2,1)} %bitcast.9, bf16[512,3072]{1,0:T(8,128)(2,1)} %collective-permute-done.1.other), custom_call_target="tpu_custom_call" | custom-call | tf_op jit(solution)/shard_map/early_integrals/pallas_call | solution.py:95
  20.3 1.6 %collective-permute-start.2 = (bf16[192,512]{1,0:T(8,128)(2,1)}, bf16[192,512]{1,0:T(8,128)(2,1)S(1)}, u32[]{:S(2)}, u32[]{:S(2)}) collective-permute-start(bf16[192,512]{1,0:T(8,128)(2,1)} %get-tuple-element.42), channel_id=1, source_target_pairs={{0,32},{32,64},{64,96},{96,0},{128,160},{160,192},{192,224},{224,1... | collective-permute-start | bytes 589832 | tf_op jit(solution)/shard_map/ppermute | solution.py:371
  22.9 2.2 %collective-permute-start.4 = (bf16[192,512]{1,0:T(8,128)(2,1)}, bf16[192,512]{1,0:T(8,128)(2,1)S(1)}, u32[]{:S(2)}, u32[]{:S(2)}) collective-permute-start(bf16[192,512]{1,0:T(8,128)(2,1)} %get-tuple-element.44), channel_id=1, source_target_pairs={{0,96},{32,0},{64,32},{96,64},{128,224},{160,128},{192,160},{224,1... | collective-permute-start | bytes 589832 | tf_op jit(solution)/shard_map/ppermute | solution.py:371
  26.2 4.6 %collective-permute-done.3 = bf16[192,512]{1,0:T(8,128)(2,1)S(1)} collective-permute-done((bf16[192,512]{1,0:T(8,128)(2,1)}, bf16[192,512]{1,0:T(8,128)(2,1)S(1)}, u32[]{:S(2)}, u32[]{:S(2)}) %collective-permute-start.3) | collective-permute-done | bytes 196640 | tf_op jit(solution)/shard_map/ppermute | solution.py:371
  32.0 2.3 %collective-permute-start.5 = (bf16[192,512]{1,0:T(8,128)(2,1)S(1)}, bf16[192,512]{1,0:T(8,128)(2,1)S(1)}, u32[]{:S(2)}, u32[]{:S(2)}) collective-permute-start(bf16[192,512]{1,0:T(8,128)(2,1)S(1)} %add_convert_fusion.here), channel_id=1, source_target_pairs={{0,160},{32,128},{64,224},{96,192},{128,32},{160,0},{192,96},{224,... | collective-permute-start | bytes 589832 | tf_op jit(solution)/shard_map/ppermute | solution.py:377
  36.7 6.0 %collective-permute-done.6.right_energy = f32[8]{0:T(128)S(1)} collective-permute-done((f32[8]{0:T(128)S(1)}, f32[8]{0:T(128)S(1)}, u32[]{:S(2)}, u32[]{:S(2)}) %collective-permute-start.6) | collective-permute-done | bytes 64 | tf_op jit(solution)/shard_map/ppermute | solution.py:382
  44.1 1.7 %early_tilde.1 = (bf16[8,128,128]{2,1,0:T(8,128)(2,1)S(1)}, f32[64,64]{1,0:T(8,128)S(1)}) custom-call(s32[4]{0:T(128)S(1)} %copy-done.2, s32[32]{0:T(128)S(1)} %copy-done.3, f32[8]{0:T(128)S(1)} %convert_element_type.39.own_energy, f32[8]{0:T(128)S(1)} %collective-permute-done.inner_energy.left_energy, bf16[192,512]{1,0:T(8,128)(2,1)S(1)} %add_convert_fusion.here, ...), custom_call_target="tpu_custom_call" | custom-call | tf_op jit(solution)/shard_map/early_tilde/pallas_call | solution.py:236
  45.9 4.6 %collective-permute-done.8.following = bf16[512,3072]{1,0:T(8,128)(2,1)} collective-permute-done((bf16[512,3072]{1,0:T(8,128)(2,1)}, bf16[512,3072]{1,0:T(8,128)(2,1)}, u32[]{:S(2)}, u32[]{:S(2)}) %collective-permute-start.8) | collective-permute-done | bytes 3145760 | tf_op jit(solution)/shard_map/ppermute | solution.py:417
  58.7 2.9 %collective-permute-done.11 = bf16[128,512]{1,0:T(8,128)(2,1)S(1)} collective-permute-done((bf16[128,512]{1,0:T(8,128)(2,1)S(1)}, bf16[128,512]{1,0:T(8,128)(2,1)S(1)}, u32[]{:S(2)}, u32[]{:S(2)}) %collective-permute-start.11) | collective-permute-done | bytes 131104 | tf_op jit(solution)/shard_map/ppermute | solution.py:382
  63.0 2.6 %collective-permute-start.13 = (bf16[128,512]{1,0:T(8,128)(2,1)S(1)}, bf16[128,512]{1,0:T(8,128)(2,1)S(1)}, u32[]{:S(2)}, u32[]{:S(2)}) collective-permute-start(bf16[128,512]{1,0:T(8,128)(2,1)S(1)} %add_convert_fusion.1.mine), channel_id=1, source_target_pairs={{0,160},{2,162},{4,164},{6,166},{8,168},{10,170},{12,172},{14,174}... | collective-permute-start | bytes 393224 | tf_op jit(solution)/shard_map/ppermute | solution.py:382
  65.6 5.2 %collective-permute-done.13.partner = bf16[128,512]{1,0:T(8,128)(2,1)S(1)} collective-permute-done((bf16[128,512]{1,0:T(8,128)(2,1)S(1)}, bf16[128,512]{1,0:T(8,128)(2,1)S(1)}, u32[]{:S(2)}, u32[]{:S(2)}) %collective-permute-start.13) | collective-permute-done | bytes 131104 | tf_op jit(solution)/shard_map/ppermute | solution.py:382
  70.9 1.8 %late_tilde.1 = (bf16[512,128]{1,0:T(8,128)(2,1)S(1)}, bf16[512,128]{1,0:T(8,128)(2,1)}, f32[64,64]{1,0:T(8,128)S(1)}) custom-call(s32[4]{0:T(128)S(1)} %copy-done.2, s32[32]{0:T(128)S(1)} %copy-done.3, f32[8]{0:T(128)S(1)} %collective-permute-done.inner_energy.left_energy, f32[8]{0:T(128)S(1)} %collective-permute-done.6.right_energy, ...), custom_call_target="tpu_custom_call" | custom-call | tf_op jit(solution)/shard_map/late_tilde/pallas_call | solution.py:270
  73.9 5.6 %collective-permute-start.18 = (bf16[512,128]{1,0:T(8,128)(2,1)}, bf16[512,128]{1,0:T(8,128)(2,1)}, u32[]{:S(2)}, u32[]{:S(2)}) collective-permute-start(bf16[512,128]{1,0:T(8,128)(2,1)} %get-tuple-element.66), channel_id=1, source_target_pairs={{0,34},{2,36},{4,38},{6,40},{8,42},{10,44},{12,46},{14,48},{16,50}... | collective-permute-start | bytes 393224 | tf_op jit(solution)/shard_map/ppermute | solution.py:382
  79.5 1.8 %collective-permute-start.23 = (f32[64,64]{1,0:T(8,128)S(1)}, f32[64,64]{1,0:T(8,128)S(1)}, u32[]{:S(2)}, u32[]{:S(2)}) collective-permute-start(f32[64,64]{1,0:T(8,128)S(1)} %get-tuple-element.71), channel_id=1, source_target_pairs={{0,4},{1,5},{2,6},{3,7},{4,0},{5,1},{6,2},{7,3},{8,12},{9,13},{10,... | collective-permute-start | bytes 49160 | tf_op jit(solution)/shard_map/ppermute | solution.py:394
  82.0 1.9 %collective-permute-start.17 = (bf16[8,128,128]{2,1,0:T(8,128)(2,1)S(1)}, bf16[8,128,128]{2,1,0:T(8,128)(2,1)}, u32[]{:S(2)}, u32[]{:S(2)}) collective-permute-start(bf16[8,128,128]{2,1,0:T(8,128)(2,1)S(1)} %get-tuple-element.62.e0), channel_id=1, source_target_pairs={{0,96},{32,0},{64,32},{96,64},{128,224},{160,128},{192,160},{224,1... | collective-permute-start | bytes 786440 | tf_op jit(solution)/shard_map/ppermute | solution.py:371
  86.6 4.0 %collective-permute-done.18 = bf16[512,128]{1,0:T(8,128)(2,1)} collective-permute-done((bf16[512,128]{1,0:T(8,128)(2,1)}, bf16[512,128]{1,0:T(8,128)(2,1)}, u32[]{:S(2)}, u32[]{:S(2)}) %collective-permute-start.18) | collective-permute-done | bytes 131104 | tf_op jit(solution)/shard_map/ppermute | solution.py:382
  92.0 3.8 %collective-permute-done.24 = f32[64,64]{1,0:T(8,128)S(1)} collective-permute-done((f32[64,64]{1,0:T(8,128)S(1)}, f32[64,64]{1,0:T(8,128)S(1)}, u32[]{:S(2)}, u32[]{:S(2)}) %collective-permute-start.24) | collective-permute-done | bytes 16416 | tf_op jit(solution)/shard_map/ppermute | solution.py:394
  95.8 1.9 %collective-permute-start.21 = (bf16[512,128]{1,0:T(8,128)(2,1)S(1)}, bf16[512,128]{1,0:T(8,128)(2,1)S(1)}, u32[]{:S(2)}, u32[]{:S(2)}) collective-permute-start(bf16[512,128]{1,0:T(8,128)(2,1)S(1)} %broadcast_select_fusion.p0), channel_id=1, source_target_pairs={{0,96},{32,0},{64,32},{96,64},{128,224},{160,128},{192,160},{224,1... | collective-permute-start | bytes 393224 | tf_op jit(solution)/shard_map/ppermute | solution.py:371
  100.1 3.3 %collective-permute-start.25 = (f32[64,64]{1,0:T(8,128)S(1)}, f32[64,64]{1,0:T(8,128)S(1)}, u32[]{:S(2)}, u32[]{:S(2)}) collective-permute-start(f32[64,64]{1,0:T(8,128)S(1)} %add.54), channel_id=1, source_target_pairs={{0,16},{1,17},{2,18},{3,19},{4,20},{5,21},{6,22},{7,23},{8,24},{9,... | collective-permute-start | bytes 49160 | tf_op jit(solution)/shard_map/ppermute | solution.py:394
  103.4 4.6 %collective-permute-done.25 = f32[64,64]{1,0:T(8,128)S(1)} collective-permute-done((f32[64,64]{1,0:T(8,128)S(1)}, f32[64,64]{1,0:T(8,128)S(1)}, u32[]{:S(2)}, u32[]{:S(2)}) %collective-permute-start.25) | collective-permute-done | bytes 16416 | tf_op jit(solution)/shard_map/ppermute | solution.py:394
  108.1 5.4 %collective-permute-done.26 = f32[64,64]{1,0:T(8,128)S(1)} collective-permute-done((f32[64,64]{1,0:T(8,128)S(1)}, f32[64,64]{1,0:T(8,128)S(1)}, u32[]{:S(2)}, u32[]{:S(2)}) %collective-permute-start.26) | collective-permute-done | bytes 16416 | tf_op jit(solution)/shard_map/ppermute | solution.py:394
  114.4 2.4 %collective-permute-start.28 = (f32[64,64]{1,0:T(8,128)S(1)}, f32[64,64]{1,0:T(8,128)S(1)}, u32[]{:S(2)}, u32[]{:S(2)}) collective-permute-start(f32[64,64]{1,0:T(8,128)S(1)} %add.56), channel_id=1, source_target_pairs={{0,64},{32,96},{64,0},{96,32},{128,192},{160,224},{192,128},{224,1... | collective-permute-start | bytes 49160 | tf_op jit(solution)/shard_map/ppermute | solution.py:371
  119.3 9.7 %gamma_block.1 = bf16[512,3072]{1,0:T(8,128)(2,1)} custom-call(s32[4]{0:T(128)} %pad_add_fusion.info, bf16[8,128,128]{2,1,0:T(8,128)(2,1)} %copy-done.1, bf16[8,128,128]{2,1,0:T(8,128)(2,1)} %copy-done.6, bf16[8,128,128]{2,1,0:T(8,128)(2,1)} %collective-permute-done.16.e2, bf16[8,128,128]{2,1,0:T(8,128)(2,1)} %collective-permute-done.17.e3, ...), custom_call_target="tpu_custom_call" | custom-call | tf_op jit(solution)/shard_map/gamma_block/pallas_call | solution.py:353
  (79 shorter events, 31.4 us)
Async XLA Ops:
  0.6 13.0 %collective-permute-start.1 = (bf16[512,3072]{1,0:T(8,128)(2,1)}, bf16[512,3072]{1,0:T(8,128)(2,1)}, u32[]{:S(2)}, u32[]{:S(2)}) collective-permute-start(bf16[512,3072]{1,0:T(8,128)(2,1)} %bitcast.7), channel_id=1, source_target_pairs={{0,1},{1,0},{2,3},{3,2},{4,5},{5,4},{6,7},{7,6},{8,9},{9,8},{10,11... | collective-permute-start | bytes 9437192 | tf_op jit(solution)/shard_map/ppermute | solution.py:394
  0.7 49.7 %collective-permute-start.8 = (bf16[512,3072]{1,0:T(8,128)(2,1)}, bf16[512,3072]{1,0:T(8,128)(2,1)}, u32[]{:S(2)}, u32[]{:S(2)}) collective-permute-start(bf16[512,3072]{1,0:T(8,128)(2,1)} %bitcast.8), channel_id=1, source_target_pairs={{0,31},{2,1},{4,3},{6,5},{8,7},{10,9},{12,11},{14,13},{16,15},{18,... | collective-permute-start | bytes 9437192 | tf_op jit(solution)/shard_map/ppermute | solution.py:417
  21.8 9.0 %collective-permute-start.3 = (bf16[192,512]{1,0:T(8,128)(2,1)}, bf16[192,512]{1,0:T(8,128)(2,1)S(1)}, u32[]{:S(2)}, u32[]{:S(2)}) collective-permute-start(bf16[192,512]{1,0:T(8,128)(2,1)} %get-tuple-element.43), channel_id=1, source_target_pairs={{0,64},{32,96},{64,0},{96,32},{128,192},{160,224},{192,128},{224,1... | collective-permute-start | bytes 589832 | tf_op jit(solution)/shard_map/ppermute | solution.py:371
  22.9 8.0 %collective-permute-start.4 = (bf16[192,512]{1,0:T(8,128)(2,1)}, bf16[192,512]{1,0:T(8,128)(2,1)S(1)}, u32[]{:S(2)}, u32[]{:S(2)}) collective-permute-start(bf16[192,512]{1,0:T(8,128)(2,1)} %get-tuple-element.44), channel_id=1, source_target_pairs={{0,96},{32,0},{64,32},{96,64},{128,224},{160,128},{192,160},{224,1... | collective-permute-start | bytes 589832 | tf_op jit(solution)/shard_map/ppermute | solution.py:371
  32.0 10.7 %collective-permute-start.5 = (bf16[192,512]{1,0:T(8,128)(2,1)S(1)}, bf16[192,512]{1,0:T(8,128)(2,1)S(1)}, u32[]{:S(2)}, u32[]{:S(2)}) collective-permute-start(bf16[192,512]{1,0:T(8,128)(2,1)S(1)} %add_convert_fusion.here), channel_id=1, source_target_pairs={{0,160},{32,128},{64,224},{96,192},{128,32},{160,0},{192,96},{224,... | collective-permute-start | bytes 589832 | tf_op jit(solution)/shard_map/ppermute | solution.py:377
  35.4 7.3 %collective-permute-start.6 = (f32[8]{0:T(128)S(1)}, f32[8]{0:T(128)S(1)}, u32[]{:S(2)}, u32[]{:S(2)}) collective-permute-start(f32[8]{0:T(128)S(1)} %collective-permute-done.inner_energy.left_energy), channel_id=1, source_target_pairs={{1,62},{3,32},{5,34},{7,36},{9,38},{11,40},{13,42},{15,44},{17,46}... | collective-permute-start | bytes 104 | tf_op jit(solution)/shard_map/ppermute | solution.py:382
  51.1 56.9 %collective-permute-start.22 = (bf16[512,3072]{1,0:T(8,128)(2,1)S(1)}, bf16[512,3072]{1,0:T(8,128)(2,1)}, u32[]{:S(2)}, u32[]{:S(2)}) collective-permute-start(bf16[512,3072]{1,0:T(8,128)(2,1)S(1)} %bitcast.12), channel_id=1, source_target_pairs={{1,2},{3,4},{5,6},{7,8},{9,10},{11,12},{13,14},{15,16},{17,18},{19... | collective-permute-start | bytes 9437192 | tf_op jit(solution)/shard_map/ppermute | solution.py:439
  52.4 6.3 %collective-permute-start.10 = (bf16[128,512]{1,0:T(8,128)(2,1)S(1)}, bf16[128,512]{1,0:T(8,128)(2,1)S(1)}, u32[]{:S(2)}, u32[]{:S(2)}) collective-permute-start(bf16[128,512]{1,0:T(8,128)(2,1)S(1)} %get-tuple-element.53), channel_id=1, source_target_pairs={{1,32},{3,34},{5,36},{7,38},{9,40},{11,42},{13,44},{15,46},{17,48}... | collective-permute-start | bytes 393224 | tf_op jit(solution)/shard_map/ppermute | solution.py:382
  53.7 7.9 %collective-permute-start.11 = (bf16[128,512]{1,0:T(8,128)(2,1)S(1)}, bf16[128,512]{1,0:T(8,128)(2,1)S(1)}, u32[]{:S(2)}, u32[]{:S(2)}) collective-permute-start(bf16[128,512]{1,0:T(8,128)(2,1)S(1)} %get-tuple-element.54), channel_id=1, source_target_pairs={{1,64},{3,66},{5,68},{7,70},{9,72},{11,74},{13,76},{15,78},{17,80}... | collective-permute-start | bytes 393224 | tf_op jit(solution)/shard_map/ppermute | solution.py:382
  55.0 7.9 %collective-permute-start.12 = (bf16[128,512]{1,0:T(8,128)(2,1)S(1)}, bf16[128,512]{1,0:T(8,128)(2,1)S(1)}, u32[]{:S(2)}, u32[]{:S(2)}) collective-permute-start(bf16[128,512]{1,0:T(8,128)(2,1)S(1)} %get-tuple-element.55), channel_id=1, source_target_pairs={{1,96},{3,98},{5,100},{7,102},{9,104},{11,106},{13,108},{15,110},{... | collective-permute-start | bytes 393224 | tf_op jit(solution)/shard_map/ppermute | solution.py:382
  56.3 6.6 %collective-permute-start.9 = (bf16[128,512]{1,0:T(8,128)(2,1)S(1)}, bf16[128,512]{1,0:T(8,128)(2,1)S(1)}, u32[]{:S(2)}, u32[]{:S(2)}) collective-permute-start(bf16[128,512]{1,0:T(8,128)(2,1)S(1)} %get-tuple-element.52), channel_id=1, source_target_pairs={{1,0},{3,2},{5,4},{7,6},{9,8},{11,10},{13,12},{15,14},{17,16},{19,... | collective-permute-start | bytes 393224 | tf_op jit(solution)/shard_map/ppermute | solution.py:382
  63.0 7.9 %collective-permute-start.13 = (bf16[128,512]{1,0:T(8,128)(2,1)S(1)}, bf16[128,512]{1,0:T(8,128)(2,1)S(1)}, u32[]{:S(2)}, u32[]{:S(2)}) collective-permute-start(bf16[128,512]{1,0:T(8,128)(2,1)S(1)} %add_convert_fusion.1.mine), channel_id=1, source_target_pairs={{0,160},{2,162},{4,164},{6,166},{8,168},{10,170},{12,172},{14,174}... | collective-permute-start | bytes 393224 | tf_op jit(solution)/shard_map/ppermute | solution.py:382
  72.6 8.7 %collective-permute-start.14 = (bf16[512,128]{1,0:T(8,128)(2,1)S(1)}, bf16[512,128]{1,0:T(8,128)(2,1)S(1)}, u32[]{:S(2)}, u32[]{:S(2)}) collective-permute-start(bf16[512,128]{1,0:T(8,128)(2,1)S(1)} %get-tuple-element.61), channel_id=1, source_target_pairs={{0,1},{2,3},{4,5},{6,7},{8,9},{10,11},{12,13},{14,15},{16,17},{18,... | collective-permute-start | bytes 393224 | tf_op jit(solution)/shard_map/ppermute | solution.py:382
  73.9 16.7 %collective-permute-start.18 = (bf16[512,128]{1,0:T(8,128)(2,1)}, bf16[512,128]{1,0:T(8,128)(2,1)}, u32[]{:S(2)}, u32[]{:S(2)}) collective-permute-start(bf16[512,128]{1,0:T(8,128)(2,1)} %get-tuple-element.66), channel_id=1, source_target_pairs={{0,34},{2,36},{4,38},{6,40},{8,42},{10,44},{12,46},{14,48},{16,50}... | collective-permute-start | bytes 393224 | tf_op jit(solution)/shard_map/ppermute | solution.py:382
  82.0 15.8 %collective-permute-start.17 = (bf16[8,128,128]{2,1,0:T(8,128)(2,1)S(1)}, bf16[8,128,128]{2,1,0:T(8,128)(2,1)}, u32[]{:S(2)}, u32[]{:S(2)}) collective-permute-start(bf16[8,128,128]{2,1,0:T(8,128)(2,1)S(1)} %get-tuple-element.62.e0), channel_id=1, source_target_pairs={{0,96},{32,0},{64,32},{96,64},{128,224},{160,128},{192,160},{224,1... | collective-permute-start | bytes 786440 | tf_op jit(solution)/shard_map/ppermute | solution.py:371
  83.9 15.0 %collective-permute-start.16 = (bf16[8,128,128]{2,1,0:T(8,128)(2,1)S(1)}, bf16[8,128,128]{2,1,0:T(8,128)(2,1)}, u32[]{:S(2)}, u32[]{:S(2)}) collective-permute-start(bf16[8,128,128]{2,1,0:T(8,128)(2,1)S(1)} %get-tuple-element.62.e0), channel_id=1, source_target_pairs={{0,64},{32,96},{64,0},{96,32},{128,192},{160,224},{192,128},{224,1... | collective-permute-start | bytes 786440 | tf_op jit(solution)/shard_map/ppermute | solution.py:371
  85.3 14.8 %collective-permute-start.15 = (bf16[8,128,128]{2,1,0:T(8,128)(2,1)S(1)}, bf16[8,128,128]{2,1,0:T(8,128)(2,1)S(1)}, u32[]{:S(2)}, u32[]{:S(2)}) collective-permute-start(bf16[8,128,128]{2,1,0:T(8,128)(2,1)S(1)} %get-tuple-element.62.e0), channel_id=1, source_target_pairs={{0,32},{32,64},{64,96},{96,0},{128,160},{160,192},{192,224},{224,1... | collective-permute-start | bytes 786440 | tf_op jit(solution)/shard_map/ppermute | solution.py:371
  95.8 21.0 %collective-permute-start.21 = (bf16[512,128]{1,0:T(8,128)(2,1)S(1)}, bf16[512,128]{1,0:T(8,128)(2,1)S(1)}, u32[]{:S(2)}, u32[]{:S(2)}) collective-permute-start(bf16[512,128]{1,0:T(8,128)(2,1)S(1)} %broadcast_select_fusion.p0), channel_id=1, source_target_pairs={{0,96},{32,0},{64,32},{96,64},{128,224},{160,128},{192,160},{224,1... | collective-permute-start | bytes 393224 | tf_op jit(solution)/shard_map/ppermute | solution.py:371
  97.7 20.3 %collective-permute-start.20 = (bf16[512,128]{1,0:T(8,128)(2,1)S(1)}, bf16[512,128]{1,0:T(8,128)(2,1)S(1)}, u32[]{:S(2)}, u32[]{:S(2)}) collective-permute-start(bf16[512,128]{1,0:T(8,128)(2,1)S(1)} %broadcast_select_fusion.p0), channel_id=1, source_target_pairs={{0,64},{32,96},{64,0},{96,32},{128,192},{160,224},{192,128},{224,1... | collective-permute-start | bytes 393224 | tf_op jit(solution)/shard_map/ppermute | solution.py:371
  98.9 19.2 %collective-permute-start.19 = (bf16[512,128]{1,0:T(8,128)(2,1)S(1)}, bf16[512,128]{1,0:T(8,128)(2,1)S(1)}, u32[]{:S(2)}, u32[]{:S(2)}) collective-permute-start(bf16[512,128]{1,0:T(8,128)(2,1)S(1)} %broadcast_select_fusion.p0), channel_id=1, source_target_pairs={{0,32},{32,64},{64,96},{96,0},{128,160},{160,192},{192,224},{224,1... | collective-permute-start | bytes 393224 | tf_op jit(solution)/shard_map/ppermute | solution.py:371
  100.1 7.9 %collective-permute-start.25 = (f32[64,64]{1,0:T(8,128)S(1)}, f32[64,64]{1,0:T(8,128)S(1)}, u32[]{:S(2)}, u32[]{:S(2)}) collective-permute-start(f32[64,64]{1,0:T(8,128)S(1)} %add.54), channel_id=1, source_target_pairs={{0,16},{1,17},{2,18},{3,19},{4,20},{5,21},{6,22},{7,23},{8,24},{9,... | collective-permute-start | bytes 49160 | tf_op jit(solution)/shard_map/ppermute | solution.py:394
  113.5 15.5 %collective-permute-start.29 = (f32[64,64]{1,0:T(8,128)S(1)}, f32[64,64]{1,0:T(8,128)S(1)}, u32[]{:S(2)}, u32[]{:S(2)}) collective-permute-start(f32[64,64]{1,0:T(8,128)S(1)} %add.56), channel_id=1, source_target_pairs={{0,96},{32,0},{64,32},{96,64},{128,224},{160,128},{192,160},{224,1... | collective-permute-start | bytes 49160 | tf_op jit(solution)/shard_map/ppermute | solution.py:371
  114.4 14.7 %collective-permute-start.28 = (f32[64,64]{1,0:T(8,128)S(1)}, f32[64,64]{1,0:T(8,128)S(1)}, u32[]{:S(2)}, u32[]{:S(2)}) collective-permute-start(f32[64,64]{1,0:T(8,128)S(1)} %add.56), channel_id=1, source_target_pairs={{0,64},{32,96},{64,0},{96,32},{128,192},{160,224},{192,128},{224,1... | collective-permute-start | bytes 49160 | tf_op jit(solution)/shard_map/ppermute | solution.py:371
  116.7 12.3 %collective-permute-start.27 = (f32[64,64]{1,0:T(8,128)S(1)}, f32[64,64]{1,0:T(8,128)S(1)}, u32[]{:S(2)}, u32[]{:S(2)}) collective-permute-start(f32[64,64]{1,0:T(8,128)S(1)} %add.56), channel_id=1, source_target_pairs={{0,32},{32,64},{64,96},{96,0},{128,160},{160,192},{192,224},{224,1... | collective-permute-start | bytes 49160 | tf_op jit(solution)/shard_map/ppermute | solution.py:371
  (19 other events, 262.2 us)
